TPU v7x, 32 devices: a whole 2x2x4 slice. The times are simulated.
32 devices in a mesh: seq: 4 (over z), head: 2 (over x), wshard: 4 (over y, core).
Axes of the slice: x: 2, y: 2, z: 4, core: 2. Of those that a mesh axis runs over, the one named last changes fastest.
Arguments:
- prompt_states: bfloat16 [4, 256, 768], P('wshard', ('seq', 'head')), may hold values from -6 to 6
- content_states: bfloat16 [4, 2048, 768], P('wshard', ('seq', 'head')), may hold values from -6 to 6
- query_states: bfloat16 [4, 2048, 768], P('wshard', ('seq', 'head')), may hold values from -6 to 6
- visible_length: int32 [4, 2], P('wshard'), may hold values from 128 to 256, as said below
- start_offsets: int32 [4, 2], P('wshard'), may hold values from 0 to 63
- prompt_segments: int32 [4, 256], P('wshard'), may hold values from 0 to 3
- token_segments: int32 [4, 2048], P('wshard'), may hold values from 0 to 3
- order_ranks: int32 [4, 2048], P('wshard'), may hold values from 0 to 1023, as said below
- query_weights: bfloat16 [768, 768], P('wshard'), may hold values from -0.21875 to 0.21875
- key_weights: bfloat16 [768, 768], P('wshard'), may hold values from -0.21875 to 0.21875
- value_weights: bfloat16 [768, 768], P('wshard'), may hold values from -0.21875 to 0.21875
- output_weights: bfloat16 [768, 768], P('wshard'), may hold values from -1.75 to 1.75
- relative_weights: bfloat16 [768, 768], P('wshard'), may hold values from -0.3125 to 0.3125
- content_bias: bfloat16 [768], P('wshard'), may hold values from -3 to 3
- position_bias: bfloat16 [768], P('wshard'), may hold values from -3 to 3
- segment_bias: bfloat16 [768], P('wshard'), may hold values from -3 to 3
- segment_vectors: bfloat16 [2, 768], P(None, 'wshard'), may hold values from -5 to 5
- attention_gain: bfloat16 [768], P('wshard'), may hold values from 0.25 to 1.75
- attention_shift: bfloat16 [768], P('wshard'), may hold values from -2 to 2
- hidden_weights: bfloat16 [768, 3072], P('wshard'), may hold values from -0.21875 to 0.21875
- hidden_bias: bfloat16 [3072], P('wshard'), may hold values from -2 to 2
- return_weights: bfloat16 [3072, 768], P('wshard'), may hold values from -0.21875 to 0.21875
- return_bias: bfloat16 [768], P('wshard'), may hold values from -2 to 2
- final_gain: bfloat16 [768], P('wshard'), may hold values from 0.25 to 1.75
- final_shift: bfloat16 [768], P('wshard'), may hold values from -2 to 2
- content_upstream: bfloat16 [4, 2048, 768], P('wshard', ('seq', 'head')), may hold values from -6 to 6
- query_upstream: bfloat16 [4, 2048, 768], P('wshard', ('seq', 'head')), may hold values from -6 to 6
Outputs:
- content_output: bfloat16 [4, 2048, 768], P('wshard', ('seq', 'head'))
- query_output: bfloat16 [4, 2048, 768], P('wshard', ('seq', 'head'))
- prompt_gradient: bfloat16 [4, 256, 768], P('wshard', ('seq', 'head'))
- content_gradient: bfloat16 [4, 2048, 768], P('wshard', ('seq', 'head'))
- queries_gradient: bfloat16 [4, 2048, 768], P('wshard', ('seq', 'head'))
- gradient_query: float32 [768, 768], P('wshard')
- gradient_key: float32 [768, 768], P('wshard')
- gradient_value: float32 [768, 768], P('wshard')
- gradient_output: float32 [768, 768], P('wshard')
- gradient_relative: float32 [768, 768], P('wshard')
- gradient_content: float32 [768], P('wshard')
- gradient_position: float32 [768], P('wshard')
- gradient_segment: float32 [768], P('wshard')
- gradient_vectors: float32 [2, 768], P(None, 'wshard')
- gradient_scale: float32 [768], P('wshard')
- gradient_offset: float32 [768], P('wshard')
- gradient_hidden: float32 [768, 3072], P('wshard')
- gradient_inner: float32 [3072], P('wshard')
- gradient_return: float32 [3072, 768], P('wshard')
- gradient_outer: float32 [768], P('wshard')
- gradient_closing: float32 [768], P('wshard')
- gradient_ending: float32 [768], P('wshard')
Inputs may be any that keep to these rules, and one draw needn't show every extreme that they name: `visible_length`: in each job one continuation, drawn from the seed, sees the whole prompt; the others see a prefix of at least half of it. `order_ranks`: the 1024 ranks of each continuation are a permutation of 0 to 1023.
All inputs are finite; a program needn't handle non-finite values.
Results may differ from a plain program's by a relative error of at most 0.03.
Values may be sent and summed in bfloat16 or wider, within the bound.
No kernel may reach another device: no remote copies, remote signals or barrier semaphores. Data moves between devices by JAX's collectives and lax.ppermute only.
A program may use at most 256 MiB of HBM per device.

v0:
```python
from functools import partial

import jax
import jax.numpy as jnp
from jax import lax
from jax.sharding import PartitionSpec as P

D = 768
HEADS = 12
HEAD_DIM = 64
OFFS = 64
LEN = 1024


highest = lax.Precision.HIGHEST
negative = -1e30
epsilon = 1e-06


def partner_2(x, axis, apart):
    return lax.ppermute(x, axis, [(i, i ^ 1 << apart) for i in range(lax.axis_size(axis))])


def layer_norm(values, gain_vector, shift_vector):
    center = values - jnp.mean(values, axis=-1, keepdims=True)
    spread = jnp.mean(center * center, axis=-1, keepdims=True)
    return center * lax.rsqrt(spread + epsilon) * gain_vector + shift_vector


def sinusoid(row_count, width_total, length):
    distance = (jnp.arange(row_count, dtype=jnp.int32) - length).astype(jnp.float32)
    frequency = jnp.power(
        10000.0, -2.0 * jnp.arange(width_total // 2, dtype=jnp.float32) / width_total
    )
    angles = distance[:, None] * frequency[None, :]
    return jnp.concatenate([jnp.sin(angles), jnp.cos(angles)], axis=1)


def shear_band(banded, width_keys):
    leading = banded.shape[:-2]
    row_count, band_width = banded.shape[-2:]
    padded = jnp.pad(banded, [(0, 0)] * len(leading) + [(0, 0), (0, 1)])
    flatten = padded.reshape(leading + (row_count * (band_width + 1),))
    part_rows = lax.slice_in_dim(
        flatten, row_count - 1, row_count - 1 + row_count * band_width, axis=len(leading)
    )
    return part_rows.reshape(leading + (row_count, band_width))[..., :width_keys]


def project(rows_in, weight):
    return jnp.dot(rows_in, weight, preferred_element_type=jnp.float32)


def back_through(grad_rows, weight):
    return jnp.einsum("rc,dc->rd", grad_rows, weight, preferred_element_type=jnp.float32)


def outer_sum(rows_in, grad_rows):
    return jnp.einsum("rd,rc->dc", rows_in, grad_rows, preferred_element_type=jnp.float32)


def table_product(position_rows, table_rows_grad):
    return jnp.einsum(
        "rd,rc->dc",
        position_rows.astype(jnp.float32),
        table_rows_grad,
        precision=highest,
        preferred_element_type=jnp.float32,
    )


def head_major(pair_rows, local_heads):
    leading = pair_rows.shape[:-3]
    row_count = pair_rows.shape[-3]
    split_rows = pair_rows.reshape(
        leading + (row_count, 2, local_heads, pair_rows.shape[-1] // local_heads)
    )
    count = len(leading)
    order = tuple(range(count)) + (count + 1, count + 2, count, count + 3)
    return jnp.transpose(split_rows, order)


def token_major(pieces):
    leading = pieces.shape[:-4]
    count = len(leading)
    order = tuple(range(count)) + (count + 2, count, count + 1, count + 3)
    moved = jnp.transpose(pieces, order)
    return moved.reshape(moved.shape[:-2] + (moved.shape[-2] * moved.shape[-1],))


def per_device(
    prompt_states,
    content_states,
    query_states,
    visible_length,
    start_offsets,
    prompt_segments,
    token_segments,
    order_ranks,
    query_weights,
    key_weights,
    value_weights,
    output_weights,
    relative_weights,
    content_bias,
    position_bias,
    segment_bias,
    segment_vectors,
    attention_gain,
    attention_shift,
    hidden_weights,
    hidden_bias,
    return_weights,
    return_bias,
    final_gain,
    final_shift,
    content_upstream,
    query_upstream,
):
    seq_count = lax.axis_size("seq")
    head_count = lax.axis_size("head")
    seq_index = lax.axis_index("seq")
    head_index = lax.axis_index("head")
    gathered = (
        lax.all_gather(query_weights, "wshard", axis=0, tiled=True),
        lax.all_gather(key_weights, "wshard", axis=0, tiled=True),
        lax.all_gather(value_weights, "wshard", axis=0, tiled=True),
        lax.all_gather(output_weights, "wshard", axis=0, tiled=True),
        lax.all_gather(relative_weights, "wshard", axis=0, tiled=True),
        lax.all_gather(content_bias, "wshard", axis=0, tiled=True),
        lax.all_gather(position_bias, "wshard", axis=0, tiled=True),
        lax.all_gather(segment_bias, "wshard", axis=0, tiled=True),
        lax.all_gather(segment_vectors, "wshard", axis=1, tiled=True),
        lax.all_gather(attention_gain, "wshard", axis=0, tiled=True),
        lax.all_gather(attention_shift, "wshard", axis=0, tiled=True),
        lax.all_gather(hidden_weights, "wshard", axis=0, tiled=True),
        lax.all_gather(hidden_bias, "wshard", axis=0, tiled=True),
        lax.all_gather(return_weights, "wshard", axis=0, tiled=True),
        lax.all_gather(return_bias, "wshard", axis=0, tiled=True),
        lax.all_gather(final_gain, "wshard", axis=0, tiled=True),
        lax.all_gather(final_shift, "wshard", axis=0, tiled=True),
    )
    (
        query_full,
        key_full,
        value_full,
        output_full,
        relative_full,
        content_full,
        position_full,
        segment_full,
        vectors_full,
        attention_scale,
        attention_offset,
        hidden_full,
        inner_full,
        return_full,
        outer_full,
        final_scale,
        final_offset,
    ) = gathered
    local_width = D // head_count
    local_heads = HEADS // head_count
    head_start = head_index * local_width
    scale_factor = HEAD_DIM ** (-0.5)

    def local_slice(vector):
        return lax.dynamic_slice_in_dim(vector, head_start, local_width, vector.ndim - 1).astype(
            jnp.float32
        )

    content_add = local_slice(content_full).reshape(local_heads, 1, HEAD_DIM)
    position_add = local_slice(position_full).reshape(local_heads, 1, HEAD_DIM)
    segment_add = local_slice(segment_full).reshape(local_heads, 1, HEAD_DIM)
    segment_pair = local_slice(vectors_full).reshape(2, local_heads, HEAD_DIM)
    prompt_rows = prompt_states[0]
    content_rows = content_states[0]
    query_rows = query_states[0]
    token_half = content_rows.shape[0]
    prompt_half = prompt_rows.shape[0]
    content_query = project(content_rows, query_full).astype(jnp.bfloat16)
    query_query = project(query_rows, query_full).astype(jnp.bfloat16)
    source_rows = jnp.concatenate([content_rows, prompt_rows], axis=0)
    key_all = project(source_rows, key_full).astype(jnp.bfloat16)
    value_all = project(source_rows, value_full).astype(jnp.bfloat16)
    token_stack = jnp.stack(
        [content_query, query_query, key_all[:token_half], value_all[:token_half]], axis=1
    ).reshape(token_half, 4, head_count, local_width)
    prompt_stack = jnp.stack([key_all[token_half:], value_all[token_half:]], axis=1).reshape(
        prompt_half, 2, head_count, local_width
    )
    token_heads, prompt_heads = (
        lax.all_to_all(token_stack, "head", split_axis=2, concat_axis=0, tiled=True),
        lax.all_to_all(prompt_stack, "head", split_axis=2, concat_axis=0, tiled=True),
    )
    token_heads = token_heads.reshape(-1, 4, local_width)
    prompt_heads = prompt_heads.reshape(-1, 2, local_width)
    block_tokens = token_heads.shape[0]
    block_prompt = prompt_heads.shape[0]
    prompt_total = block_prompt * seq_count
    span_count = LEN // block_tokens
    seq_total = visible_length.shape[1]
    sequence_index = seq_index * block_tokens // LEN
    chosen = jnp.arange(seq_total, dtype=jnp.int32) == sequence_index
    seen_length = jnp.sum(jnp.where(chosen, visible_length[0], 0))
    offset_value = jnp.sum(jnp.where(chosen, start_offsets[0], 0))
    local_start = seq_index * block_tokens % LEN
    query_base = seen_length + offset_value + local_start
    token_start = seq_index * block_tokens
    query_segments = lax.dynamic_slice_in_dim(token_segments[0], token_start, block_tokens)
    query_ranks = lax.dynamic_slice_in_dim(order_ranks[0], token_start, block_tokens)
    group_start = sequence_index * LEN
    group_segments = lax.dynamic_slice_in_dim(token_segments[0], group_start, LEN).reshape(
        span_count, block_tokens
    )
    group_ranks = lax.dynamic_slice_in_dim(order_ranks[0], group_start, LEN).reshape(
        span_count, block_tokens
    )
    table_rows = prompt_total + seq_count * ((2 * LEN + OFFS + seq_count - 1) // seq_count)
    positions = sinusoid(table_rows, D, LEN).astype(jnp.bfloat16)
    relative_local = lax.dynamic_slice_in_dim(relative_full, head_start, local_width, 1)
    rel_table = project(positions, relative_local).astype(jnp.bfloat16)
    reversed_heads = jnp.transpose(
        jnp.flip(rel_table, 0).reshape(table_rows, local_heads, HEAD_DIM), (1, 0, 2)
    )
    queries = jnp.transpose(
        token_heads[:, 0:2].reshape(block_tokens, 2, local_heads, HEAD_DIM), (1, 2, 0, 3)
    )
    queries_wide = queries.astype(jnp.float32)
    with_content = (queries_wide + content_add).astype(jnp.bfloat16)
    with_position = (queries_wide + position_add).astype(jnp.bfloat16)
    with_segment = queries_wide + segment_add
    same_term = jnp.einsum("shte,he->sht", with_segment, segment_pair[0], precision=highest)
    other_term = jnp.einsum("shte,he->sht", with_segment, segment_pair[1], precision=highest)
    group_rows = token_heads[:, 2:4][None]
    bit_number = 0
    partner = partner_2(group_rows, "seq", bit_number)
    upper_bit = seq_index // 2**bit_number % 2 == 1
    group_rows = jnp.where(
        upper_bit, jnp.concatenate([partner, group_rows]), jnp.concatenate([group_rows, partner])
    )
    group_heads = head_major(group_rows, local_heads)
    block_group = max(1, min(512, LEN) // block_prompt)
    block_group = min(block_group, seq_count)
    while seq_count % block_group != 0:
        block_group -= 1
    key_block = block_group * block_prompt
    block_total = prompt_total // key_block
    prompt_blocks = lax.all_gather(prompt_heads[None], "seq", axis=0, tiled=True).reshape(
        block_total, key_block, 2, local_width
    )
    prompt_major = head_major(prompt_blocks, local_heads)

    def block_scores(key_heads, band_start, width_keys, differ):
        band_width = block_tokens + width_keys - 1
        band_heads = lax.dynamic_slice_in_dim(
            reversed_heads, table_rows - band_start - band_width, band_width, 1
        )
        content = jnp.einsum(
            "shte,hke->shtk", with_content, key_heads, preferred_element_type=jnp.float32
        )
        banded = jnp.einsum(
            "shte,hwe->shtw", with_position, band_heads, preferred_element_type=jnp.float32
        )
        segment = jnp.where(differ[None, None], other_term[..., None], same_term[..., None])
        return ((content + shear_band(banded, width_keys) + segment) * scale_factor, band_heads)

    def prompt_info(block_index):
        start_key = block_index * key_block
        band_start = query_base - start_key - key_block + 1 + LEN
        key_places = start_key + jnp.arange(key_block, dtype=jnp.int32)
        visible = (key_places < seen_length)[None, None, None, :]
        differ = (
            query_segments[:, None]
            != lax.dynamic_slice_in_dim(prompt_segments[0], start_key, key_block)[None, :]
        )
        return (start_key, band_start, visible, differ)

    def token_info(member, key_segments, key_ranks):
        band_start = local_start - member * block_tokens - block_tokens + 1 + LEN
        differ = query_segments[:, None] != key_segments[None, :]
        visible = jnp.stack(
            [key_ranks[None, :] <= query_ranks[:, None], key_ranks[None, :] < query_ranks[:, None]]
        )[:, None]
        return (band_start, visible, differ)

    def forward_step(running, scores, visible, value_heads):
        largest, weight_total, accumulated = running
        scores = jnp.where(visible, scores, negative)
        new_largest = jnp.maximum(largest, jnp.max(scores, axis=-1))
        weights = jnp.where(visible, jnp.exp(scores - new_largest[..., None]), 0.0)
        factor = jnp.exp(largest - new_largest)
        weight_total = weight_total * factor + jnp.sum(weights, axis=-1)
        accumulated = accumulated * factor[..., None] + jnp.einsum(
            "shtk,hke->shte",
            weights.astype(jnp.bfloat16),
            value_heads,
            preferred_element_type=jnp.float32,
        )
        return (new_largest, weight_total, accumulated)

    def token_forward(running, entries):
        member, pair_heads, key_segments, key_ranks = entries
        band_start, visible, differ = token_info(member, key_segments, key_ranks)
        scores, _ = block_scores(pair_heads[0], band_start, block_tokens, differ)
        return (forward_step(running, scores, visible, pair_heads[1]), None)

    def prompt_forward(running, entries):
        block_index, pair_heads = entries
        start_key, band_start, visible, differ = prompt_info(block_index)

        def active_block(current):
            scores, _ = block_scores(pair_heads[0], band_start, key_block, differ)
            return forward_step(current, scores, visible, pair_heads[1])

        return (
            lax.cond(start_key < seen_length, active_block, lambda current: current, running),
            None,
        )

    zero_rows = jnp.zeros((2, local_heads, block_tokens), jnp.float32)
    initial = (
        jnp.full((2, local_heads, block_tokens), negative, jnp.float32),
        zero_rows,
        jnp.zeros((2, local_heads, block_tokens, HEAD_DIM), jnp.float32),
    )
    member_ids = jnp.arange(span_count, dtype=jnp.int32)
    block_ids = jnp.arange(block_total, dtype=jnp.int32)
    running, _ = lax.scan(
        token_forward, initial, (member_ids, group_heads, group_segments, group_ranks)
    )
    running, _ = lax.scan(prompt_forward, running, (block_ids, prompt_major))
    largest, weight_total, accumulated = running
    mixture = accumulated / weight_total[..., None]
    log_total = largest + jnp.log(weight_total)
    mixture_rows = (
        jnp.transpose(mixture, (2, 0, 1, 3))
        .reshape(block_tokens, 2, local_width)
        .astype(jnp.bfloat16)
    )
    back_rows = lax.all_to_all(
        mixture_rows.reshape(head_count, token_half, 2, 1, local_width),
        "head",
        split_axis=0,
        concat_axis=3,
        tiled=True,
    ).reshape(token_half, 2, D)
    streams_in = jnp.concatenate([content_rows, query_rows], axis=0).astype(jnp.float32)
    mixed_flat = jnp.concatenate([back_rows[:, 0], back_rows[:, 1]], axis=0)
    branch = project(mixed_flat, output_full)
    middle, norm_back = jax.vjp(
        layer_norm,
        streams_in + branch,
        attention_scale.astype(jnp.float32),
        attention_offset.astype(jnp.float32),
    )
    inner_in = middle.astype(jnp.bfloat16)
    inner_sum = project(inner_in, hidden_full) + inner_full.astype(jnp.float32)
    active, gelu_back = jax.vjp(partial(jax.nn.gelu, approximate=True), inner_sum)
    active_low = active.astype(jnp.bfloat16)
    returned = project(active_low, return_full) + outer_full.astype(jnp.float32)
    normed, final_back = jax.vjp(
        layer_norm,
        middle + returned,
        final_scale.astype(jnp.float32),
        final_offset.astype(jnp.float32),
    )
    upstream = jnp.concatenate([content_upstream[0], query_upstream[0]], axis=0).astype(jnp.float32)
    sum_grad, closing_grad, ending_grad = final_back(upstream)
    returned_grad = sum_grad.astype(jnp.bfloat16)
    outer_grad = jnp.sum(returned_grad.astype(jnp.float32), axis=0)
    return_grad = outer_sum(active_low, returned_grad)
    active_grad = back_through(returned_grad, return_full)
    inner_grad = gelu_back(active_grad)[0].astype(jnp.bfloat16)
    inner_bias_grad = jnp.sum(inner_grad.astype(jnp.float32), axis=0)
    hidden_grad = outer_sum(inner_in, inner_grad)
    middle_grad = sum_grad + back_through(inner_grad, hidden_full)
    residual_grad, scale_grad, offset_grad = norm_back(middle_grad)
    branch_grad = residual_grad.astype(jnp.bfloat16)
    output_grad = outer_sum(mixed_flat, branch_grad)
    mixed_grad = back_through(branch_grad, output_full).astype(jnp.bfloat16)
    grad_stack = jnp.stack([mixed_grad[:token_half], mixed_grad[token_half:]], axis=1).reshape(
        token_half, 2, head_count, local_width
    )
    heads_grad = lax.all_to_all(
        grad_stack, "head", split_axis=2, concat_axis=0, tiled=True
    ).reshape(block_tokens, 2, local_heads, HEAD_DIM)
    out_grad = jnp.transpose(heads_grad, (1, 2, 0, 3))
    row_dots = jnp.sum(out_grad.astype(jnp.float32) * mixture, axis=-1)

    def backward_step(
        running, scores, band_heads, visible, differ, pair_heads, width_keys, band_start
    ):
        query_content, query_position, same_grad, other_grad, table_grad = running
        shares = jnp.where(visible, jnp.exp(scores - log_total[..., None]), 0.0)
        key_heads = pair_heads[0]
        value_heads = pair_heads[1]
        share_grad = jnp.einsum(
            "shte,hke->shtk", out_grad, value_heads, preferred_element_type=jnp.float32
        )
        score_grad = (shares * (share_grad - row_dots[..., None])).astype(jnp.bfloat16)
        scaled = (score_grad.astype(jnp.float32) * scale_factor).astype(jnp.bfloat16)
        value_grad = jnp.einsum(
            "shtk,shte->hke",
            shares.astype(jnp.bfloat16),
            out_grad,
            preferred_element_type=jnp.float32,
        )
        key_grad = jnp.einsum(
            "shtk,shte->hke", scaled, with_content, preferred_element_type=jnp.float32
        )
        query_content = query_content + jnp.einsum(
            "shtk,hke->shte", scaled, key_heads, preferred_element_type=jnp.float32
        )
        band_width = block_tokens + width_keys - 1
        _, shear_back = jax.vjp(
            lambda banded_in: shear_band(banded_in, width_keys),
            jnp.zeros(scaled.shape[:-1] + (band_width,), jnp.float32),
        )
        scaled_wide = scaled.astype(jnp.float32)
        band_grad = shear_back(scaled_wide)[0].astype(jnp.bfloat16)
        query_position = query_position + jnp.einsum(
            "shtw,hwe->shte", band_grad, band_heads, preferred_element_type=jnp.float32
        )
        table_piece = jnp.einsum(
            "shtw,shte->hwe", band_grad, with_position, preferred_element_type=jnp.float32
        )
        table_begin = table_rows - band_start - band_width
        table_grad = lax.dynamic_update_slice_in_dim(
            table_grad,
            lax.dynamic_slice_in_dim(table_grad, table_begin, band_width, 1) + table_piece,
            table_begin,
            1,
        )
        same_grad = same_grad + jnp.sum(jnp.where(differ[None, None], 0.0, scaled_wide), axis=-1)
        other_grad = other_grad + jnp.sum(jnp.where(differ[None, None], scaled_wide, 0.0), axis=-1)
        pieces_out = jnp.stack([key_grad, value_grad])
        return ((query_content, query_position, same_grad, other_grad, table_grad), pieces_out)

    def token_backward(running, entries):
        member, pair_heads, key_segments, key_ranks = entries
        band_start, visible, differ = token_info(member, key_segments, key_ranks)
        scores, band_heads = block_scores(pair_heads[0], band_start, block_tokens, differ)
        return backward_step(
            running, scores, band_heads, visible, differ, pair_heads, block_tokens, band_start
        )

    def prompt_backward(running, entries):
        block_index, pair_heads = entries
        start_key, band_start, visible, differ = prompt_info(block_index)

        def active_block(current):
            scores, band_heads = block_scores(pair_heads[0], band_start, key_block, differ)
            return backward_step(
                current, scores, band_heads, visible, differ, pair_heads, key_block, band_start
            )

        def skipped_block(current):
            return (current, jnp.zeros((2, local_heads, key_block, HEAD_DIM), jnp.float32))

        return lax.cond(start_key < seen_length, active_block, skipped_block, running)

    zero_query = jnp.zeros((2, local_heads, block_tokens, HEAD_DIM), jnp.float32)
    running = (
        zero_query,
        zero_query,
        zero_rows,
        zero_rows,
        jnp.zeros((local_heads, table_rows, HEAD_DIM), jnp.float32),
    )
    running, token_grads = lax.scan(
        token_backward, running, (member_ids, group_heads, group_segments, group_ranks)
    )
    running, prompt_grads = lax.scan(prompt_backward, running, (block_ids, prompt_major))
    query_content, query_position, same_grad, other_grad, reversed_grad = running
    table_grad = jnp.flip(jnp.transpose(reversed_grad, (1, 0, 2)), 0).reshape(
        table_rows, local_width
    )
    partial_sums = token_major(token_grads)
    for bit_number in reversed(range(span_count.bit_length() - 1)):
        half_size = 2**bit_number
        upper_bit = seq_index // half_size % 2 == 1
        lower_half = partial_sums[:half_size]
        upper_half = partial_sums[half_size : 2 * half_size]
        kept_half = jnp.where(upper_bit, upper_half, lower_half)
        sent_half = jnp.where(upper_bit, lower_half, upper_half)
        partial_sums = kept_half + partner_2(
            sent_half.astype(jnp.bfloat16), "seq", bit_number
        ).astype(sent_half.dtype)
    token_key_grads = partial_sums[0]
    prompt_pieces = token_major(prompt_grads).reshape(seq_count, block_prompt, 2, local_width)
    prompt_sum, table_sum = (
        lax.psum_scatter(
            prompt_pieces.astype(jnp.bfloat16), "seq", scatter_dimension=0, tiled=True
        ).astype(jnp.float32),
        lax.psum_scatter(
            table_grad.astype(jnp.bfloat16), "seq", scatter_dimension=0, tiled=True
        ).astype(jnp.float32),
    )
    shard_rows = table_rows // seq_count
    position_rows = lax.dynamic_slice_in_dim(positions, seq_index * shard_rows, shard_rows, 0)
    relative_cols = table_product(position_rows, table_sum)
    segment_term = jnp.einsum(
        "sht,he->shte", same_grad, segment_pair[0], precision=highest
    ) + jnp.einsum("sht,he->shte", other_grad, segment_pair[1], precision=highest)
    query_grad = query_content + query_position + segment_term
    content_bias_grad = jnp.sum(query_content, axis=(0, 2)).reshape(local_width)
    position_bias_grad = jnp.sum(query_position, axis=(0, 2)).reshape(local_width)
    segment_bias_grad = jnp.sum(segment_term, axis=(0, 2)).reshape(local_width)
    vector_grad = jnp.stack(
        [
            jnp.einsum("sht,shte->he", same_grad, with_segment, precision=highest),
            jnp.einsum("sht,shte->he", other_grad, with_segment, precision=highest),
        ]
    ).reshape(2, local_width)
    query_rows_grad = jnp.transpose(query_grad, (2, 0, 1, 3)).reshape(block_tokens, 2, local_width)
    token_back = jnp.concatenate([query_rows_grad, token_key_grads], axis=1).astype(jnp.bfloat16)
    prompt_back = prompt_sum[0].astype(jnp.bfloat16)
    token_rows, prompt_rows_back = (
        lax.all_to_all(
            token_back.reshape(head_count, token_half, 4, 1, local_width),
            "head",
            split_axis=0,
            concat_axis=3,
            tiled=True,
        ),
        lax.all_to_all(
            prompt_back.reshape(head_count, prompt_half, 2, 1, local_width),
            "head",
            split_axis=0,
            concat_axis=3,
            tiled=True,
        ),
    )
    token_rows = token_rows.reshape(token_half, 4, D)
    prompt_rows_back = prompt_rows_back.reshape(prompt_half, 2, D)
    content_grad = (
        residual_grad[:token_half]
        + back_through(token_rows[:, 0], query_full)
        + back_through(token_rows[:, 2], key_full)
        + back_through(token_rows[:, 3], value_full)
    )
    queries_grad = residual_grad[token_half:] + back_through(token_rows[:, 1], query_full)
    prompt_grad = back_through(prompt_rows_back[:, 0], key_full) + back_through(
        prompt_rows_back[:, 1], value_full
    )
    query_weight_grad = outer_sum(content_rows, token_rows[:, 0]) + outer_sum(
        query_rows, token_rows[:, 1]
    )
    key_weight_grad = outer_sum(content_rows, token_rows[:, 2]) + outer_sum(
        prompt_rows, prompt_rows_back[:, 0]
    )
    value_weight_grad = outer_sum(content_rows, token_rows[:, 3]) + outer_sum(
        prompt_rows, prompt_rows_back[:, 1]
    )
    relative_grad = lax.dynamic_update_slice_in_dim(
        jnp.zeros((D, D), jnp.float32), relative_cols, head_start, 1
    )

    def place(vector):
        return lax.dynamic_update_slice_in_dim(
            jnp.zeros(vector.shape[:-1] + (D,), jnp.float32), vector, head_start, vector.ndim - 1
        )

    content_placed = place(content_bias_grad)
    position_placed = place(position_bias_grad)
    segment_placed = place(segment_bias_grad)
    vector_placed = place(vector_grad)
    reduced = (
        lax.psum_scatter(
            query_weight_grad.astype(jnp.bfloat16), "wshard", scatter_dimension=0, tiled=True
        ).astype(jnp.float32),
        lax.psum_scatter(
            key_weight_grad.astype(jnp.bfloat16), "wshard", scatter_dimension=0, tiled=True
        ).astype(jnp.float32),
        lax.psum_scatter(
            value_weight_grad.astype(jnp.bfloat16), "wshard", scatter_dimension=0, tiled=True
        ).astype(jnp.float32),
        lax.psum_scatter(
            output_grad.astype(jnp.bfloat16), "wshard", scatter_dimension=0, tiled=True
        ).astype(jnp.float32),
        lax.psum_scatter(
            relative_grad.astype(jnp.bfloat16), "wshard", scatter_dimension=0, tiled=True
        ).astype(jnp.float32),
        lax.psum_scatter(
            content_placed.astype(jnp.bfloat16), "wshard", scatter_dimension=0, tiled=True
        ).astype(jnp.float32),
        lax.psum_scatter(
            position_placed.astype(jnp.bfloat16), "wshard", scatter_dimension=0, tiled=True
        ).astype(jnp.float32),
        lax.psum_scatter(
            segment_placed.astype(jnp.bfloat16), "wshard", scatter_dimension=0, tiled=True
        ).astype(jnp.float32),
        lax.psum_scatter(
            vector_placed.astype(jnp.bfloat16), "wshard", scatter_dimension=1, tiled=True
        ).astype(jnp.float32),
        lax.psum_scatter(
            scale_grad.astype(jnp.bfloat16), "wshard", scatter_dimension=0, tiled=True
        ).astype(jnp.float32),
        lax.psum_scatter(
            offset_grad.astype(jnp.bfloat16), "wshard", scatter_dimension=0, tiled=True
        ).astype(jnp.float32),
        lax.psum_scatter(
            hidden_grad.astype(jnp.bfloat16), "wshard", scatter_dimension=0, tiled=True
        ).astype(jnp.float32),
        lax.psum_scatter(
            inner_bias_grad.astype(jnp.bfloat16), "wshard", scatter_dimension=0, tiled=True
        ).astype(jnp.float32),
        lax.psum_scatter(
            return_grad.astype(jnp.bfloat16), "wshard", scatter_dimension=0, tiled=True
        ).astype(jnp.float32),
        lax.psum_scatter(
            outer_grad.astype(jnp.bfloat16), "wshard", scatter_dimension=0, tiled=True
        ).astype(jnp.float32),
        lax.psum_scatter(
            closing_grad.astype(jnp.bfloat16), "wshard", scatter_dimension=0, tiled=True
        ).astype(jnp.float32),
        lax.psum_scatter(
            ending_grad.astype(jnp.bfloat16), "wshard", scatter_dimension=0, tiled=True
        ).astype(jnp.float32),
    )
    reduced = lax.psum(
        (
            reduced[0],
            reduced[1],
            reduced[2],
            reduced[3],
            reduced[4],
            reduced[5],
            reduced[6],
            reduced[7],
            reduced[8],
            reduced[9],
            reduced[10],
            reduced[11],
            reduced[12],
            reduced[13],
            reduced[14],
            reduced[15],
            reduced[16],
        ),
        ("seq", "head"),
    )
    return (
        normed[:token_half].astype(jnp.bfloat16)[None],
        normed[token_half:].astype(jnp.bfloat16)[None],
        prompt_grad.astype(jnp.bfloat16)[None],
        content_grad.astype(jnp.bfloat16)[None],
        queries_grad.astype(jnp.bfloat16)[None],
        reduced[0],
        reduced[1],
        reduced[2],
        reduced[3],
        reduced[4],
        reduced[5],
        reduced[6],
        reduced[7],
        reduced[8],
        reduced[9],
        reduced[10],
        reduced[11],
        reduced[12],
        reduced[13],
        reduced[14],
        reduced[15],
        reduced[16],
    )


def solution(mesh):
    in_specs = (
        P("wshard", ("seq", "head"), None),
        P("wshard", ("seq", "head"), None),
        P("wshard", ("seq", "head"), None),
        P("wshard", None),
        P("wshard", None),
        P("wshard", None),
        P("wshard", None),
        P("wshard", None),
        P("wshard", None),
        P("wshard", None),
        P("wshard", None),
        P("wshard", None),
        P("wshard", None),
        P("wshard"),
        P("wshard"),
        P("wshard"),
        P(None, "wshard"),
        P("wshard"),
        P("wshard"),
        P("wshard", None),
        P("wshard"),
        P("wshard", None),
        P("wshard"),
        P("wshard"),
        P("wshard"),
        P("wshard", ("seq", "head"), None),
        P("wshard", ("seq", "head"), None),
    )
    out_specs = (
        P("wshard", ("seq", "head"), None),
        P("wshard", ("seq", "head"), None),
        P("wshard", ("seq", "head"), None),
        P("wshard", ("seq", "head"), None),
        P("wshard", ("seq", "head"), None),
        P("wshard", None),
        P("wshard", None),
        P("wshard", None),
        P("wshard", None),
        P("wshard", None),
        P("wshard"),
        P("wshard"),
        P("wshard"),
        P(None, "wshard"),
        P("wshard"),
        P("wshard"),
        P("wshard", None),
        P("wshard"),
        P("wshard", None),
        P("wshard"),
        P("wshard"),
        P("wshard"),
    )
    return jax.shard_map(
        per_device, mesh=mesh, in_specs=in_specs, out_specs=out_specs, check_vma=False
    )
```

profile of v0, /device:TPU:0, one launch (start us, length us, event | category | flops | bytes accessed | tf_op | source)
XLA Modules:
  0.0 2304.0 jit_solution(17879719739338833495)
XLA Ops:
  172.4 380.3 %while.14 = (s32[]{:T(128)}, f32[2,6,512]{2,0,1:T(2,128)S(1)}, f32[2,6,512]{2,0,1:T(2,128)S(1)}, f32[2,6,512,64]{2,3,0,1:T(8,128)}, s32[2,512]{1,0:T(2,128)S(1)}...) while((s32[]{:T(128)}, f32[2,6,512]{2,0,1:T(2,128)S(1)}, ...), condition=%wide.region_4.5_spmd.clone, body=%wide.region_1.4_spmd.clone.sunk | while | flops 1650096128 | bytes 387711296 | solution.py:329
  230.4 26.0 %reshape.851 = f32[2,6,524288]{2,0,1:T(2,128)} reshape(f32[2,6,512,1024]{3,2,0,1:T(8,128)} %pad.65.clone.2) | data formatting | bytes 50331648 | tf_op jit(solution)/shard_map/while/body/eval_jaxpr/reshape | solution.py:43
  256.4 30.2 %slice.330 = f32[2,6,523776]{2,0,1:T(2,128)} slice(f32[2,6,524288]{2,0,1:T(2,128)} %reshape.851), slice={[0:2], [0:6], [511:524287]} | slice | bytes 50282496 | tf_op jit(solution)/shard_map/while/body/eval_jaxpr/slice | solution.py:44
  286.6 36.3 %reshape.852 = f32[2,6,512,1023]{3,2,0,1:T(8,128)} reshape(f32[2,6,523776]{2,0,1:T(2,128)} %slice.330) | data formatting | bytes 50282496 | tf_op jit(solution)/shard_map/while/body/eval_jaxpr/reshape | solution.py:47
  420.1 26.0 %reshape.851 = f32[2,6,524288]{2,0,1:T(2,128)} reshape(f32[2,6,512,1024]{3,2,0,1:T(8,128)} %pad.65.clone.2) | data formatting | bytes 50331648 | tf_op jit(solution)/shard_map/while/body/eval_jaxpr/reshape | solution.py:43
  446.1 30.2 %slice.330 = f32[2,6,523776]{2,0,1:T(2,128)} slice(f32[2,6,524288]{2,0,1:T(2,128)} %reshape.851), slice={[0:2], [0:6], [511:524287]} | slice | bytes 50282496 | tf_op jit(solution)/shard_map/while/body/eval_jaxpr/slice | solution.py:44
  476.4 36.3 %reshape.852 = f32[2,6,512,1023]{3,2,0,1:T(8,128)} reshape(f32[2,6,523776]{2,0,1:T(2,128)} %slice.330) | data formatting | bytes 50282496 | tf_op jit(solution)/shard_map/while/body/eval_jaxpr/reshape | solution.py:47
  552.7 139.5 %conditional.2 = (f32[2,6,512]{2,0,1:T(2,128)S(1)}, f32[2,6,512,64]{2,3,0,1:T(8,128)}, f32[2,6,512]{2,0,1:T(2,128)S(1)}) conditional(s32[]{:T(128)} %convert_element_type.381, (f32[2,6,512]{2,0,1:T(2,128)S(1)}, f32[2,6,512]{2,0,1:T(2,128)S(1)}, f32[2,6,512,64]{2,3,0,1:T(8,128)}) %tuple.78, (pred[1,1,1,256]{3,2,1,0:T(4,128)(4,1)S(1)}, ...), branch_computations={%region_6.7_spmd.clone, %region_7.10_spmd.clone} | conditional | flops 1025525760 | bytes 281307072 | solution.py:317
  638.5 31.9 %reshape.722 = f32[2,6,512,767]{3,2,0,1:T(8,128)} reshape(f32[2,6,392704]{2,0,1:T(2,128)} %slice.240) | data formatting | bytes 37699584 | tf_op jit(solution)/shard_map/while/body/eval_jaxpr/cond/branch_1_fun/reshape | solution.py:47
  770.9 639.4 %while.60 = (s32[]{:T(128)}, f32[2,6,512,64]{2,3,0,1:T(8,128)}, f32[2,6,512,64]{2,3,0,1:T(8,128)}, f32[2,6,512]{2,0,1:T(2,128)}, f32[2,6,512]{2,0,1:T(2,128)}, /...) while((s32[]{:T(128)}, f32[2,6,512,64]{2,3,0,1:T(8,128)}, ...), condition=%wide.region_22.23_spmd.clone, body=%wide.region_19.22_spmd.clone.sunk | while | flops 4487130624 | bytes 606628352 | solution.py:471
  852.4 26.0 %reshape.853 = f32[2,6,524288]{2,0,1:T(2,128)} reshape(f32[2,6,512,1024]{3,2,0,1:T(8,128)} %pad.66.clone.2) | data formatting | bytes 50331648 | tf_op jit(solution)/shard_map/while/body/eval_jaxpr/reshape | solution.py:43
  878.4 30.2 %slice.332 = f32[2,6,523776]{2,0,1:T(2,128)} slice(f32[2,6,524288]{2,0,1:T(2,128)} %reshape.853), slice={[0:2], [0:6], [511:524287]} | slice | bytes 50282496 | tf_op jit(solution)/shard_map/while/body/eval_jaxpr/slice | solution.py:44
  908.6 36.3 %reshape.854 = f32[2,6,512,1023]{3,2,0,1:T(8,128)} reshape(f32[2,6,523776]{2,0,1:T(2,128)} %slice.332) | data formatting | bytes 50282496 | tf_op jit(solution)/shard_map/while/body/eval_jaxpr/reshape | solution.py:47
  1158.5 26.0 %reshape.853 = f32[2,6,524288]{2,0,1:T(2,128)} reshape(f32[2,6,512,1024]{3,2,0,1:T(8,128)} %pad.66.clone.2) | data formatting | bytes 50331648 | tf_op jit(solution)/shard_map/while/body/eval_jaxpr/reshape | solution.py:43
  1184.5 30.2 %slice.332 = f32[2,6,523776]{2,0,1:T(2,128)} slice(f32[2,6,524288]{2,0,1:T(2,128)} %reshape.853), slice={[0:2], [0:6], [511:524287]} | slice | bytes 50282496 | tf_op jit(solution)/shard_map/while/body/eval_jaxpr/slice | solution.py:44
  1214.7 36.3 %reshape.854 = f32[2,6,512,1023]{3,2,0,1:T(8,128)} reshape(f32[2,6,523776]{2,0,1:T(2,128)} %slice.332) | data formatting | bytes 50282496 | tf_op jit(solution)/shard_map/while/body/eval_jaxpr/reshape | solution.py:47
  1410.3 218.9 %conditional.3 = (f32[2,6,512,64]{2,3,0,1:T(8,128)}, f32[2,6,512,64]{2,3,0,1:T(8,128)}, f32[2,6,512]{2,0,1:T(2,128)}, f32[2,6,512]{2,0,1:T(2,128)}, f32[6,2368,6...) conditional(s32[]{:T(128)} %convert_element_type.381, (f32[2,6,512,64]{2,3,0,1:T(8,128)}, ...), branch_computations={%region_23.24_spmd, %region_24.27_spmd} | conditional | flops 2845801984 | bytes 444853632 | solution.py:461
  1497.7 31.9 %reshape.696 = f32[2,6,512,767]{3,2,0,1:T(8,128)} reshape(f32[2,6,392704]{2,0,1:T(2,128)} %slice.238) | data formatting | bytes 37699584 | tf_op jit(solution)/shard_map/while/body/eval_jaxpr/cond/branch_1_fun/reshape | solution.py:47
  1668.2 35.1 %collective-permute-done.1 = bf16[1,512,2,384]{1,3,2,0:T(8,128)(2,1)} collective-permute-done((bf16[1,512,2,384]{1,3,2,0:T(8,128)(2,1)}, bf16[1,512,2,384]{1,3,2,0:T(8,128)(2,1)}, u32[]{:S(2)}, u32[]{:S(2)}) %collective-permute-start.1) | collective-permute-done | bytes 786464 | tf_op jit(solution)/shard_map/ppermute | solution.py:21
  1813.9 27.0 %reduce-scatter.33.cloned.1.call-done = bf16[192,768]{1,0:T(8,128)(2,1)} async-done(((bf16[768,768]{1,0:T(8,128)(2,1)}), bf16[192,768]{1,0:T(8,128)(2,1)}) %reduce-scatter.33.cloned.1.call-update) | async-done | bytes 294928
  1842.1 27.8 %reduce-scatter.25.cloned.1.call-done = bf16[192,768]{1,0:T(8,128)(2,1)} async-done(((bf16[768,768]{1,0:T(8,128)(2,1)}), bf16[192,768]{1,0:T(8,128)(2,1)}) %reduce-scatter.25.cloned.1.call-update) | async-done | bytes 294928 | tf_op jit(solution)/shard_map/reduce_scatter | solution.py:582
  1869.8 50.2 %reduce-scatter.27.cloned.1.call-done = bf16[192,3072]{1,0:T(8,128)(2,1)} async-done(((bf16[768,3072]{1,0:T(8,128)(2,1)}), bf16[192,3072]{1,0:T(8,128)(2,1)}) %reduce-scatter.27.cloned.1.call-update) | async-done | bytes 1179664 | tf_op jit(solution)/shard_map/reduce_scatter | solution.py:603
  1920.1 50.4 %reduce-scatter.29.cloned.1.call-done = bf16[768,768]{1,0:T(8,128)(2,1)} async-done(((bf16[3072,768]{1,0:T(8,128)(2,1)}), bf16[768,768]{1,0:T(8,128)(2,1)}) %reduce-scatter.29.cloned.1.call-update) | async-done | bytes 1179664 | tf_op jit(solution)/shard_map/reduce_scatter | solution.py:609
  1970.5 323.6 %all-reduce.29 = (f32[192,768]{0,1:T(8,128)S(1)}, f32[192,768]{0,1:T(8,128)S(1)}, f32[192,768]{0,1:T(8,128)S(1)}, f32[192,768]{1,0:T(8,128)}, f32[192,768]{1,0:T...) all-reduce(bf16[192,768]{0,1:T(8,128)(2,1)S(1)} %copy.294, ...), channel_id=1, replica_groups=mesh['seq'=4,'head'=2,'wshard'=4] {'seq','head'}, use_global_device_ids=true, to_apply=%region_29.30 | all-reduce | flops 1919616 | bytes 11522304 | tf_op jit(solution)/shard_map/psum | solution.py:622
  (674 shorter events, 1305.1 us)
Async XLA Ops:
  7.2 43.2 %all-gather.14.cloned.1.call-start = ((), (), s32[]{:S(2)}) async-start(), calls=%async_computation.18 | async-start | bytes 1474560 | tf_op jit(solution)/shard_map/all_gather | solution.py:127
  8.0 45.6 %all-gather.12.cloned.1.call-start = ((), (), s32[]{:S(2)}) async-start(), calls=%async_computation.17 | async-start | bytes 1474560 | tf_op jit(solution)/shard_map/all_gather | solution.py:126
  8.8 59.2 %all-gather.10.cloned.1.call-start = ((), (), s32[]{:S(2)}) async-start(), calls=%async_computation.16 | async-start | bytes 1474560 | tf_op jit(solution)/shard_map/all_gather | solution.py:125
  9.5 90.0 %all-gather.16.cloned.1.call-start = ((), (), s32[]{:S(2)}) async-start(), calls=%async_computation.19 | async-start | bytes 1474560 | tf_op jit(solution)/shard_map/all_gather | solution.py:129
  10.1 697.9 %all-gather.18.cloned.1.call-start = ((), (), s32[]{:S(2)}) async-start(), calls=%async_computation.20 | async-start | bytes 1474560 | tf_op jit(solution)/shard_map/all_gather | solution.py:128
  10.7 700.2 %all-gather.20.cloned.1.call-start = ((), (), s32[]{:S(2)}) async-start(), calls=%async_computation.21 | async-start | bytes 5898240 | tf_op jit(solution)/shard_map/all_gather | solution.py:136
  11.3 706.9 %all-gather.22.cloned.1.call-start = ((), (), s32[]{:S(2)}) async-start(), calls=%async_computation.22 | async-start | bytes 5898240 | tf_op jit(solution)/shard_map/all_gather | solution.py:138
  82.8 7.6 all-to-all-start.1
  90.4 56.3 %all-to-all-start = ((bf16[256,4,2,384]{3,0,1,2:T(8,128)(2,1)}), bf16[256,4,2,384]{3,0,1,2:T(8,128)(2,1)}, u32[]{:S(2)}, u32[]{:S(2)}) async-start(bf16[256,4,2,384]{3,0,1,2:T(8,128)(2,1)} %pad_maximum_fusion.3), calls=%async_computation | async-start | bytes 3145728 | tf_op jit(solution)/shard_map/all_to_all | solution.py:193
  152.5 17.1 collective-permute-start
  695.1 11.5 all-to-all-start.2
  746.6 13.6 all-to-all-start.3
  750.9 979.0 %reduce-scatter.21.cloned.1.call-start = ((), (), s32[]{:S(2)}) async-start(), calls=%async_computation.23 | async-start | bytes 491520 | tf_op jit(solution)/shard_map/reduce_scatter | solution.py:493
  770.8 639.5 %copy-start.53 = (pred[512,256]{0,1:T(8,128)(4,1)S(1)}, pred[512,256]{0,1:T(8,128)(4,1)}, u32[]{:S(2)}) copy-start(pred[512,256]{0,1:T(8,128)(4,1)} %broadcast_compare_fusion.6) | copy-start | bytes 393220
  1632.3 118.3 %reduce-scatter.37.cloned.1.call-start = ((), (), s32[]{:S(2)}) async-start(), calls=%async_computation.31 | async-start | bytes 2273280
  1648.5 147.9 %reduce-scatter.39.cloned.1.call-start = ((), (), s32[]{:S(2)}) async-start(), calls=%async_computation.32 | async-start | bytes 245760
  1658.3 45.0 %collective-permute-start.1 = (bf16[1,512,2,384]{1,3,2,0:T(8,128)(2,1)}, bf16[1,512,2,384]{1,3,2,0:T(8,128)(2,1)}, u32[]{:S(2)}, u32[]{:S(2)}) collective-permute-start(bf16[1,512,2,384]{1,3,2,0:T(8,128)(2,1)} %bitcast.92), channel_id=1, source_target_pairs={{0,8},{8,0},{16,24},{24,16},{1,9},{9,1},{17,25},{25,17},{2,10},{10... | collective-permute-start | bytes 2359304 | tf_op jit(solution)/shard_map/ppermute | solution.py:21
  1659.8 146.9 %reduce-scatter.23.cloned.1.call-start = ((), (), s32[]{:S(2)}) async-start(), calls=%async_computation.24 | async-start | bytes 1474560 | tf_op jit(solution)/shard_map/reduce_scatter | solution.py:579
  1662.9 143.9 %reduce-scatter.31.cloned.1.call-start = ((), (), s32[]{:S(2)}) async-start(), calls=%async_computation.28 | async-start | bytes 1474560
  1729.9 82.9 %reduce-scatter.35.cloned.1.call-start = ((), (), s32[]{:S(2)}) async-start(), calls=%async_computation.30 | async-start | bytes 1474560
  1745.2 95.7 %reduce-scatter.33.cloned.1.call-start = ((), (), s32[]{:S(2)}) async-start(), calls=%async_computation.29 | async-start | bytes 1474560
  1750.5 119.3 %reduce-scatter.25.cloned.1.call-start = ((), (), s32[]{:S(2)}) async-start(), calls=%async_computation.25 | async-start | bytes 1474560 | tf_op jit(solution)/shard_map/reduce_scatter | solution.py:582
  1754.7 165.3 %reduce-scatter.27.cloned.1.call-start = ((), (), s32[]{:S(2)}) async-start(), calls=%async_computation.26 | async-start | bytes 5898240 | tf_op jit(solution)/shard_map/reduce_scatter | solution.py:603
  1761.4 209.1 %reduce-scatter.29.cloned.1.call-start = ((), (), s32[]{:S(2)}) async-start(), calls=%async_computation.27 | async-start | bytes 5898240 | tf_op jit(solution)/shard_map/reduce_scatter | solution.py:609
  (134 other events, 3713.0 us)
Sparse Core Ops, SparseCore 0:
  9.6 20.2 all-gather.13
  31.4 17.4 all-gather.11
  50.5 17.4 all-gather.9
  69.4 17.4 all-gather.15
  88.3 17.4 all-gather.17
  107.2 37.4 all-gather.19
  146.3 37.4 all-gather.21
  1632.4 19.4 reduce-scatter.20
  1654.9 50.6 reduce-scatter.36
  1708.6 18.7 reduce-scatter.38
  1730.1 25.7 reduce-scatter.22
  1758.3 25.7 reduce-scatter.30
  1786.8 25.9 reduce-scatter.34
  1815.2 25.7 reduce-scatter.32
  1844.1 25.6 reduce-scatter.24
  1872.2 47.8 reduce-scatter.26
  1922.6 47.8 reduce-scatter.28
where the time goes:
time: 2320 us; the launch traced here: 2300 us
  local copies, waits for them, and re-layouts  1230 us (53%)
  blocking collectives  395 us (17%)
  matrix products  297 us (13%)
  waiting for transfers between devices  237 us (10%)
  other arithmetic  69.2 us (3%)
  loops' own time  31 us (1%)
    psum x1, blocking collectives, per_device(): lax.psum((reduced[0], reduced[1], reduced[2], reduced[3], reduced[4], red...  324 us
    reshape x9, local copies, waits for them, and re-layouts, shear_band(): part_rows.reshape(leading + (row_count, band_width))[..., :width_keys]  277 us
    reshape x9, local copies, waits for them, and re-layouts, shear_band(): flatten = padded.reshape(leading + (row_count * (band_width + 1),))  184 us
    while x64, local copies, waits for them, and re-layouts  173 us
    slice x6, local copies, waits for them, and re-layouts, shear_band(): lax.slice_in_dim(flatten, row_count - 1, row_count - 1 + row_count * band...  168 us
    pad x6, local copies, waits for them, and re-layouts, shear_band(): padded = jnp.pad(banded, [(0, 0)] * len(leading) + [(0, 0), (0, 1)])  100 us
    dot_general x6, matrix products, block_scores(): jnp.einsum('shte,hwe->shtw', with_position, band_heads, preferred_element...  73.9 us
    cond x33, local copies, waits for them, and re-layouts  56 us
  transfers between devices with their start and end apart: 23, of which 11 were waited for; matrix products, arithmetic and copies ran while one was open for 31% of the time, Pallas kernels for 0%

commit v1 on v0

v1 whole, which is shorter than its diff:
```python
from functools import partial

import jax
import jax.numpy as jnp
import numpy as np
from jax import lax
from jax.experimental import pallas as pl
from jax.experimental.pallas import tpu as pltpu
from jax.sharding import Mesh, PartitionSpec as P

D = 768
HEADS = 12
HEAD_DIM = 64
LEN = 1024
SEGMENTS = 4
TQ = 128

negative = -1e30
epsilon = 1e-06
scale_factor = HEAD_DIM ** (-0.5)
NT = (((1,), (1,)), ((), ()))
NN = (((1,), (0,)), ((), ()))
TN = (((0,), (0,)), ((), ()))

COL_HIGH = HEAD_DIM
COL_LOW = HEAD_DIM + SEGMENTS
COL_ONE = HEAD_DIM + 2 * SEGMENTS
COL_ONE_LOW = COL_ONE + 1
COL_MASK = COL_ONE + 2


def mm(a, b, dims=NN):
    return lax.dot_general(a, b, dims, preferred_element_type=jnp.float32)


def reverse_rows(x):
    groups = x.shape[0] // 8
    index = 7 - lax.broadcasted_iota(jnp.int32, (8, x.shape[1]), 0)
    return jnp.concatenate(
        [
            jnp.take_along_axis(x[8 * (groups - 1 - g) : 8 * (groups - g)], index, axis=0)
            for g in range(groups)
        ],
        axis=0,
    )


def prepare_keys(head, k_ref, v_ref, rt_ref, kinfo_ref, kaug, vaug, rt):
    cols = slice(head * HEAD_DIM, (head + 1) * HEAD_DIM)
    rows = k_ref.shape[0]
    lane = lax.broadcasted_iota(jnp.int32, (rows, HEAD_DIM), 1)
    segment = kinfo_ref[:, 0:1]
    hidden = kinfo_ref[:, 1:2]
    one_hot = ((lane == segment) | (lane - SEGMENTS == segment)) & (lane < 2 * SEGMENTS)
    ones = (lane == COL_ONE - HEAD_DIM) | (lane == COL_ONE_LOW - HEAD_DIM)
    extra = jnp.where(one_hot | ones, 1.0, 0.0)
    extra = jnp.where((lane == COL_MASK - HEAD_DIM) & (hidden > 0), negative, extra)
    kaug[:, :HEAD_DIM] = k_ref[:, cols]
    kaug[:, HEAD_DIM:] = extra.astype(jnp.bfloat16)
    vaug[:, :HEAD_DIM] = v_ref[:, cols]
    vaug[:, HEAD_DIM:] = jnp.where(lane < 2, 1.0, 0.0).astype(jnp.bfloat16)
    rt[...] = rt_ref[:, cols]


def query_terms(head, s, q_ref, bias_ref):
    cols = slice(head * HEAD_DIM, (head + 1) * HEAD_DIM)
    q = q_ref[s, :, cols].astype(jnp.float32)
    content = (q + bias_ref[0:1, cols]).astype(jnp.bfloat16).astype(jnp.float32)
    position = (q + bias_ref[1:2, cols]).astype(jnp.bfloat16).astype(jnp.float32)
    segment = q + bias_ref[2:3, cols]
    return content, position, segment


def forward_kernel(
    head, q_ref, k_ref, v_ref, rt_ref, bias_ref, qinfo_ref, kinfo_ref, rank_ref,
    p_ref, a_ref, kaug, vaug, rt, qaug,
):
    step = pl.program_id(0)
    keys = k_ref.shape[0]
    prompt = keys - LEN
    cols = slice(head * HEAD_DIM, (head + 1) * HEAD_DIM)

    @pl.when(step == 0)
    def _():
        prepare_keys(head, k_ref, v_ref, rt_ref, kinfo_ref, kaug, vaug, rt)

    start = pl.multiple_of(LEN - TQ - step * TQ, TQ)
    lane = lax.broadcasted_iota(jnp.int32, (TQ, HEAD_DIM), 1)
    segment_id = qinfo_ref[:, 0:1]
    rank = qinfo_ref[:, 1:2]
    table_p = rt[pl.ds(start, TQ + prompt), :]
    table_c = rt[pl.ds(pl.multiple_of(LEN + prompt + start, TQ), TQ + LEN), :]
    for s in range(2):
        content, position, with_segment = query_terms(head, s, q_ref, bias_ref)
        same = jnp.sum(with_segment * bias_ref[3:4, cols], axis=1, keepdims=True) * scale_factor
        other = jnp.sum(with_segment * bias_ref[4:5, cols], axis=1, keepdims=True) * scale_factor
        differ = same - other
        differ_high = differ.astype(jnp.bfloat16).astype(jnp.float32)
        other_high = other.astype(jnp.bfloat16).astype(jnp.float32)
        extra = jnp.where(lane == segment_id, differ_high, 0.0)
        extra = jnp.where(lane - SEGMENTS == segment_id, differ - differ_high, extra)
        extra = jnp.where(lane == COL_ONE - HEAD_DIM, other_high, extra)
        extra = jnp.where(lane == COL_ONE_LOW - HEAD_DIM, other - other_high, extra)
        extra = jnp.where(lane == COL_MASK - HEAD_DIM, 1.0, extra)
        qaug[:, :HEAD_DIM] = (content * scale_factor).astype(jnp.bfloat16)
        qaug[:, HEAD_DIM:] = extra.astype(jnp.bfloat16)
        scores = mm(qaug[...], kaug[...], NT)
        position = (position * scale_factor).astype(jnp.bfloat16)
        band_p = pltpu.roll(
            mm(position, table_p, NT), prompt + 1, axis=1, stride=1, stride_axis=0
        )
        band_c = pltpu.roll(mm(position, table_c, NT), LEN + 1, axis=1, stride=1, stride_axis=0)
        scores_p = scores[:, :prompt] + band_p[:, :prompt]
        scores_c = scores[:, prompt:] + band_c[:, :LEN]
        scores_c = jnp.where(rank_ref[0:1, :] <= rank - s, scores_c, negative)
        largest = jnp.maximum(
            jnp.max(scores_p, axis=1, keepdims=True), jnp.max(scores_c, axis=1, keepdims=True)
        )
        weights_p = jnp.exp(scores_p - largest)
        weights_c = jnp.exp(scores_c - largest)
        mixed = mm(weights_p.astype(jnp.bfloat16), vaug[:prompt, :])
        mixed += mm(weights_c.astype(jnp.bfloat16), vaug[prompt:, :])
        inverse = 1.0 / mixed[:, HEAD_DIM : HEAD_DIM + 1]
        wide = lax.broadcasted_iota(jnp.int32, (TQ, 2 * HEAD_DIM), 1)
        a_ref[s] = jnp.where(wide < HEAD_DIM, mixed * inverse, inverse)
        rows = slice(s * TQ, (s + 1) * TQ)
        p_ref[0, rows, :prompt] = reverse_rows(weights_p).astype(jnp.bfloat16)
        p_ref[0, rows, prompt:] = reverse_rows(weights_c).astype(jnp.bfloat16)


def backward_kernel(
    head, q_ref, k_ref, v_ref, rt_ref, bias_ref, qinfo_ref, kinfo_ref, p_ref, a_ref, ag_ref,
    dq_ref, dk_ref, dv_ref, dt_ref, sum_ref,
    kaug, vaug, rt, agaug, cw, cr, g_all, band_p, band_c, dk_acc, dv_acc, dt_acc,
):
    step = pl.program_id(0)
    keys = k_ref.shape[0]
    prompt = keys - LEN
    cols = slice(head * HEAD_DIM, (head + 1) * HEAD_DIM)

    @pl.when(step == 0)
    def _():
        prepare_keys(head, k_ref, v_ref, rt_ref, kinfo_ref, kaug, vaug, rt)
        dk_acc[...] = jnp.zeros_like(dk_acc)
        dv_acc[...] = jnp.zeros_like(dv_acc)
        dt_acc[...] = jnp.zeros_like(dt_acc)
        sum_ref[...] = jnp.zeros_like(sum_ref)

    start = pl.multiple_of(LEN - TQ - step * TQ, TQ)
    start_c = pl.multiple_of(LEN + prompt + start, TQ)
    lane = lax.broadcasted_iota(jnp.int32, (TQ, HEAD_DIM), 1)
    segment_id = qinfo_ref[:, 2:3]
    segments = []
    for s in range(2):
        rows = slice(s * TQ, (s + 1) * TQ)
        content, position, with_segment = query_terms(head, s, q_ref, bias_ref)
        cw[rows, :] = reverse_rows(content).astype(jnp.bfloat16)
        cr[rows, :] = reverse_rows(position).astype(jnp.bfloat16)
        segments.append(reverse_rows(with_segment))
        grad = ag_ref[0, s, :, cols].astype(jnp.float32)
        inverse = a_ref[s, :, HEAD_DIM : HEAD_DIM + 1] * scale_factor
        delta = jnp.sum(grad * a_ref[s, :, :HEAD_DIM], axis=1, keepdims=True) * inverse
        delta_high = delta.astype(jnp.bfloat16).astype(jnp.float32)
        extra = jnp.where(lane == 0, -delta_high, jnp.where(lane == 1, delta_high - delta, 0.0))
        agaug[rows, :HEAD_DIM] = reverse_rows(grad * inverse).astype(jnp.bfloat16)
        agaug[rows, HEAD_DIM:] = reverse_rows(extra).astype(jnp.bfloat16)
    share_grad = mm(agaug[...], vaug[...], NT)
    g_all[...] = (p_ref[0].astype(jnp.float32) * share_grad).astype(jnp.bfloat16)
    for s in range(2):
        rows = slice(s * TQ, (s + 1) * TQ)
        blank = jnp.zeros((TQ, TQ), jnp.bfloat16)
        wide_p = jnp.concatenate([g_all[rows, :prompt], blank], axis=1)
        wide_c = jnp.concatenate([g_all[rows, prompt:], blank], axis=1)
        band_p[rows, :] = pltpu.roll(wide_p, 0, axis=1, stride=1, stride_axis=0)
        band_c[rows, :] = pltpu.roll(wide_c, 0, axis=1, stride=1, stride_axis=0)
    dv_acc[...] += mm(agaug[:, :HEAD_DIM], p_ref[0], TN)
    dk_acc[...] += mm(cw[...], g_all[...], TN)
    dt_acc[:, pl.ds(start, TQ + prompt)] += mm(cr[...], band_p[...], TN)
    dt_acc[:, pl.ds(start_c, TQ + LEN)] += mm(cr[...], band_c[...], TN)
    query_content = mm(g_all[...], kaug[...])
    query_position = mm(band_p[...], rt[pl.ds(start, TQ + prompt), :])
    query_position += mm(band_c[...], rt[pl.ds(start_c, TQ + LEN), :])
    same_vector = bias_ref[3:4, cols]
    other_vector = bias_ref[4:5, cols]

    def add_row(row, value):
        sum_ref[row : row + 1, :] += jnp.sum(value, axis=0, keepdims=True)

    for s in range(2):
        rows = slice(s * TQ, (s + 1) * TQ)
        from_content = query_content[rows, :HEAD_DIM]
        extra = query_content[rows, HEAD_DIM:]
        hit = (lane == segment_id) & (lane < SEGMENTS)
        same = jnp.sum(jnp.where(hit, extra, 0.0), axis=1, keepdims=True)
        other = extra[:, COL_ONE - HEAD_DIM : COL_ONE - HEAD_DIM + 1] - same
        from_segment = same * same_vector + other * other_vector
        from_position = query_position[rows, :]
        total = reverse_rows(from_content + from_position + from_segment)
        dq_ref[0, s] = total.astype(jnp.bfloat16)
        add_row(0, from_content)
        add_row(1, from_position)
        add_row(2, from_segment)
        add_row(3, same * segments[s])
        add_row(4, other * segments[s])

    @pl.when(step == pl.num_programs(0) - 1)
    def _():
        dk_ref[...] = dk_acc[...].T.astype(jnp.bfloat16)
        dv_ref[...] = (dv_acc[...].T * HEAD_DIM**0.5).astype(jnp.bfloat16)
        dt_ref[...] = dt_acc[...].T.astype(jnp.bfloat16)


def whole(shape):
    return pl.BlockSpec(shape, lambda i: (0,) * len(shape))


def attend_forward(head, q, k, v, rt, bias, qinfo, kinfo, ranks):
    keys, width = k.shape
    table = rt.shape[0]
    steps = LEN // TQ
    return pl.pallas_call(
        partial(forward_kernel, head),
        grid=(steps,),
        in_specs=[
            pl.BlockSpec((2, TQ, width), lambda i: (0, i, 0)),
            whole((keys, width)),
            whole((keys, width)),
            whole((table, width)),
            whole(bias.shape),
            pl.BlockSpec((TQ, qinfo.shape[1]), lambda i: (i, 0)),
            whole(kinfo.shape),
            whole(ranks.shape),
        ],
        out_specs=[
            pl.BlockSpec((1, 2 * TQ, keys), lambda i: (i, 0, 0)),
            pl.BlockSpec((2, TQ, 2 * HEAD_DIM), lambda i: (0, i, 0)),
        ],
        out_shape=[
            jax.ShapeDtypeStruct((steps, 2 * TQ, keys), jnp.bfloat16),
            jax.ShapeDtypeStruct((2, LEN, 2 * HEAD_DIM), jnp.float32),
        ],
        scratch_shapes=[
            pltpu.VMEM((keys, 2 * HEAD_DIM), jnp.bfloat16),
            pltpu.VMEM((keys, 2 * HEAD_DIM), jnp.bfloat16),
            pltpu.VMEM((table, HEAD_DIM), jnp.bfloat16),
            pltpu.VMEM((TQ, 2 * HEAD_DIM), jnp.bfloat16),
        ],
        compiler_params=pltpu.CompilerParams(vmem_limit_bytes=48 * 2**20),
        cost_estimate=pl.CostEstimate(
            flops=6 * 2 * LEN * keys * 256, bytes_accessed=2 * LEN * keys * 2, transcendentals=2 * LEN * keys
        ),
        name="attend_forward",
    )(q, k, v, rt, bias, qinfo, kinfo, ranks)


def attend_backward(head, q, k, v, rt, bias, qinfo, kinfo, p, a, ag):
    keys, width = k.shape
    table = rt.shape[0]
    steps = LEN // TQ
    prompt = keys - LEN
    per = ag.shape[2] // TQ
    return pl.pallas_call(
        partial(backward_kernel, head),
        grid=(steps,),
        in_specs=[
            pl.BlockSpec((2, TQ, width), lambda i: (0, i, 0)),
            whole((keys, width)),
            whole((keys, width)),
            whole((table, width)),
            whole(bias.shape),
            pl.BlockSpec((TQ, qinfo.shape[1]), lambda i: (i, 0)),
            whole(kinfo.shape),
            pl.BlockSpec((1, 2 * TQ, keys), lambda i: (i, 0, 0)),
            pl.BlockSpec((2, TQ, 2 * HEAD_DIM), lambda i: (0, i, 0)),
            pl.BlockSpec((1, 2, TQ, width), lambda i: (i // per, 0, i % per, 0)),
        ],
        out_specs=[
            pl.BlockSpec((1, 2, TQ, HEAD_DIM), lambda i: (i // per, 0, i % per, 0)),
            whole((keys, HEAD_DIM)),
            whole((keys, HEAD_DIM)),
            whole((table, HEAD_DIM)),
            whole((8, HEAD_DIM)),
        ],
        out_shape=[
            jax.ShapeDtypeStruct(ag.shape[:3] + (HEAD_DIM,), jnp.bfloat16),
            jax.ShapeDtypeStruct((keys, HEAD_DIM), jnp.bfloat16),
            jax.ShapeDtypeStruct((keys, HEAD_DIM), jnp.bfloat16),
            jax.ShapeDtypeStruct((table, HEAD_DIM), jnp.bfloat16),
            jax.ShapeDtypeStruct((8, HEAD_DIM), jnp.float32),
        ],
        scratch_shapes=[
            pltpu.VMEM((keys, 2 * HEAD_DIM), jnp.bfloat16),
            pltpu.VMEM((keys, 2 * HEAD_DIM), jnp.bfloat16),
            pltpu.VMEM((table, HEAD_DIM), jnp.bfloat16),
            pltpu.VMEM((2 * TQ, 2 * HEAD_DIM), jnp.bfloat16),
            pltpu.VMEM((2 * TQ, HEAD_DIM), jnp.bfloat16),
            pltpu.VMEM((2 * TQ, HEAD_DIM), jnp.bfloat16),
            pltpu.VMEM((2 * TQ, keys), jnp.bfloat16),
            pltpu.VMEM((2 * TQ, TQ + prompt), jnp.bfloat16),
            pltpu.VMEM((2 * TQ, TQ + LEN), jnp.bfloat16),
            pltpu.VMEM((HEAD_DIM, keys), jnp.float32),
            pltpu.VMEM((HEAD_DIM, keys), jnp.float32),
            pltpu.VMEM((HEAD_DIM, table), jnp.float32),
        ],
        compiler_params=pltpu.CompilerParams(vmem_limit_bytes=48 * 2**20),
        cost_estimate=pl.CostEstimate(
            flops=12 * 2 * LEN * keys * 256, bytes_accessed=2 * LEN * keys * 2, transcendentals=0
        ),
        name="attend_backward",
    )(q, k, v, rt, bias, qinfo, kinfo, p, a, ag)


def axes_size(axes):
    size = 1
    for name in axes:
        size *= lax.axis_size(name)
    return size


def flat_index(axes):
    index = 0
    for name in axes:
        index = index * lax.axis_size(name) + lax.axis_index(name)
    return index


def swap(x, axes, mask):
    return lax.ppermute(x, axes, [(i, i ^ mask) for i in range(axes_size(axes))])


def gather(x, axes, order=None):
    count = axes_size(axes)
    index = flat_index(axes)
    pieces = {0: x}
    bits = list(range(count.bit_length() - 1))
    for bit in reversed(bits) if order is None else order:
        for mask in list(pieces):
            pieces[mask | 1 << bit] = swap(pieces[mask], axes, 1 << bit)
    result = jnp.zeros((count,) + x.shape, x.dtype)
    for mask, piece in pieces.items():
        result = lax.dynamic_update_slice(
            result, piece[None], (index ^ mask,) + (0,) * x.ndim
        )
    return result


def pick(x, index):
    return lax.dynamic_index_in_dim(x, index, 0, keepdims=False)


def scatter_sum(x, axes):
    count = axes_size(axes)
    index = flat_index(axes)
    for bit in range(count.bit_length() - 1):
        x = x.reshape((x.shape[0] // 2, 2) + x.shape[1:])
        own = index >> bit & 1
        kept = lax.dynamic_index_in_dim(x, own, 1, keepdims=False)
        sent = lax.dynamic_index_in_dim(x, 1 - own, 1, keepdims=False)
        x = kept.astype(jnp.float32) + swap(sent.astype(jnp.bfloat16), axes, 1 << bit).astype(
            jnp.float32
        )
    return x[0]


def total_sum(x, stages):
    taken = []
    for axes, mask in stages:
        bit = mask.bit_length() - 1
        own = flat_index(axes) >> bit & 1
        x = x.reshape((2, x.shape[0] // 2) + x.shape[1:])
        sent = pick(x, 1 - own).astype(jnp.bfloat16)
        x = pick(x, own).astype(jnp.float32) + swap(sent, axes, mask).astype(jnp.float32)
        taken.append((axes, mask, own))
    x = x.astype(jnp.bfloat16)
    for axes, mask, own in reversed(taken):
        other = swap(x, axes, mask)
        pair = jnp.zeros((2,) + x.shape, x.dtype)
        pair = lax.dynamic_update_slice(pair, x[None], (own,) + (0,) * x.ndim)
        pair = lax.dynamic_update_slice(pair, other[None], (1 - own,) + (0,) * x.ndim)
        x = pair.reshape((2 * x.shape[0],) + x.shape[1:])
    return x


def bit_stages(axes):
    return [((name,), 1 << bit) for name in axes for bit in range(lax.axis_size(name).bit_length() - 1)]


def layer_norm(values, gain_vector, shift_vector):
    center = values - jnp.mean(values, axis=-1, keepdims=True)
    spread = jnp.mean(center * center, axis=-1, keepdims=True)
    return center * lax.rsqrt(spread + epsilon) * gain_vector + shift_vector


def project(rows_in, weight):
    return jnp.dot(rows_in, weight, preferred_element_type=jnp.float32)


def back_through(grad_rows, weight):
    return jnp.einsum("rc,dc->rd", grad_rows, weight, preferred_element_type=jnp.float32)


def outer_sum(rows_in, grad_rows):
    return jnp.einsum("rd,rc->dc", rows_in, grad_rows, preferred_element_type=jnp.float32)


def sinusoid_rows(first, rows):
    frequency = jnp.asarray(
        np.power(10000.0, -2.0 * np.arange(D // 2) / D).astype(np.float32)
    )
    fine = jnp.arange(64, dtype=jnp.float32)[:, None] * frequency
    coarse = (first - 64 * jnp.arange(rows // 64, dtype=jnp.int32)).astype(jnp.float32)
    coarse = coarse[:, None] * frequency
    fs, fc = jnp.sin(fine)[None], jnp.cos(fine)[None]
    cs, cc = jnp.sin(coarse)[:, None], jnp.cos(coarse)[:, None]
    both = jnp.concatenate([cs * fc - cc * fs, cc * fc + cs * fs], axis=-1)
    return both.reshape(rows, D).astype(jnp.bfloat16)


GROUP = ("half", "head")
JOB = ("cont", "half", "head")


def per_device(
    prompt_states, content_states, query_states, visible_length, start_offsets,
    prompt_segments, token_segments, order_ranks,
    query_weights, key_weights, value_weights, output_weights, relative_weights,
    content_bias, position_bias, segment_bias, segment_vectors,
    attention_gain, attention_shift, hidden_weights, hidden_bias, return_weights, return_bias,
    final_gain, final_shift, content_upstream, query_upstream,
):
    members = axes_size(GROUP)
    member = flat_index(GROUP)
    shards = lax.axis_size("wshard")
    shard = lax.axis_index("wshard")
    chapter = lax.axis_index("cont")
    width = D // members
    local_heads = HEADS // members
    prompt_rows = prompt_states[0]
    content_rows = content_states[0]
    query_rows = query_states[0]
    tokens = content_rows.shape[0]
    prompt_part = prompt_rows.shape[0]
    prompt_total = prompt_segments.shape[1]
    keys = prompt_total + LEN
    rows_w = query_weights.shape[0]

    def columns(x):
        return lax.dynamic_slice_in_dim(x, member * width, width, x.ndim - 1)

    first_weights = jnp.stack(
        [columns(w) for w in (query_weights, key_weights, value_weights, relative_weights)], axis=0
    )
    small = jnp.concatenate(
        [
            jnp.stack([content_bias, position_bias, segment_bias]),
            segment_vectors,
            jnp.stack([attention_gain, attention_shift, return_bias, final_gain, final_shift]),
            hidden_bias.reshape(-1, rows_w),
        ],
        axis=0,
    )
    first_full = gather(first_weights, ("wshard",))
    small_full = gather(small, ("wshard",))
    content_all = gather(content_rows, GROUP, (1, 0)).reshape(LEN, D)
    query_all = gather(query_rows, GROUP, (0, 1)).reshape(LEN, D)
    prompt_all = gather(prompt_rows, JOB).reshape(prompt_total, D)
    output_full = gather(output_weights, ("wshard",)).reshape(D, D)
    hidden_full = gather(hidden_weights, ("wshard",)).reshape(D, -1)
    return_full = gather(return_weights, ("wshard",)).reshape(-1, D)
    query_full = gather(query_weights, ("wshard",)).reshape(D, D)
    key_full = gather(key_weights, ("wshard",)).reshape(D, D)
    value_full = gather(value_weights, ("wshard",)).reshape(D, D)

    vectors = jnp.transpose(small_full, (1, 0, 2))
    inner_full = small_full[:, 10:].reshape(-1).astype(jnp.float32)
    vectors = vectors[:10].reshape(10, D).astype(jnp.float32)
    head_bias = jnp.concatenate([columns(vectors[:5]), jnp.zeros((3, width), jnp.float32)])
    attention_scale, attention_offset, outer_full, final_scale, final_offset = vectors[5:]

    seen = pick(visible_length[0], chapter)
    base = seen + pick(start_offsets[0], chapter)
    segments = lax.dynamic_slice_in_dim(token_segments[0], chapter * LEN, LEN)
    ranks = lax.dynamic_slice_in_dim(order_ranks[0], chapter * LEN, LEN)
    reversed_segments = jnp.flip(segments.reshape(-1, TQ), 1).reshape(-1)
    qinfo = jnp.stack([segments, ranks, reversed_segments, segments], axis=1)
    key_segments = jnp.concatenate([prompt_segments[0], segments])
    hidden_keys = (jnp.arange(keys, dtype=jnp.int32) < prompt_total) & (
        jnp.arange(keys, dtype=jnp.int32) >= seen
    )
    kinfo = jnp.stack([key_segments, hidden_keys.astype(jnp.int32)], axis=1)
    rank_row = ranks[None]
    positions = jnp.concatenate(
        [
            sinusoid_rows(base + LEN - 1, LEN + prompt_total),
            sinusoid_rows(jnp.int32(LEN - 1), 2 * LEN),
        ]
    )

    first_full = jnp.transpose(first_full, (1, 0, 2, 3)).reshape(4, D, width)
    streams_all = jnp.concatenate([content_all, query_all])
    sources_all = jnp.concatenate([prompt_all, content_all])
    q = project(streams_all, first_full[0]).astype(jnp.bfloat16).reshape(2, LEN, width)
    k = project(sources_all, first_full[1]).astype(jnp.bfloat16)
    v = project(sources_all, first_full[2]).astype(jnp.bfloat16)
    rt = project(positions, first_full[3]).astype(jnp.bfloat16)

    forward = [
        attend_forward(h, q, k, v, rt, head_bias, qinfo, kinfo, rank_row)
        for h in range(local_heads)
    ]
    mixture = jnp.concatenate([a[:, :, :HEAD_DIM] for _, a in forward], axis=-1)
    mixture = jnp.transpose(
        mixture.astype(jnp.bfloat16).reshape(2, members, tokens, width), (1, 0, 2, 3)
    )
    mixture = lax.all_to_all(mixture, GROUP, 0, 0, tiled=True)
    mixed_flat = jnp.transpose(mixture, (1, 2, 0, 3)).reshape(2 * tokens, D)

    streams_in = jnp.concatenate([content_rows, query_rows], axis=0).astype(jnp.float32)
    branch = project(mixed_flat, output_full)
    middle, norm_back = jax.vjp(
        layer_norm, streams_in + branch, attention_scale, attention_offset
    )
    inner_in = middle.astype(jnp.bfloat16)
    inner_sum = project(inner_in, hidden_full) + inner_full
    active, gelu_back = jax.vjp(partial(jax.nn.gelu, approximate=True), inner_sum)
    active_low = active.astype(jnp.bfloat16)
    returned = project(active_low, return_full) + outer_full
    normed, final_back = jax.vjp(layer_norm, middle + returned, final_scale, final_offset)
    upstream = jnp.concatenate([content_upstream[0], query_upstream[0]], axis=0).astype(jnp.float32)
    sum_grad, closing_grad, ending_grad = final_back(upstream)
    returned_grad = sum_grad.astype(jnp.bfloat16)
    outer_grad = jnp.sum(returned_grad.astype(jnp.float32), axis=0)
    active_grad = back_through(returned_grad, return_full)
    inner_grad = gelu_back(active_grad)[0].astype(jnp.bfloat16)
    inner_bias_grad = jnp.sum(inner_grad.astype(jnp.float32), axis=0)
    middle_grad = sum_grad + back_through(inner_grad, hidden_full)
    residual_grad, scale_grad, offset_grad = norm_back(middle_grad)
    branch_grad = residual_grad.astype(jnp.bfloat16)
    mixed_grad = back_through(branch_grad, output_full).astype(jnp.bfloat16)
    grad_out = jnp.transpose(mixed_grad.reshape(2, tokens, members, width), (2, 0, 1, 3))
    grad_out = lax.all_to_all(grad_out, GROUP, 0, 0, tiled=True)

    return_grad = outer_sum(active_low, returned_grad)
    hidden_grad = outer_sum(inner_in, inner_grad)
    output_grad = outer_sum(mixed_flat, branch_grad)
    stages = bit_stages(("head", "half", "cont"))
    return_part = scatter_sum(return_grad.reshape(shards, -1, D), ("wshard",))
    hidden_part = scatter_sum(hidden_grad.reshape(shards, rows_w, -1), ("wshard",))
    output_part = scatter_sum(output_grad.reshape(shards, rows_w, D), ("wshard",))
    return_total = total_sum(return_part, stages).astype(jnp.float32)
    hidden_total = total_sum(hidden_part, stages).astype(jnp.float32)
    output_total = total_sum(output_part, stages).astype(jnp.float32)

    backward = [
        attend_backward(
            h, q, k, v, rt, head_bias, qinfo, kinfo, forward[h][0], forward[h][1], grad_out
        )
        for h in range(local_heads)
    ]
    dq = jnp.concatenate([b[0] for b in backward], axis=-1)
    dk = jnp.concatenate([b[1] for b in backward], axis=-1)
    dv = jnp.concatenate([b[2] for b in backward], axis=-1)
    dt = jnp.concatenate([b[3] for b in backward], axis=-1)
    sums = jnp.concatenate([b[4] for b in backward], axis=-1)

    token_back = jnp.concatenate(
        [
            dq,
            dk[prompt_total:].reshape(members, 1, tokens, width),
            dv[prompt_total:].reshape(members, 1, tokens, width),
        ],
        axis=1,
    )
    token_back = lax.all_to_all(token_back, GROUP, 0, 0, tiled=True)
    token_back = jnp.transpose(token_back, (1, 2, 0, 3)).reshape(4, tokens, D)
    chapters = lax.axis_size("cont")
    prompt_back = jnp.stack([dk[:prompt_total], dv[:prompt_total]]).reshape(
        2, chapters * members, prompt_part, width
    )
    prompt_back = lax.all_to_all(jnp.transpose(prompt_back, (1, 0, 2, 3)), JOB, 0, 0, tiled=True)
    prompt_back = jnp.sum(
        prompt_back.reshape(chapters, members, 2, prompt_part, width).astype(jnp.float32), axis=0
    ).astype(jnp.bfloat16)
    prompt_back = jnp.transpose(prompt_back, (1, 2, 0, 3)).reshape(2, prompt_part, D)

    dq_rows = jnp.transpose(dq, (1, 0, 2, 3)).reshape(2 * LEN, width)
    head_grads = jnp.concatenate(
        [
            outer_sum(streams_all, dq_rows),
            outer_sum(sources_all, dk),
            outer_sum(sources_all, dv),
            outer_sum(positions, dt),
        ],
        axis=1,
    ).reshape(shards, rows_w, 4 * width)

    placed = lax.dynamic_update_slice_in_dim(
        jnp.zeros((5, D), jnp.float32), sums[:5], member * width, 1
    )
    token_sums = jnp.stack([scale_grad, offset_grad, outer_grad, closing_grad, ending_grad])
    small_grads = jnp.concatenate([placed, token_sums]).reshape(10, shards, rows_w)
    small_grads = jnp.transpose(small_grads, (1, 0, 2)).reshape(shards, -1)
    small_grads = jnp.concatenate([small_grads, inner_bias_grad.reshape(shards, -1)], axis=1)
    unit = 8 * lax.axis_size("cont")
    small_rows = rows_w - (-small_grads.shape[1] // (4 * width))
    small_rows = -(-small_rows // unit) * unit - rows_w
    small_grads = jnp.pad(
        small_grads, ((0, 0), (0, small_rows * 4 * width - small_grads.shape[1]))
    ).reshape(shards, small_rows, 4 * width)
    head_part = scatter_sum(jnp.concatenate([head_grads, small_grads], axis=1), ("wshard",))
    head_part = total_sum(head_part, bit_stages(("cont",)))
    head_total = gather(head_part, GROUP).astype(jnp.float32)
    weights_total = jnp.transpose(
        head_total[:, :rows_w].reshape(members, rows_w, 4, width), (2, 1, 0, 3)
    ).reshape(4, rows_w, D)
    small_total = jnp.sum(head_total[:, rows_w:], axis=0).reshape(-1)
    vector_total = small_total[: 10 * rows_w].reshape(10, rows_w)
    inner_total = small_total[10 * rows_w : 10 * rows_w + inner_bias_grad.shape[0] // shards]

    content_grad = (
        residual_grad[:tokens]
        + back_through(token_back[0], query_full)
        + back_through(token_back[2], key_full)
        + back_through(token_back[3], value_full)
    )
    queries_grad = residual_grad[tokens:] + back_through(token_back[1], query_full)
    prompt_grad = back_through(prompt_back[0], key_full) + back_through(prompt_back[1], value_full)
    return (
        normed[:tokens].astype(jnp.bfloat16)[None],
        normed[tokens:].astype(jnp.bfloat16)[None],
        prompt_grad.astype(jnp.bfloat16)[None],
        content_grad.astype(jnp.bfloat16)[None],
        queries_grad.astype(jnp.bfloat16)[None],
        weights_total[0],
        weights_total[1],
        weights_total[2],
        output_total,
        weights_total[3],
        vector_total[0],
        vector_total[1],
        vector_total[2],
        vector_total[3:5],
        vector_total[5],
        vector_total[6],
        hidden_total,
        inner_total,
        return_total,
        vector_total[7],
        vector_total[8],
        vector_total[9],
    )


def solution(mesh):
    rows = P("wshard", JOB, None)
    job = P("wshard", None)
    matrix = P("wshard", None)
    vector = P("wshard")
    pair = P(None, "wshard")
    in_specs = (
        (rows,) * 3 + (job,) * 5 + (matrix,) * 5 + (vector,) * 3 + (pair,)
        + (vector, vector, matrix, vector, matrix, vector, vector, vector, rows, rows)
    )
    out_specs = (
        (rows,) * 5 + (matrix,) * 5 + (vector,) * 3 + (pair,)
        + (vector, vector, matrix, vector, matrix, vector, vector, vector)
    )

    def run(*arguments):
        seq_count, head_count, shard_count = mesh.devices.shape
        tokens = arguments[1].shape[1] // (seq_count * head_count)
        halves = LEN // (tokens * head_count)
        split = Mesh(
            mesh.devices.reshape(seq_count // halves, halves, head_count, shard_count),
            ("cont", "half", "head", "wshard"),
        )
        return jax.shard_map(
            per_device, mesh=split, in_specs=in_specs, out_specs=out_specs, check_vma=False
        )(*arguments)

    return run
```

time: 2320 us -> 632 us (0.27)
  local copies, waits for them, and re-layouts: 1230 us -> 146 us
  blocking collectives: 395 us -> 0 us
  matrix products: 297 us -> 90.3 us
  Pallas kernels: 0 us -> 112 us
  waiting for transfers between devices: 237 us -> 137 us
  starting transfers between devices: 20.4 us -> 87.1 us
  loops' own time: 31 us -> 0 us
  other arithmetic: 69.2 us -> 44.2 us
    reshape x25 -> x7, local copies, waits for them, and re-layouts: 468 us -> 9.94 us  [the longest x1 3.65 us: per_device(): head_total[:, :rows_w].reshape(members, rows_w, 4, width)]
    psum x1 -> x0, blocking collectives: 324 us -> none  [per_device(): lax.psum((reduced[0], reduced[1], reduced[2], reduced[3], reduced[4], red...]
    dot_general x38 -> x0, matrix products: 221 us -> none  [the longest x6 73.9 us: block_scores(): jnp.einsum('shte,hwe->shtw', with_position, band_heads, preferred_element...]
    slice x19 -> x21, local copies, waits for them, and re-layouts: 226 us -> 13.7 us  [the longest x2 4.05 us: per_device(): weights_total[3]]
    pad x12 -> x0, local copies, waits for them, and re-layouts: 180 us -> none  [the longest x6 100 us: shear_band(): padded = jnp.pad(banded, [(0, 0)] * len(leading) + [(0, 0), (0, 1)])]
    while x64 -> x0, local copies, waits for them, and re-layouts: 173 us -> none
    reduce_scatter x5 -> x0, waiting for transfers between devices: 128 us -> none  [the longest x1 50.4 us: per_device(): lax.psum_scatter(return_grad.astype(jnp.bfloat16), 'wshard', scatter_dime...]
    pallas_call x0 -> x6, Pallas kernels: none -> 112 us  [the longest x3 60.3 us: attend_forward(): pl.pallas_call(partial(forward_kernel, head), grid=(steps,), in_specs=[pl...]
  transfers between devices with their start and end apart: 23 -> 72, of which waited for: 11 -> 35; matrix products, arithmetic and copies ran while one was open for 31% -> 36% of each run, Pallas kernels for 0% -> 18%
where the time goes in v1:
time: 632 us; the launch traced here: 621 us
  local copies, waits for them, and re-layouts  146 us (23%)
  waiting for transfers between devices  137 us (22%)
  Pallas kernels  112 us (18%)
  matrix products  90.3 us (14%)
  starting transfers between devices  87.1 us (14%)
  other arithmetic  44.2 us (7%)
    ppermute x68, waiting for transfers between devices, swap(): lax.ppermute(x, axes, [(i, i ^ mask) for i in range(axes_size(axes))])  136 us
    ppermute x68, starting transfers between devices, swap(): lax.ppermute(x, axes, [(i, i ^ mask) for i in range(axes_size(axes))])  70.1 us
    pallas_call x3, Pallas kernels, attend_forward(): pl.pallas_call(partial(forward_kernel, head), grid=(steps,), in_specs=[pl...  60.3 us
    pallas_call x3, Pallas kernels, attend_backward(): pl.pallas_call(partial(backward_kernel, head), grid=(steps,), in_specs=[p...  52.1 us
    dynamic_update_slice x51, local copies, waits for them, and re-layouts, gather(): lax.dynamic_update_slice(result, piece[None], (index ^ mask,) + (0,) * x....  40.9 us
    dot_general x7, matrix products, project(): return jnp.dot(rows_in, weight, preferred_element_type=jnp.float32)  36.8 us
    dot_general x9, matrix products, back_through(): jnp.einsum('rc,dc->rd', grad_rows, weight, preferred_element_type=jnp.flo...  28 us
    dot_general x7, matrix products, outer_sum(): jnp.einsum('rd,rc->dc', rows_in, grad_rows, preferred_element_type=jnp.fl...  25.5 us
  transfers between devices with their start and end apart: 72, of which 35 were waited for; matrix products, arithmetic and copies ran while one was open for 36% of the time, Pallas kernels for 18%

profile of v1, /device:TPU:0, one launch (start us, length us, event | category | flops | bytes accessed | tf_op | source)
XLA Modules:
  0.0 620.9 jit_solution(408498590558293714)
XLA Ops:
  75.4 6.2 %collective-permute-done.19 = bf16[192,768]{1,0:T(8,128)(2,1)S(1)} collective-permute-done((bf16[192,768]{1,0:T(8,128)(2,1)}, bf16[192,768]{1,0:T(8,128)(2,1)S(1)}, u32[]{:S(2)}, u32[]{:S(2)}) %collective-permute-start.19) | collective-permute-done | bytes 294944 | tf_op jit(solution)/shard_map/ppermute | solution.py:328
  84.8 5.6 collective-permute-done.31
  108.1 5.4 collective-permute-done.3
  129.2 17.8 %convolution_convert_fusion.rt_ref = bf16[3328,192]{1,0:T(8,128)(2,1)} fusion(bf16[768,192]{1,0:T(8,128)(2,1)S(1)} %bitcast.469, bf16[2048,384]{1,0:T(8,128)(2,1)S(1)} %bitcast.438, bf16[2048,384]{1,0:T(8,128)(2,1)S(1)} %bitcast.436, bf16[1280,384]{1,0:T(8,128)(2,1)S(1)} %bitcast.454, bf16[1280,384]{1,0:T(8,128)(2,1)S(1)} %bitcast.452), kind=kOutput, calls=%fused_computation.11 | convolution fusion | flops 1002553344 | bytes 6684672 | tf_op jit(solution)/shard_map/dot_general | solution.py:395
  152.7 7.4 %collective-permute-done.5 = bf16[256,768]{1,0:T(8,128)(2,1)S(1)} collective-permute-done((bf16[256,768]{1,0:T(8,128)(2,1)S(1)}, bf16[256,768]{1,0:T(8,128)(2,1)S(1)}, u32[]{:S(2)}, u32[]{:S(2)}) %collective-permute-start.5) | collective-permute-done | bytes 393248 | tf_op jit(solution)/shard_map/ppermute | solution.py:328
  170.9 19.0 %attend_forward.5 = (bf16[8,256,1280]{2,1,0:T(8,128)(2,1)}, f32[2,1024,128]{2,1,0:T(8,128)S(1)}) custom-call(bf16[2,1024,192]{2,1,0:T(8,128)(2,1)S(1)} %bitcast.381, bf16[1280,192]{1,0:T(8,128)(2,1)S(1)} %convolution_convert_fusion.2.k_ref, bf16[1280,192]{1,0:T(8,128)(2,1)S(1)} %convolution_convert_fusion.1.v_ref, ...), custom_call_target="tpu_custom_call" | custom-call | flops 4026531840 | bytes 5242880 | tf_op jit(solution)/shard_map/attend_forward/pallas_call | solution.py:221
  194.3 22.3 %attend_forward.4 = (bf16[8,256,1280]{2,1,0:T(8,128)(2,1)}, f32[2,1024,128]{2,1,0:T(8,128)S(1)}) custom-call(bf16[2,1024,192]{2,1,0:T(8,128)(2,1)S(1)} %bitcast.382, bf16[1280,192]{1,0:T(8,128)(2,1)S(1)} %convolution_convert_fusion.2.k_ref, bf16[1280,192]{1,0:T(8,128)(2,1)S(1)} %copy-done.11, bf16[3328,192]{1,0:T(8,128)(2,1)} %convolution_convert_fusion.rt_ref, ...), custom_call_target="tpu_custom_call" | custom-call | flops 4026531840 | bytes 5242880 | tf_op jit(solution)/shard_map/attend_forward/pallas_call | solution.py:221
  220.8 18.9 %attend_forward.3 = (bf16[8,256,1280]{2,1,0:T(8,128)(2,1)}, f32[2,1024,128]{2,1,0:T(8,128)S(1)}) custom-call(bf16[2,1024,192]{2,1,0:T(8,128)(2,1)S(1)} %bitcast.383, bf16[1280,192]{1,0:T(8,128)(2,1)S(1)} %convolution_convert_fusion.2.k_ref, bf16[1280,192]{1,0:T(8,128)(2,1)S(1)} %copy-done.12, bf16[3328,192]{1,0:T(8,128)(2,1)} %convolution_convert_fusion.rt_ref, ...), custom_call_target="tpu_custom_call" | custom-call | flops 4026531840 | bytes 5242880 | tf_op jit(solution)/shard_map/attend_forward/pallas_call | solution.py:221
  264.8 4.8 fusion.78
  278.1 6.6 %convert_reduce_fusion = (f32[3072]{0:T(1024)S(1)}, bf16[512,3072]{1,0:T(8,128)(2,1)S(1)}) fusion(f32[512,3072]{1,0:T(8,128)S(1)} %fusion.78, f32[3072]{0:T(1024)S(1)} %copy-done.64, bf16[512,768]{1,0:T(8,128)(2,1)S(1)} %get-tuple-element.84, bf16[3072,768]{1,0:T(8,128)(2,1)S(1)} %bitcast.405), kind=kOutput, calls=%fused_computation.9 | convolution fusion | flops 2452091904 | bytes 14966784 | tf_op jit(solution)/shard_map/rc,dc->rd/dot_general | solution.py:399
  284.7 6.5 %fusion.80 = f32[3072,768]{1,0:T(8,128)} fusion(bf16[512,768]{1,0:T(8,128)(2,1)S(1)} %get-tuple-element.84, f32[512,3072]{1,0:T(8,128)S(1)} %fusion.78, f32[3072]{0:T(1024)S(1)} %copy-done.64), kind=kOutput, calls=%fused_computation.291 | convolution fusion | flops 2431647744 | bytes 16527360 | tf_op jit(solution)/shard_map/rd,rc->dc/dot_general | solution.py:403
  291.2 5.5 multiply_reduce_fusion
  298.5 5.5 fusion.76
  329.8 7.2 %collective-permute-done.46 = bf16[96,768]{1,0:T(8,128)(2,1)S(1)} collective-permute-done((bf16[96,768]{1,0:T(8,128)(2,1)S(1)}, bf16[96,768]{1,0:T(8,128)(2,1)S(1)}, u32[]{:S(2)}, u32[]{:S(2)}) %collective-permute-start.46) | collective-permute-done | bytes 147488 | tf_op jit(solution)/shard_map/ppermute | solution.py:328
  354.5 16.3 %attend_backward.5 = (bf16[4,2,256,64]{3,2,1,0:T(8,128)(2,1)S(1)}, bf16[1280,64]{1,0:T(8,128)(2,1)S(1)}, bf16[1280,64]{1,0:T(8,128)(2,1)S(1)}, bf16[3328,64]{1,0:T(8,128)(2,1)S(1)}, f32[8,64]{1,0:T(8,128)S(1)}) custom-call(bf16[2,1024,192]{2,1,0:T(8,128)(2,1)S(1)} %bitcast.384, bf16[1280,192]{1,0:T(8,128)(2,1)S(1)} %copy-done.8, ...), custom_call_target="tpu_custom_call" | custom-call | flops 8053063680 | bytes 5242880 | tf_op jit(solution)/shard_map/attend_backward/pallas_call | solution.py:262
  371.8 19.2 %attend_backward.4 = (bf16[4,2,256,64]{3,2,1,0:T(8,128)(2,1)S(1)}, bf16[1280,64]{1,0:T(8,128)(2,1)S(1)}, bf16[1280,64]{1,0:T(8,128)(2,1)S(1)}, bf16[3328,64]{1,0:T(8,128)(2,1)S(1)}, f32[8,64]{1,0:T(8,128)S(1)}) custom-call(bf16[2,1024,192]{2,1,0:T(8,128)(2,1)S(1)} %bitcast.385, bf16[1280,192]{1,0:T(8,128)(2,1)S(1)} %copy-done.8, ...), custom_call_target="tpu_custom_call" | custom-call | flops 8053063680 | bytes 5242880 | tf_op jit(solution)/shard_map/attend_backward/pallas_call | solution.py:262
  393.0 16.6 %attend_backward.3 = (bf16[4,2,256,64]{3,2,1,0:T(8,128)(2,1)S(1)}, bf16[1280,64]{1,0:T(8,128)(2,1)S(1)}, bf16[1280,64]{1,0:T(8,128)(2,1)S(1)}, bf16[3328,64]{1,0:T(8,128)(2,1)S(1)}, f32[8,64]{1,0:T(8,128)S(1)}) custom-call(bf16[2,1024,192]{2,1,0:T(8,128)(2,1)S(1)} %bitcast.386, bf16[1280,192]{1,0:T(8,128)(2,1)S(1)} %copy-done.9, ...), custom_call_target="tpu_custom_call" | custom-call | flops 8053063680 | bytes 5242880 | tf_op jit(solution)/shard_map/attend_backward/pallas_call | solution.py:262
  455.5 4.7 all-to-all-start.3
  467.6 5.9 collective-permute-done.38
  504.0 8.1 %collective-permute-done.42 = bf16[208,768]{1,0:T(8,128)(2,1)S(1)} collective-permute-done((bf16[208,768]{1,0:T(8,128)(2,1)S(1)}, bf16[208,768]{1,0:T(8,128)(2,1)S(1)}, u32[]{:S(2)}, u32[]{:S(2)}) %collective-permute-start.42) | collective-permute-done | bytes 319520 | tf_op jit(solution)/shard_map/ppermute | solution.py:328
  555.5 5.2 collective-permute-done.62
  573.3 9.8 %collective-permute-done.64 = bf16[96,768]{1,0:T(8,128)(2,1)S(1)} collective-permute-done((bf16[96,768]{1,0:T(8,128)(2,1)S(1)}, bf16[96,768]{1,0:T(8,128)(2,1)S(1)}, u32[]{:S(2)}, u32[]{:S(2)}) %collective-permute-start.64) | collective-permute-done | bytes 147488 | tf_op jit(solution)/shard_map/ppermute | solution.py:328
  591.7 5.8 collective-permute-done.58
  602.1 10.5 %collective-permute-done.59 = bf16[96,3072]{1,0:T(8,128)(2,1)S(1)} collective-permute-done((bf16[96,3072]{1,0:T(8,128)(2,1)S(1)}, bf16[96,3072]{1,0:T(8,128)(2,1)S(1)}, u32[]{:S(2)}, u32[]{:S(2)}) %collective-permute-start.59) | collective-permute-done | bytes 589856 | tf_op jit(solution)/shard_map/ppermute | solution.py:328
  (569 shorter events, 376.0 us)
Async XLA Ops:
  7.5 36.0 %collective-permute-start.16 = (bf16[14,192]{1,0:T(8,128)(2,1)S(1)}, bf16[14,192]{1,0:T(8,128)(2,1)S(1)}, u32[]{:S(2)}, u32[]{:S(2)}) collective-permute-start(bf16[14,192]{1,0:T(8,128)(2,1)S(1)} %concatenate.100), channel_id=1, source_target_pairs={{0,2},{1,3},{2,0},{3,1},{4,6},{5,7},{6,4},{7,5},{8,10},{9,11},{10,... | collective-permute-start | bytes 16136 | tf_op jit(solution)/shard_map/ppermute | solution.py:328
  10.5 35.6 %collective-permute-start.17 = (bf16[14,192]{1,0:T(8,128)(2,1)S(1)}, bf16[14,192]{1,0:T(8,128)(2,1)S(1)}, u32[]{:S(2)}, u32[]{:S(2)}) collective-permute-start(bf16[14,192]{1,0:T(8,128)(2,1)S(1)} %concatenate.100), channel_id=1, source_target_pairs={{0,1},{1,0},{2,3},{3,2},{4,5},{5,4},{6,7},{7,6},{8,9},{9,8},{10,11... | collective-permute-start | bytes 16136 | tf_op jit(solution)/shard_map/ppermute | solution.py:328
  10.5 237.9 %collective-permute-start.25 = (bf16[768,768]{1,0:T(8,128)(2,1)}, bf16[768,768]{1,0:T(8,128)(2,1)}, u32[]{:S(2)}, u32[]{:S(2)}) collective-permute-start(bf16[768,768]{1,0:T(8,128)(2,1)} %param.50), channel_id=1, source_target_pairs={{0,2},{1,3},{2,0},{3,1},{4,6},{5,7},{6,4},{7,5},{8,10},{9,11},{10,... | collective-permute-start | bytes 3538952 | tf_op jit(solution)/shard_map/ppermute | solution.py:328
  10.7 245.5 %collective-permute-start.26 = (bf16[768,768]{1,0:T(8,128)(2,1)}, bf16[768,768]{1,0:T(8,128)(2,1)}, u32[]{:S(2)}, u32[]{:S(2)}) collective-permute-start(bf16[768,768]{1,0:T(8,128)(2,1)} %param.50), channel_id=1, source_target_pairs={{0,1},{1,0},{2,3},{3,2},{4,5},{5,4},{6,7},{7,6},{8,9},{9,8},{10,11... | collective-permute-start | bytes 3538952 | tf_op jit(solution)/shard_map/ppermute | solution.py:328
  11.0 237.4 %collective-permute-start.22 = (bf16[192,3072]{1,0:T(8,128)(2,1)}, bf16[192,3072]{1,0:T(8,128)(2,1)}, u32[]{:S(2)}, u32[]{:S(2)}) collective-permute-start(bf16[192,3072]{1,0:T(8,128)(2,1)} %param.48), channel_id=1, source_target_pairs={{0,2},{1,3},{2,0},{3,1},{4,6},{5,7},{6,4},{7,5},{8,10},{9,11},{10,... | collective-permute-start | bytes 3538952 | tf_op jit(solution)/shard_map/ppermute | solution.py:328
  57.7 15.1 %collective-permute-start.6 = (bf16[4,192,192]{2,1,0:T(8,128)(2,1)}, bf16[4,192,192]{2,1,0:T(8,128)(2,1)S(1)}, u32[]{:S(2)}, u32[]{:S(2)}) collective-permute-start(bf16[4,192,192]{2,1,0:T(8,128)(2,1)} %pad_maximum_fusion.9), channel_id=1, source_target_pairs={{0,2},{1,3},{2,0},{3,1},{4,6},{5,7},{6,4},{7,5},{8,10},{9,11},{10,... | collective-permute-start | bytes 884744 | tf_op jit(solution)/shard_map/ppermute | solution.py:328
  124.6 22.4 %collective-permute-start.21 = (bf16[192,768]{1,0:T(8,128)(2,1)S(1)}, bf16[192,768]{1,0:T(8,128)(2,1)S(1)}, u32[]{:S(2)}, u32[]{:S(2)}) collective-permute-start(bf16[192,768]{1,0:T(8,128)(2,1)S(1)} %collective-permute-done.19), channel_id=1, source_target_pairs={{0,1},{1,0},{2,3},{3,2},{4,5},{5,4},{6,7},{7,6},{8,9},{9,8},{10,11... | collective-permute-start | bytes 884744 | tf_op jit(solution)/shard_map/ppermute | solution.py:328
  125.4 22.3 %collective-permute-start.33 = (bf16[192,768]{1,0:T(8,128)(2,1)S(1)}, bf16[192,768]{1,0:T(8,128)(2,1)S(1)}, u32[]{:S(2)}, u32[]{:S(2)}) collective-permute-start(bf16[192,768]{1,0:T(8,128)(2,1)S(1)} %collective-permute-done.31), channel_id=1, source_target_pairs={{0,1},{1,0},{2,3},{3,2},{4,5},{5,4},{6,7},{7,6},{8,9},{9,8},{10,11... | collective-permute-start | bytes 884744 | tf_op jit(solution)/shard_map/ppermute | solution.py:328
  160.0 93.7 %collective-permute-start.23 = (bf16[192,3072]{1,0:T(8,128)(2,1)}, bf16[192,3072]{1,0:T(8,128)(2,1)}, u32[]{:S(2)}, u32[]{:S(2)}) collective-permute-start(bf16[192,3072]{1,0:T(8,128)(2,1)} %param.48), channel_id=1, source_target_pairs={{0,1},{1,0},{2,3},{3,2},{4,5},{5,4},{6,7},{7,6},{8,9},{9,8},{10,11... | collective-permute-start | bytes 3538952 | tf_op jit(solution)/shard_map/ppermute | solution.py:328
  248.4 21.2 %collective-permute-start.27 = (bf16[768,768]{1,0:T(8,128)(2,1)}, bf16[768,768]{1,0:T(8,128)(2,1)}, u32[]{:S(2)}, u32[]{:S(2)}) collective-permute-start(bf16[768,768]{1,0:T(8,128)(2,1)} %collective-permute-done.25), channel_id=1, source_target_pairs={{0,1},{1,0},{2,3},{3,2},{4,5},{5,4},{6,7},{7,6},{8,9},{9,8},{10,11... | collective-permute-start | bytes 3538952 | tf_op jit(solution)/shard_map/ppermute | solution.py:328
  306.0 16.4 %collective-permute-start.45 = (bf16[1,192,768]{2,1,0:T(8,128)(2,1)}, bf16[1,192,768]{2,1,0:T(8,128)(2,1)}, u32[]{:S(2)}, u32[]{:S(2)}) collective-permute-start(bf16[1,192,768]{2,1,0:T(8,128)(2,1)} %dynamic-slice_convert_fusion.10), channel_id=1, source_target_pairs={{0,2},{1,3},{2,0},{3,1},{4,6},{5,7},{6,4},{7,5},{8,10},{9,11},{10,... | collective-permute-start | bytes 884744 | tf_op jit(solution)/shard_map/ppermute | solution.py:328
  318.0 32.1 %all-to-all-start.1 = ((bf16[4,2,256,192]{2,3,1,0:T(8,128)(2,1)}), bf16[4,2,256,192]{2,3,1,0:T(8,128)(2,1)}, u32[]{:S(2)}, u32[]{:S(2)}) async-start(bf16[4,2,256,192]{2,3,1,0:T(8,128)(2,1)} %copy.126), calls=%async_computation.1 | async-start | bytes 1572864 | tf_op jit(solution)/shard_map/all_to_all | solution.py:541
  340.5 143.6 %collective-permute-start.52 = (bf16[2,192,3072]{2,1,0:T(8,128)(2,1)}, bf16[2,192,3072]{2,1,0:T(8,128)(2,1)}, u32[]{:S(2)}, u32[]{:S(2)}) collective-permute-start(bf16[2,192,3072]{2,1,0:T(8,128)(2,1)} %fusion.7), channel_id=1, source_target_pairs={{0,1},{1,0},{2,3},{3,2},{4,5},{5,4},{6,7},{7,6},{8,9},{9,8},{10,11... | collective-permute-start | bytes 7077896 | tf_op jit(solution)/shard_map/ppermute | solution.py:328
  348.8 144.8 %collective-permute-start.60 = (bf16[2,768,768]{2,1,0:T(8,128)(2,1)}, bf16[2,768,768]{2,1,0:T(8,128)(2,1)}, u32[]{:S(2)}, u32[]{:S(2)}) collective-permute-start(bf16[2,768,768]{2,1,0:T(8,128)(2,1)} %fusion.8), channel_id=1, source_target_pairs={{0,1},{1,0},{2,3},{3,2},{4,5},{5,4},{6,7},{7,6},{8,9},{9,8},{10,11... | collective-permute-start | bytes 7077896 | tf_op jit(solution)/shard_map/ppermute | solution.py:328
  348.9 93.0 %collective-permute-start.49 = (bf16[24,768]{1,0:T(8,128)(2,1)S(1)}, bf16[24,768]{1,0:T(8,128)(2,1)S(1)}, u32[]{:S(2)}, u32[]{:S(2)}) collective-permute-start(bf16[24,768]{1,0:T(8,128)(2,1)S(1)} %get-tuple-element.80), channel_id=1, source_target_pairs={{0,16},{16,0},{1,17},{17,1},{2,18},{18,2},{3,19},{19,3},{4,20},{20... | collective-permute-start | bytes 110600 | tf_op jit(solution)/shard_map/ppermute | solution.py:328
  419.0 36.5 %all-to-all-start.2 = ((bf16[8,2,32,192]{3,2,1,0:T(8,128)(2,1)}), bf16[8,2,32,192]{3,2,1,0:T(8,128)(2,1)}, u32[]{:S(2)}, u32[]{:S(2)}) async-start(bf16[8,2,32,192]{3,2,1,0:T(8,128)(2,1)} %maximum_bitcast_fusion.2), calls=%async_computation.2 | async-start | bytes 524288 | tf_op jit(solution)/shard_map/all_to_all | solution.py:580
  441.6 19.6 %collective-permute-start.37 = (bf16[2,208,768]{2,1,0:T(8,128)(2,1)S(1)}, bf16[2,208,768]{2,1,0:T(8,128)(2,1)}, u32[]{:S(2)}, u32[]{:S(2)}) collective-permute-start(bf16[2,208,768]{2,1,0:T(8,128)(2,1)S(1)} %fusion.48), channel_id=1, source_target_pairs={{0,1},{1,0},{2,3},{3,2},{4,5},{5,4},{6,7},{7,6},{8,9},{9,8},{10,11... | collective-permute-start | bytes 1916936 | tf_op jit(solution)/shard_map/ppermute | solution.py:328
  455.5 82.2 %all-to-all-start.3 = ((bf16[4,4,256,192]{2,3,1,0:T(8,128)(2,1)}), bf16[4,4,256,192]{2,3,1,0:T(8,128)(2,1)}, u32[]{:S(2)}, u32[]{:S(2)}) async-start(bf16[4,4,256,192]{2,3,1,0:T(8,128)(2,1)} %copy.143), calls=%async_computation.3 | async-start | bytes 3145728 | tf_op jit(solution)/shard_map/all_to_all | solution.py:574
  489.2 44.6 %collective-permute-start.53 = (bf16[1,192,3072]{2,1,0:T(8,128)(2,1)}, bf16[1,192,3072]{2,1,0:T(8,128)(2,1)}, u32[]{:S(2)}, u32[]{:S(2)}) collective-permute-start(bf16[1,192,3072]{2,1,0:T(8,128)(2,1)} %dynamic-slice_convert_fusion.3), channel_id=1, source_target_pairs={{0,2},{1,3},{2,0},{3,1},{4,6},{5,7},{6,4},{7,5},{8,10},{9,11},{10,... | collective-permute-start | bytes 3538952 | tf_op jit(solution)/shard_map/ppermute | solution.py:328
  500.8 40.4 %collective-permute-start.61 = (bf16[1,768,768]{2,1,0:T(8,128)(2,1)}, bf16[1,768,768]{2,1,0:T(8,128)(2,1)}, u32[]{:S(2)}, u32[]{:S(2)}) collective-permute-start(bf16[1,768,768]{2,1,0:T(8,128)(2,1)} %dynamic-slice_convert_fusion.2), channel_id=1, source_target_pairs={{0,2},{1,3},{2,0},{3,1},{4,6},{5,7},{6,4},{7,5},{8,10},{9,11},{10,... | collective-permute-start | bytes 3538952 | tf_op jit(solution)/shard_map/ppermute | solution.py:328
  536.1 16.3 %collective-permute-start.54 = (bf16[96,3072]{1,0:T(8,128)(2,1)S(1)}, bf16[96,3072]{1,0:T(8,128)(2,1)S(1)}, u32[]{:S(2)}, u32[]{:S(2)}) collective-permute-start(bf16[96,3072]{1,0:T(8,128)(2,1)S(1)} %fusion.50), channel_id=1, source_target_pairs={{0,4},{4,0},{1,5},{5,1},{2,6},{6,2},{3,7},{7,3},{8,12},{12,8},{9,1... | collective-permute-start | bytes 1769480 | tf_op jit(solution)/shard_map/ppermute | solution.py:328
  543.6 17.1 %collective-permute-start.62 = (bf16[384,768]{1,0:T(8,128)(2,1)S(1)}, bf16[384,768]{1,0:T(8,128)(2,1)S(1)}, u32[]{:S(2)}, u32[]{:S(2)}) collective-permute-start(bf16[384,768]{1,0:T(8,128)(2,1)S(1)} %fusion.51), channel_id=1, source_target_pairs={{0,4},{4,0},{1,5},{5,1},{2,6},{6,2},{3,7},{7,3},{8,12},{12,8},{9,1... | collective-permute-start | bytes 1769480 | tf_op jit(solution)/shard_map/ppermute | solution.py:328
  597.5 15.2 %collective-permute-start.59 = (bf16[96,3072]{1,0:T(8,128)(2,1)S(1)}, bf16[96,3072]{1,0:T(8,128)(2,1)S(1)}, u32[]{:S(2)}, u32[]{:S(2)}) collective-permute-start(bf16[96,3072]{1,0:T(8,128)(2,1)S(1)} %bitcast.414), channel_id=1, source_target_pairs={{0,4},{4,0},{1,5},{5,1},{2,6},{6,2},{3,7},{7,3},{8,12},{12,8},{9,1... | collective-permute-start | bytes 1769480 | tf_op jit(solution)/shard_map/ppermute | solution.py:328
  600.6 18.3 %collective-permute-start.67 = (bf16[384,768]{1,0:T(8,128)(2,1)S(1)}, bf16[384,768]{1,0:T(8,128)(2,1)S(1)}, u32[]{:S(2)}, u32[]{:S(2)}) collective-permute-start(bf16[384,768]{1,0:T(8,128)(2,1)S(1)} %bitcast.416), channel_id=1, source_target_pairs={{0,4},{4,0},{1,5},{5,1},{2,6},{6,2},{3,7},{7,3},{8,12},{12,8},{9,1... | collective-permute-start | bytes 1769480 | tf_op jit(solution)/shard_map/ppermute | solution.py:328
  (125 other events, 1372.8 us)

commit v2 on v1

v2 whole, which is shorter than its diff:
```python
from functools import partial

import jax
import jax.numpy as jnp
import numpy as np
from jax import lax
from jax.experimental import pallas as pl
from jax.experimental.pallas import tpu as pltpu
from jax.sharding import Mesh, PartitionSpec as P

D = 768
HEADS = 12
HEAD_DIM = 64
LEN = 1024
SEGMENTS = 4
TQ = 128

negative = -1e30
epsilon = 1e-06
scale_factor = HEAD_DIM ** (-0.5)
NT = (((1,), (1,)), ((), ()))
NN = (((1,), (0,)), ((), ()))
TN = (((0,), (0,)), ((), ()))

COL_HIGH = HEAD_DIM
COL_LOW = HEAD_DIM + SEGMENTS
COL_ONE = HEAD_DIM + 2 * SEGMENTS
COL_ONE_LOW = COL_ONE + 1
COL_MASK = COL_ONE + 2


def mm(a, b, dims=NN):
    return lax.dot_general(a, b, dims, preferred_element_type=jnp.float32)


def reverse_rows(x):
    groups = x.shape[0] // 8
    index = 7 - lax.broadcasted_iota(jnp.int32, (8, x.shape[1]), 0)
    return jnp.concatenate(
        [
            jnp.take_along_axis(x[8 * (groups - 1 - g) : 8 * (groups - g)], index, axis=0)
            for g in range(groups)
        ],
        axis=0,
    )


def prepare_keys(head, k_ref, v_ref, rt_ref, kinfo_ref, kaug, vaug, rt):
    cols = slice(head * HEAD_DIM, (head + 1) * HEAD_DIM)
    rows = k_ref.shape[0]
    lane = lax.broadcasted_iota(jnp.int32, (rows, HEAD_DIM), 1)
    segment = kinfo_ref[:, 0:1]
    hidden = kinfo_ref[:, 1:2]
    one_hot = ((lane == segment) | (lane - SEGMENTS == segment)) & (lane < 2 * SEGMENTS)
    ones = (lane == COL_ONE - HEAD_DIM) | (lane == COL_ONE_LOW - HEAD_DIM)
    extra = jnp.where(one_hot | ones, 1.0, 0.0)
    extra = jnp.where((lane == COL_MASK - HEAD_DIM) & (hidden > 0), negative, extra)
    kaug[:, :HEAD_DIM] = k_ref[:, cols]
    kaug[:, HEAD_DIM:] = extra.astype(jnp.bfloat16)
    vaug[:, :HEAD_DIM] = v_ref[:, cols]
    vaug[:, HEAD_DIM:] = jnp.where(lane < 2, 1.0, 0.0).astype(jnp.bfloat16)
    rt[...] = rt_ref[:, cols]


def query_terms(head, s, q_ref, bias_ref):
    cols = slice(head * HEAD_DIM, (head + 1) * HEAD_DIM)
    q = q_ref[s, :, cols].astype(jnp.float32)
    content = (q + bias_ref[0:1, cols]).astype(jnp.bfloat16).astype(jnp.float32)
    position = (q + bias_ref[1:2, cols]).astype(jnp.bfloat16).astype(jnp.float32)
    segment = q + bias_ref[2:3, cols]
    return content, position, segment


def forward_kernel(
    q_ref, k_ref, v_ref, rt_ref, bias_ref, qinfo_ref, kinfo_ref, rank_ref,
    p_ref, a_ref, mix_ref, kaug_ref, vaug_ref, table_ref, qaug,
):
    step = pl.program_id(0)
    keys = k_ref.shape[0]
    prompt = keys - LEN
    heads = p_ref.shape[0]

    @pl.when(step == 0)
    def _():
        for head in range(heads):
            prepare_keys(
                head, k_ref, v_ref, rt_ref, kinfo_ref,
                kaug_ref.at[head], vaug_ref.at[head], table_ref.at[head],
            )

    start = pl.multiple_of(LEN - TQ - step * TQ, TQ)
    lane = lax.broadcasted_iota(jnp.int32, (TQ, HEAD_DIM), 1)
    segment_id = qinfo_ref[:, 0:1]
    rank = qinfo_ref[:, 1:2]
    wide = lax.broadcasted_iota(jnp.int32, (TQ, 2 * HEAD_DIM), 1)
    for head, s in [(head, s) for head in range(heads) for s in range(2)]:
        cols = slice(head * HEAD_DIM, (head + 1) * HEAD_DIM)
        table_p = table_ref[head, pl.ds(start, TQ + prompt), :]
        table_c = table_ref[head, pl.ds(pl.multiple_of(LEN + prompt + start, TQ), TQ + LEN), :]
        content, position, with_segment = query_terms(head, s, q_ref, bias_ref)
        same = jnp.sum(with_segment * bias_ref[3:4, cols], axis=1, keepdims=True) * scale_factor
        other = jnp.sum(with_segment * bias_ref[4:5, cols], axis=1, keepdims=True) * scale_factor
        differ = same - other
        differ_high = differ.astype(jnp.bfloat16).astype(jnp.float32)
        other_high = other.astype(jnp.bfloat16).astype(jnp.float32)
        extra = jnp.where(lane == segment_id, differ_high, 0.0)
        extra = jnp.where(lane - SEGMENTS == segment_id, differ - differ_high, extra)
        extra = jnp.where(lane == COL_ONE - HEAD_DIM, other_high, extra)
        extra = jnp.where(lane == COL_ONE_LOW - HEAD_DIM, other - other_high, extra)
        extra = jnp.where(lane == COL_MASK - HEAD_DIM, 1.0, extra)
        qaug[:, :HEAD_DIM] = (content * scale_factor).astype(jnp.bfloat16)
        qaug[:, HEAD_DIM:] = extra.astype(jnp.bfloat16)
        scores = mm(qaug[...], kaug_ref[head], NT)
        position = (position * scale_factor).astype(jnp.bfloat16)
        band_p = pltpu.roll(
            mm(position, table_p, NT), prompt + 1, axis=1, stride=1, stride_axis=0
        )
        band_c = pltpu.roll(mm(position, table_c, NT), LEN + 1, axis=1, stride=1, stride_axis=0)
        scores_p = scores[:, :prompt] + band_p[:, :prompt]
        scores_c = scores[:, prompt:] + band_c[:, :LEN]
        scores_c = jnp.where(rank_ref[0:1, :] <= rank - s, scores_c, negative)
        largest = jnp.maximum(
            jnp.max(scores_p, axis=1, keepdims=True), jnp.max(scores_c, axis=1, keepdims=True)
        )
        weights_p = jnp.exp(scores_p - largest)
        weights_c = jnp.exp(scores_c - largest)
        mixed = mm(weights_p.astype(jnp.bfloat16), vaug_ref[head, :prompt, :])
        mixed += mm(weights_c.astype(jnp.bfloat16), vaug_ref[head, prompt:, :])
        inverse = 1.0 / mixed[:, HEAD_DIM : HEAD_DIM + 1]
        mixed = mixed * inverse
        a_ref[head, s] = jnp.where(wide < HEAD_DIM, mixed, inverse)
        mix_ref[0, head, :, s * HEAD_DIM : (s + 1) * HEAD_DIM] = mixed[:, :HEAD_DIM].astype(
            jnp.bfloat16
        )
        rows = slice(s * TQ, (s + 1) * TQ)
        p_ref[head, 0, rows, :prompt] = reverse_rows(weights_p).astype(jnp.bfloat16)
        p_ref[head, 0, rows, prompt:] = reverse_rows(weights_c).astype(jnp.bfloat16)


def backward_kernel(
    head, q_ref, bias_ref, qinfo_ref, kaug_ref, vaug_ref, table_ref, p_ref, a_ref, ag_ref,
    dq_ref, dkv_ref, dt_ref, sum_ref,
    agaug, cw, cr, g_all, band_p, band_c, dk_acc, dv_acc, dt_acc,
):
    step = pl.program_id(0)
    keys = kaug_ref.shape[1]
    prompt = keys - LEN
    cols = slice(head * HEAD_DIM, (head + 1) * HEAD_DIM)

    @pl.when(step == 0)
    def _():
        dk_acc[...] = jnp.zeros_like(dk_acc)
        dv_acc[...] = jnp.zeros_like(dv_acc)
        dt_acc[...] = jnp.zeros_like(dt_acc)
        sum_ref[...] = jnp.zeros_like(sum_ref)

    start = pl.multiple_of(LEN - TQ - step * TQ, TQ)
    start_c = pl.multiple_of(LEN + prompt + start, TQ)
    lane = lax.broadcasted_iota(jnp.int32, (TQ, HEAD_DIM), 1)
    segment_id = qinfo_ref[:, 2:3]
    segments = []
    for s in range(2):
        rows = slice(s * TQ, (s + 1) * TQ)
        content, position, with_segment = query_terms(head, s, q_ref, bias_ref)
        cw[rows, :] = reverse_rows(content).astype(jnp.bfloat16)
        cr[rows, :] = reverse_rows(position).astype(jnp.bfloat16)
        segments.append(reverse_rows(with_segment))
        grad = ag_ref[0, 0, :, s * HEAD_DIM : (s + 1) * HEAD_DIM].astype(jnp.float32)
        inverse = a_ref[0, s, :, HEAD_DIM : HEAD_DIM + 1] * scale_factor
        delta = jnp.sum(grad * a_ref[0, s, :, :HEAD_DIM], axis=1, keepdims=True) * inverse
        delta_high = delta.astype(jnp.bfloat16).astype(jnp.float32)
        extra = jnp.where(lane == 0, -delta_high, jnp.where(lane == 1, delta_high - delta, 0.0))
        agaug[rows, :HEAD_DIM] = reverse_rows(grad * inverse).astype(jnp.bfloat16)
        agaug[rows, HEAD_DIM:] = reverse_rows(extra).astype(jnp.bfloat16)
    share_grad = mm(agaug[...], vaug_ref[0], NT)
    g_all[...] = (p_ref[0, 0].astype(jnp.float32) * share_grad).astype(jnp.bfloat16)
    for s in range(2):
        rows = slice(s * TQ, (s + 1) * TQ)
        blank = jnp.zeros((TQ, TQ), jnp.bfloat16)
        wide_p = jnp.concatenate([g_all[rows, :prompt], blank], axis=1)
        wide_c = jnp.concatenate([g_all[rows, prompt:], blank], axis=1)
        band_p[rows, :] = pltpu.roll(wide_p, 0, axis=1, stride=1, stride_axis=0)
        band_c[rows, :] = pltpu.roll(wide_c, 0, axis=1, stride=1, stride_axis=0)
    dv_acc[...] += mm(agaug[:, :HEAD_DIM], p_ref[0, 0], TN)
    dk_acc[...] += mm(cw[...], g_all[...], TN)
    dt_acc[:, pl.ds(start, TQ + prompt)] += mm(cr[...], band_p[...], TN)
    dt_acc[:, pl.ds(start_c, TQ + LEN)] += mm(cr[...], band_c[...], TN)
    query_content = mm(g_all[...], kaug_ref[0])
    query_position = mm(band_p[...], table_ref[0, pl.ds(start, TQ + prompt), :])
    query_position += mm(band_c[...], table_ref[0, pl.ds(start_c, TQ + LEN), :])
    same_vector = bias_ref[3:4, cols]
    other_vector = bias_ref[4:5, cols]

    def add_row(row, value):
        sum_ref[row : row + 1, :] += jnp.sum(value, axis=0, keepdims=True)

    for s in range(2):
        rows = slice(s * TQ, (s + 1) * TQ)
        from_content = query_content[rows, :HEAD_DIM]
        extra = query_content[rows, HEAD_DIM:]
        hit = (lane == segment_id) & (lane < SEGMENTS)
        same = jnp.sum(jnp.where(hit, extra, 0.0), axis=1, keepdims=True)
        other = extra[:, COL_ONE - HEAD_DIM : COL_ONE - HEAD_DIM + 1] - same
        from_segment = same * same_vector + other * other_vector
        from_position = query_position[rows, :]
        total = reverse_rows(from_content + from_position + from_segment)
        dq_ref[0, :, s * HEAD_DIM : (s + 1) * HEAD_DIM] = total.astype(jnp.bfloat16)
        add_row(0, from_content)
        add_row(1, from_position)
        add_row(2, from_segment)
        add_row(3, same * segments[s])
        add_row(4, other * segments[s])

    @pl.when(step == pl.num_programs(0) - 1)
    def _():
        dkv_ref[:, :HEAD_DIM] = dk_acc[...].T.astype(jnp.bfloat16)
        dkv_ref[:, HEAD_DIM:] = (dv_acc[...].T * HEAD_DIM**0.5).astype(jnp.bfloat16)
        dt_ref[...] = dt_acc[...].T.astype(jnp.bfloat16)


def whole(shape):
    return pl.BlockSpec(shape, lambda i: (0,) * len(shape))


def attend_forward(q, k, v, rt, bias, qinfo, kinfo, ranks, tokens):
    keys, width = k.shape
    table = rt.shape[0]
    steps = LEN // TQ
    heads = width // HEAD_DIM
    per = tokens // TQ
    return pl.pallas_call(
        forward_kernel,
        grid=(steps,),
        in_specs=[
            pl.BlockSpec((2, TQ, width), lambda i: (0, i, 0)),
            whole((keys, width)),
            whole((keys, width)),
            whole((table, width)),
            whole(bias.shape),
            pl.BlockSpec((TQ, qinfo.shape[1]), lambda i: (i, 0)),
            whole(kinfo.shape),
            whole(ranks.shape),
        ],
        out_specs=[
            pl.BlockSpec((heads, 1, 2 * TQ, keys), lambda i: (0, i, 0, 0)),
            pl.BlockSpec((heads, 2, TQ, 2 * HEAD_DIM), lambda i: (0, 0, i, 0)),
            pl.BlockSpec((1, heads, TQ, 2 * HEAD_DIM), lambda i: (i // per, 0, i % per, 0)),
            whole((heads, keys, 2 * HEAD_DIM)),
            whole((heads, keys, 2 * HEAD_DIM)),
            whole((heads, table, HEAD_DIM)),
        ],
        out_shape=[
            jax.ShapeDtypeStruct((heads, steps, 2 * TQ, keys), jnp.bfloat16),
            jax.ShapeDtypeStruct((heads, 2, LEN, 2 * HEAD_DIM), jnp.float32),
            jax.ShapeDtypeStruct((LEN // tokens, heads, tokens, 2 * HEAD_DIM), jnp.bfloat16),
            jax.ShapeDtypeStruct((heads, keys, 2 * HEAD_DIM), jnp.bfloat16),
            jax.ShapeDtypeStruct((heads, keys, 2 * HEAD_DIM), jnp.bfloat16),
            jax.ShapeDtypeStruct((heads, table, HEAD_DIM), jnp.bfloat16),
        ],
        scratch_shapes=[pltpu.VMEM((TQ, 2 * HEAD_DIM), jnp.bfloat16)],
        compiler_params=pltpu.CompilerParams(vmem_limit_bytes=56 * 2**20),
        cost_estimate=pl.CostEstimate(
            flops=heads * 6 * 2 * LEN * keys * 256,
            bytes_accessed=heads * 2 * LEN * keys * 2,
            transcendentals=heads * 2 * LEN * keys,
        ),
        name="attend_forward",
    )(q, k, v, rt, bias, qinfo, kinfo, ranks)


def attend_backward(head, q, bias, qinfo, kaug, vaug, rows_of, p, a, ag):
    _, keys, wide = kaug.shape
    table = rows_of.shape[1]
    width = q.shape[2]
    steps = LEN // TQ
    prompt = keys - LEN
    members, heads, tokens, _ = ag.shape
    per = tokens // TQ

    def one(shape):
        return pl.BlockSpec((1,) + shape, lambda i: (head,) + (0,) * len(shape))

    return pl.pallas_call(
        partial(backward_kernel, head),
        grid=(steps,),
        in_specs=[
            pl.BlockSpec((2, TQ, width), lambda i: (0, i, 0)),
            whole(bias.shape),
            pl.BlockSpec((TQ, qinfo.shape[1]), lambda i: (i, 0)),
            one((keys, wide)),
            one((keys, wide)),
            one((table, HEAD_DIM)),
            pl.BlockSpec((1, 1, 2 * TQ, keys), lambda i: (head, i, 0, 0)),
            pl.BlockSpec((1, 2, TQ, wide), lambda i: (head, 0, i, 0)),
            pl.BlockSpec((1, 1, TQ, wide), lambda i: (i // per, head, i % per, 0)),
        ],
        out_specs=[
            pl.BlockSpec((1, TQ, wide), lambda i: (i // per, i % per, 0)),
            whole((keys, wide)),
            whole((table, HEAD_DIM)),
            whole((8, HEAD_DIM)),
        ],
        out_shape=[
            jax.ShapeDtypeStruct((members, tokens, wide), jnp.bfloat16),
            jax.ShapeDtypeStruct((keys, wide), jnp.bfloat16),
            jax.ShapeDtypeStruct((table, HEAD_DIM), jnp.bfloat16),
            jax.ShapeDtypeStruct((8, HEAD_DIM), jnp.float32),
        ],
        scratch_shapes=[
            pltpu.VMEM((2 * TQ, wide), jnp.bfloat16),
            pltpu.VMEM((2 * TQ, HEAD_DIM), jnp.bfloat16),
            pltpu.VMEM((2 * TQ, HEAD_DIM), jnp.bfloat16),
            pltpu.VMEM((2 * TQ, keys), jnp.bfloat16),
            pltpu.VMEM((2 * TQ, TQ + prompt), jnp.bfloat16),
            pltpu.VMEM((2 * TQ, TQ + LEN), jnp.bfloat16),
            pltpu.VMEM((HEAD_DIM, keys), jnp.float32),
            pltpu.VMEM((HEAD_DIM, keys), jnp.float32),
            pltpu.VMEM((HEAD_DIM, table), jnp.float32),
        ],
        compiler_params=pltpu.CompilerParams(vmem_limit_bytes=56 * 2**20),
        cost_estimate=pl.CostEstimate(
            flops=12 * 2 * LEN * keys * 256, bytes_accessed=2 * LEN * keys * 2, transcendentals=0
        ),
        name="attend_backward",
    )(q, bias, qinfo, kaug, vaug, rows_of, p, a, ag)


def table_kernel(shards, place_ref, *refs):
    pieces, small, rest = refs[:shards], refs[shards : 2 * shards], refs[2 * shards :]
    (
        coarse_ref, fine_ref, weight_ref, rt_ref, position_ref, vector_ref, inner_ref, bias_ref,
        held, sem,
    ) = rest
    _, rows, width = pieces[0].shape
    shard, member = place_ref[0], place_ref[1]
    copies = []
    for m in range(shards):
        spot = pl.multiple_of((shard ^ m) * rows, rows)
        copies.append(
            pltpu.make_async_copy(pieces[m], weight_ref.at[:, pl.ds(spot, rows), :], sem.at[m])
        )
    for copy in copies:
        copy.start()
    for m in range(shards):
        held[m] = small[m][...].astype(jnp.float32)
    bias_ref[...] = held[shard ^ member][0:8, :]
    for w in range(shards):
        block = held[shard ^ w]
        at = slice(w * width, (w + 1) * width)
        vector_ref[0:5, at] = block[5:10, :]
        for j in range(4):
            spot = (w * 4 + j) * width
            inner_ref[0:1, spot : spot + width] = block[10 + j : 11 + j, :]
    half = fine_ref.shape[2]
    fine_sin, fine_cos = fine_ref[0], fine_ref[1]
    step = 64

    def build(i, carry):
        at = pl.ds(pl.multiple_of(i * step, step), step)
        coarse_sin, coarse_cos = coarse_ref[0, pl.ds(i, 1), :], coarse_ref[1, pl.ds(i, 1), :]
        position_ref[at, :half] = (coarse_sin * fine_cos - coarse_cos * fine_sin).astype(
            jnp.bfloat16
        )
        position_ref[at, half:] = (coarse_cos * fine_cos + coarse_sin * fine_sin).astype(
            jnp.bfloat16
        )
        return carry

    lax.fori_loop(0, position_ref.shape[0] // step, build, 0)
    for copy in copies:
        copy.wait()
    block = 256
    relative = weight_ref[3]

    def body(i, carry):
        at = pl.ds(pl.multiple_of(i * block, block), block)
        rt_ref[at, :] = mm(position_ref[at, :], relative).astype(jnp.bfloat16)
        return carry

    lax.fori_loop(0, position_ref.shape[0] // block, body, 0)


def project_table(place, pieces, small, coarse, fine):
    _, rows, width = pieces[0].shape
    shards = len(pieces)
    table = coarse.shape[1] * fine.shape[1]
    vmem = pl.BlockSpec(memory_space=pltpu.VMEM)
    return pl.pallas_call(
        partial(table_kernel, shards),
        in_specs=[pl.BlockSpec(memory_space=pltpu.SMEM)]
        + [pl.BlockSpec(memory_space=pl.ANY)] * shards
        + [vmem] * (shards + 2),
        out_specs=[vmem] * 6,
        out_shape=[
            jax.ShapeDtypeStruct((4, shards * rows, width), jnp.bfloat16),
            jax.ShapeDtypeStruct((table, width), jnp.bfloat16),
            jax.ShapeDtypeStruct((table, D), jnp.bfloat16),
            jax.ShapeDtypeStruct((8, D), jnp.float32),
            jax.ShapeDtypeStruct((1, 4 * D), jnp.float32),
            jax.ShapeDtypeStruct((8, width), jnp.float32),
        ],
        scratch_shapes=[
            pltpu.VMEM((shards,) + small[0].shape, jnp.float32),
            pltpu.SemaphoreType.DMA((shards,)),
        ],
        compiler_params=pltpu.CompilerParams(vmem_limit_bytes=48 * 2**20),
        name="project_table",
    )(place, *pieces, *small, coarse, fine)


def states_kernel(members, place_ref, *refs):
    pieces, (prompt_ref, weight_ref, q_ref, k_ref, v_ref, states_ref, sem) = (
        (refs[:members], refs[members : 2 * members]),
        refs[2 * members :],
    )
    tokens = pieces[0][0].shape[0]
    prompt = prompt_ref.shape[0]
    copies = [pltpu.make_async_copy(prompt_ref, states_ref.at[pl.ds(0, prompt)], sem.at[0])]
    for s in range(2):
        for m, piece in enumerate(pieces[s]):
            spot = prompt + s * LEN + pl.multiple_of((place_ref[1] ^ m) * tokens, tokens)
            copies.append(
                pltpu.make_async_copy(
                    piece, states_ref.at[pl.ds(spot, tokens)], sem.at[1 + 2 * m + s]
                )
            )
    for copy in copies:
        copy.start()
    for copy in copies:
        copy.wait()
    step = 256
    query, key, value = weight_ref[0], weight_ref[1], weight_ref[2]
    for i in range(2 * LEN // step):
        rows = states_ref[prompt + i * step : prompt + (i + 1) * step, :]
        stream, at = divmod(i * step, LEN)
        q_ref[stream, at : at + step, :] = mm(rows, query).astype(jnp.bfloat16)
    for i in range((prompt + LEN) // step):
        rows = states_ref[i * step : (i + 1) * step, :]
        k_ref[i * step : (i + 1) * step, :] = mm(rows, key).astype(jnp.bfloat16)
        v_ref[i * step : (i + 1) * step, :] = mm(rows, value).astype(jnp.bfloat16)


def project_states(place, content, query, prompt_all, weights):
    members = len(content)
    width = weights.shape[2]
    prompt = prompt_all.shape[0]
    return pl.pallas_call(
        partial(states_kernel, members),
        in_specs=[pl.BlockSpec(memory_space=pltpu.SMEM)]
        + [pl.BlockSpec(memory_space=pl.ANY)] * (2 * members + 1)
        + [pl.BlockSpec(memory_space=pltpu.VMEM)],
        out_specs=[pl.BlockSpec(memory_space=pltpu.VMEM)] * 4,
        out_shape=[
            jax.ShapeDtypeStruct((2, LEN, width), jnp.bfloat16),
            jax.ShapeDtypeStruct((prompt + LEN, width), jnp.bfloat16),
            jax.ShapeDtypeStruct((prompt + LEN, width), jnp.bfloat16),
            jax.ShapeDtypeStruct((prompt + 2 * LEN, D), jnp.bfloat16),
        ],
        scratch_shapes=[pltpu.SemaphoreType.DMA((1 + 2 * members,))],
        compiler_params=pltpu.CompilerParams(vmem_limit_bytes=48 * 2**20),
        name="project_states",
    )(place, *content, *query, prompt_all, weights)


def normalise(x):
    center = x - jnp.mean(x, axis=1, keepdims=True)
    inverse = lax.rsqrt(jnp.mean(center * center, axis=1, keepdims=True) + epsilon)
    return center * inverse, inverse


def norm_backward(grad, unit, inverse, gain):
    scaled = grad * gain
    mean = jnp.mean(scaled, axis=1, keepdims=True)
    along = jnp.mean(scaled * unit, axis=1, keepdims=True)
    return (scaled - mean - unit * along) * inverse


def layer_kernel(
    a_ref, content_ref, query_ref, up_content_ref, up_query_ref, vector_ref, inner_ref,
    output_hbm, hidden_hbm, return_hbm,
    out_content_ref, out_query_ref, flat_ref, inner_in_ref, active_ref, returned_ref, zgrad_ref,
    residual_ref, branch_ref, ag_ref, sum_ref, inner_sum_ref,
    output_w, hidden_w, return_w, flat, inner_in, slope, acc, unit, sem,
):
    members, heads, tokens, _ = a_ref.shape
    shards, _, rows_w = flat_ref.shape
    copies = [
        pltpu.make_async_copy(output_hbm, output_w, sem.at[0]),
        pltpu.make_async_copy(hidden_hbm, hidden_w, sem.at[1]),
        pltpu.make_async_copy(return_hbm, return_w, sem.at[2]),
    ]
    for copy in copies:
        copy.start()
    for g in range(members):
        for h in range(heads):
            spot = (g * heads + h) * HEAD_DIM
            for s in range(2):
                flat[s * tokens : (s + 1) * tokens, spot : spot + HEAD_DIM] = a_ref[
                    g, h, :, s * HEAD_DIM : (s + 1) * HEAD_DIM
                ]
    for w in range(shards):
        flat_ref[w] = flat[:, w * rows_w : (w + 1) * rows_w]
    gain, shift, outer, final_gain, final_shift = (vector_ref[i : i + 1, :] for i in range(5))
    copies[0].wait()
    inverses = []
    for s, source in enumerate((content_ref, query_ref)):
        at = slice(s * tokens, (s + 1) * tokens)
        mixed = mm(flat[at, :], output_w[...])
        normal, inverse = normalise(source[...].astype(jnp.float32) + mixed)
        inverses.append(inverse)
        unit[at, :] = normal
        middle = normal * gain + shift
        low = middle.astype(jnp.bfloat16)
        inner_in[at, :] = low
        for w in range(shards):
            inner_in_ref[w, at, :] = low[:, w * rows_w : (w + 1) * rows_w]
        acc[at, :] = middle + outer
    copies[1].wait()
    copies[2].wait()
    step = 512
    chunks = hidden_w.shape[1] // step
    root = 0.7978845608028654

    def forward(i, carry):
        at = pl.ds(pl.multiple_of(i * step, step), step)
        for s in range(2):
            part = slice(s * tokens, (s + 1) * tokens)
            z = mm(inner_in[part, :], hidden_w[:, at]) + inner_ref[:, at]
            square = z * z
            curve = jnp.tanh(root * (z + 0.044715 * (z * square)))
            half = 0.5 + 0.5 * curve
            active = (z * half).astype(jnp.bfloat16)
            slope[part, at] = half + (0.5 * root) * z * (1.0 - curve * curve) * (
                1.0 + (3 * 0.044715) * square
            )
            active_ref[part, at] = active
            acc[part, :] += mm(active, return_w[at, :])
        return carry

    lax.fori_loop(0, chunks, forward, 0)
    sums = []
    for s, (upstream, result) in enumerate(
        ((up_content_ref, out_content_ref), (up_query_ref, out_query_ref))
    ):
        at = slice(s * tokens, (s + 1) * tokens)
        normal, inverse = normalise(acc[at, :])
        result[...] = (normal * final_gain + final_shift).astype(jnp.bfloat16)
        grad = upstream[...].astype(jnp.float32)
        back = norm_backward(grad, normal, inverse, final_gain)
        low = back.astype(jnp.bfloat16)
        returned_ref[at, :] = low
        acc[at, :] = back
        sums.append(
            [
                jnp.sum(low.astype(jnp.float32), axis=0, keepdims=True),
                jnp.sum(grad * normal, axis=0, keepdims=True),
                jnp.sum(grad, axis=0, keepdims=True),
            ]
        )
    for i in range(3):
        sum_ref[2 + i : 3 + i, :] = sums[0][i] + sums[1][i]

    def backward(i, carry):
        at = pl.ds(pl.multiple_of(i * step, step), step)
        total = jnp.zeros((1, step), jnp.float32)
        for s in range(2):
            part = slice(s * tokens, (s + 1) * tokens)
            grad = mm(returned_ref[part, :], return_w[at, :], NT) * slope[part, at]
            low = grad.astype(jnp.bfloat16)
            zgrad_ref[part, at] = low
            total += jnp.sum(low.astype(jnp.float32), axis=0, keepdims=True)
            acc[part, :] += mm(low, hidden_w[:, at], NT)
        inner_sum_ref[:, at] = total
        return carry

    lax.fori_loop(0, chunks, backward, 0)
    sums = []
    for s in range(2):
        at = slice(s * tokens, (s + 1) * tokens)
        grad = acc[at, :]
        normal = unit[at, :]
        back = norm_backward(grad, normal, inverses[s], gain)
        residual_ref[at, :] = back
        low = back.astype(jnp.bfloat16)
        branch_ref[at, :] = low
        sums.append(
            [
                jnp.sum(grad * normal, axis=0, keepdims=True),
                jnp.sum(grad, axis=0, keepdims=True),
            ]
        )
        mixed = mm(low, output_w[...], NT).astype(jnp.bfloat16)
        for g in range(members):
            for h in range(heads):
                spot = (g * heads + h) * HEAD_DIM
                ag_ref[g, h, :, s * HEAD_DIM : (s + 1) * HEAD_DIM] = mixed[
                    :, spot : spot + HEAD_DIM
                ]
    for i in range(2):
        sum_ref[i : i + 1, :] = sums[0][i] + sums[1][i]


def layer(shards, a, content, query, up_content, up_query, vectors, inner, output_w, hidden_w, return_w):
    tokens = content.shape[0]
    rows = 2 * tokens
    hidden = hidden_w.shape[1]
    vmem = pl.BlockSpec(memory_space=pltpu.VMEM)
    low = partial(jax.ShapeDtypeStruct, dtype=jnp.bfloat16)
    wide = partial(jax.ShapeDtypeStruct, dtype=jnp.float32)
    return pl.pallas_call(
        layer_kernel,
        in_specs=[vmem] * 7 + [pl.BlockSpec(memory_space=pl.ANY)] * 3,
        out_specs=[vmem] * 12,
        out_shape=[
            low((tokens, D)),
            low((tokens, D)),
            low((shards, rows, D // shards)),
            low((shards, rows, D // shards)),
            low((rows, hidden)),
            low((rows, D)),
            low((rows, hidden)),
            wide((rows, D)),
            low((rows, D)),
            low(a.shape),
            wide((5, D)),
            wide((1, hidden)),
        ],
        scratch_shapes=[
            pltpu.VMEM((D, D), jnp.bfloat16),
            pltpu.VMEM((D, hidden), jnp.bfloat16),
            pltpu.VMEM((hidden, D), jnp.bfloat16),
            pltpu.VMEM((rows, D), jnp.bfloat16),
            pltpu.VMEM((rows, D), jnp.bfloat16),
            pltpu.VMEM((rows, hidden), jnp.float32),
            pltpu.VMEM((rows, D), jnp.float32),
            pltpu.VMEM((rows, D), jnp.float32),
            pltpu.SemaphoreType.DMA((3,)),
        ],
        compiler_params=pltpu.CompilerParams(vmem_limit_bytes=60 * 2**20),
        cost_estimate=pl.CostEstimate(
            flops=8 * rows * D * hidden, bytes_accessed=24 * 2**20, transcendentals=rows * hidden
        ),
        name="layer",
    )(a, content, query, up_content, up_query, vectors, inner, output_w, hidden_w, return_w)


def token_grads_kernel(
    core_ref, active_ref, inner_ref, mixed_ref, returned_ref, zgrad_ref, branch_ref, out_ref
):
    rows_w = inner_ref.shape[2]
    low = partial(jnp.asarray, dtype=jnp.bfloat16)
    count = zgrad_ref.shape[1] // D
    block = mm(inner_ref[0], zgrad_ref[...], TN)
    spots = [0, 1, 2, 6]
    for j in range(count):
        at = spots[j] * rows_w
        out_ref[0, at : at + rows_w, :] = low(block[:, j * D : (j + 1) * D])
    block = mm(active_ref[...], returned_ref[...], TN)
    spots = [3, 4, 5, 7]
    for j in range(count):
        at = spots[j] * rows_w
        out_ref[0, at : at + rows_w, :] = low(block[j * rows_w : (j + 1) * rows_w])
    out_ref[0, 8 * rows_w :, :] = low(mm(mixed_ref[0], branch_ref[...], TN))


def token_grads(core, active, inner, mixed, returned, zgrad, branch):
    shards, rows, rows_w = inner.shape
    hidden = active.shape[1]
    per = hidden // shards
    block = (1, 9 * rows_w, D)
    return pl.pallas_call(
        token_grads_kernel,
        grid_spec=pltpu.PrefetchScalarGridSpec(
            num_scalar_prefetch=1,
            grid=(shards // 2,),
            in_specs=[
                pl.BlockSpec((rows, per), lambda i, c: (0, 2 * i + c[0])),
                pl.BlockSpec((1, rows, rows_w), lambda i, c: (2 * i + c[0], 0, 0)),
                pl.BlockSpec((1, rows, rows_w), lambda i, c: (2 * i + c[0], 0, 0)),
                pl.BlockSpec((rows, D), lambda i, c: (0, 0)),
                pl.BlockSpec((rows, hidden), lambda i, c: (0, 0)),
                pl.BlockSpec((rows, D), lambda i, c: (0, 0)),
            ],
            out_specs=pl.BlockSpec(block, lambda i, c: (i, 0, 0)),
        ),
        out_shape=jax.ShapeDtypeStruct((shards // 2,) + block[1:], jnp.bfloat16),
        compiler_params=pltpu.CompilerParams(vmem_limit_bytes=56 * 2**20),
        cost_estimate=pl.CostEstimate(
            flops=2 * rows * D * hidden, bytes_accessed=16 * 2**20, transcendentals=0
        ),
        name="token_grads",
    )(core.reshape(1), active, inner, mixed, returned, zgrad, branch)


def unpack_tokens_kernel(members, head_count, place_ref, *refs):
    pieces, (hidden_ref, return_ref, output_ref, held) = refs[:members], refs[members:]
    rows_w = hidden_ref.shape[0]
    chains, per, _ = held.shape[1:]
    for m in range(members):
        held[m] = pieces[m][...]
    member = place_ref[1]
    targets = {0: 0, 1: 1, 2: 2, 6: 3}
    for g in range(members):
        head, half = g % head_count, g // head_count
        for c in range(chains):
            if c == 2:
                spot = (half * head_count + head) * per
            else:
                spot = (head * (members // head_count) + half) * per
            row = c * members * per + spot
            done = 0
            while done < per:
                block, at = divmod(row + done, rows_w)
                count = min(per - done, rows_w - at)
                value = held[member ^ g, c, done : done + count, :].astype(jnp.float32)
                if block == 8:
                    output_ref[at : at + count, :] = value
                elif block in targets:
                    j = targets[block]
                    hidden_ref[at : at + count, j * D : (j + 1) * D] = value
                else:
                    j = {3: 0, 4: 1, 5: 2, 7: 3}[block]
                    return_ref[j * rows_w + at : j * rows_w + at + count, :] = value
                done += count


def unpack_tokens(place, rows_w, head_count, pieces):
    members = len(pieces)
    vmem = pl.BlockSpec(memory_space=pltpu.VMEM)
    return pl.pallas_call(
        partial(unpack_tokens_kernel, members, head_count),
        in_specs=[pl.BlockSpec(memory_space=pltpu.SMEM)] + [vmem] * members,
        out_specs=[vmem] * 3,
        out_shape=[
            jax.ShapeDtypeStruct((rows_w, 4 * D), jnp.float32),
            jax.ShapeDtypeStruct((4 * rows_w, D), jnp.float32),
            jax.ShapeDtypeStruct((rows_w, D), jnp.float32),
        ],
        scratch_shapes=[pltpu.VMEM((members,) + pieces[0].shape, jnp.bfloat16)],
        compiler_params=pltpu.CompilerParams(vmem_limit_bytes=48 * 2**20),
        name="unpack_tokens",
    )(place, *pieces)


def head_grads_kernel(shards, heads, place_ref, states_ref, position_ref, *rest):
    dq, dkv, dt = (rest[i * heads : (i + 1) * heads] for i in range(3))
    small, out_ref = rest[3 * heads : -1], rest[-1]
    keys = dkv[0].shape[0]
    prompt = keys - LEN
    rows_w = D // shards
    wide = 2 * HEAD_DIM
    side = partial(jnp.concatenate, axis=1)
    dq = side([ref[...].reshape(LEN, wide) for ref in dq])
    key_value = mm(side([ref[...] for ref in dkv]), states_ref[:keys, :], TN)
    content = mm(dq, states_ref[prompt:keys, :], TN)
    query = mm(dq, states_ref[keys:, :], TN)
    table = mm(side([ref[...] for ref in dt]), position_ref[...], TN)
    parts = []
    for h in range(heads):
        at = h * wide
        parts += [
            content[at : at + HEAD_DIM] + query[at + HEAD_DIM : at + wide],
            key_value[at : at + wide],
            table[h * HEAD_DIM : (h + 1) * HEAD_DIM],
        ]
    turned = jnp.concatenate(parts, axis=0).T.astype(jnp.bfloat16)
    for w in range(shards):
        out_ref[w, :rows_w, :] = turned[w * rows_w : (w + 1) * rows_w, :]
    if small:
        token_ref, inner_ref, sums = small[0], small[1], small[2:]
        member = place_ref[1]
        out_ref[:, rows_w:, :] = jnp.zeros_like(out_ref[:, rows_w:, :])
        own_sums = side([ref[0:5, :] for ref in sums])
        for w in range(shards):
            own = jnp.where(member == w, own_sums, 0.0)
            parts = [token_ref[0:5, w * rows_w : (w + 1) * rows_w], own]
            parts += [
                inner_ref[0:1, (4 * w + j) * rows_w : (4 * w + j + 1) * rows_w] for j in range(4)
            ]
            parts.append(jnp.zeros((2, rows_w), jnp.float32))
            out_ref[w, rows_w : rows_w + 16, :rows_w] = jnp.concatenate(parts, axis=0).astype(
                jnp.bfloat16
            )


def head_grads(place, shards, states, positions, dq, dkv, dt, small=()):
    vmem = pl.BlockSpec(memory_space=pltpu.VMEM)
    heads = len(dq)
    operands = (states, positions) + tuple(dq) + tuple(dkv) + tuple(dt) + tuple(small)
    rows = D // shards + (16 if small else 0)
    return pl.pallas_call(
        partial(head_grads_kernel, shards, heads),
        in_specs=[pl.BlockSpec(memory_space=pltpu.SMEM)] + [vmem] * len(operands),
        out_specs=vmem,
        out_shape=jax.ShapeDtypeStruct((shards, rows, 4 * HEAD_DIM * heads), jnp.bfloat16),
        compiler_params=pltpu.CompilerParams(vmem_limit_bytes=56 * 2**20),
        cost_estimate=pl.CostEstimate(
            flops=2 * 6656 * D * 256, bytes_accessed=12 * 2**20, transcendentals=0
        ),
        name="head_grads",
    )(place, *operands)


def unpack_kernel(members, groups, place_ref, *refs):
    pieces = [refs[i * members : (i + 1) * members] for i in range(groups)]
    outs = refs[groups * members : groups * members + 4]
    small_ref = refs[groups * members + 4]
    held = refs[groups * members + 5 : groups * members + 5 + groups]
    rows_w = outs[0].shape[0]
    for i in range(groups):
        for m in range(members):
            held[i][m] = pieces[i][m][...]
    member = place_ref[1]
    for g in range(members):
        head = 0
        for i in range(groups):
            block = held[i][member ^ g].astype(jnp.float32)
            for j in range(block.shape[1] // (4 * HEAD_DIM)):
                spot = (g * groups_heads(held) + head) * HEAD_DIM
                for kind in range(4):
                    at = (4 * j + kind) * HEAD_DIM
                    outs[kind][:, spot : spot + HEAD_DIM] = block[:rows_w, at : at + HEAD_DIM]
                head += 1
    last = held[-1]
    total = last[0, rows_w : rows_w + 16, :].astype(jnp.float32)
    for m in range(1, members):
        total += last[m, rows_w : rows_w + 16, :].astype(jnp.float32)
    small_ref[...] = total


def groups_heads(held):
    return sum(ref.shape[2] // (4 * HEAD_DIM) for ref in held)


def unpack(place, rows_w, *pieces):
    members = len(pieces[0])
    vmem = pl.BlockSpec(memory_space=pltpu.VMEM)
    flat = [x for group in pieces for x in group]
    return pl.pallas_call(
        partial(unpack_kernel, members, len(pieces)),
        in_specs=[pl.BlockSpec(memory_space=pltpu.SMEM)] + [vmem] * len(flat),
        out_specs=[vmem] * 5,
        out_shape=[jax.ShapeDtypeStruct((rows_w, D), jnp.float32)] * 4
        + [jax.ShapeDtypeStruct((16, 4 * HEAD_DIM), jnp.float32)],
        scratch_shapes=[pltpu.VMEM((members,) + group[0].shape, jnp.bfloat16) for group in pieces],
        compiler_params=pltpu.CompilerParams(vmem_limit_bytes=48 * 2**20),
        name="unpack",
    )(place, *flat)


def finish_kernel(
    token_ref, prompt_ref, residual_ref, weight_hbm, content_ref, query_ref, out_prompt_ref,
    weight, parts, prompts, sem,
):
    copy = pltpu.make_async_copy(weight_hbm, weight, sem)
    copy.start()
    members, heads, _, tokens, wide = token_ref.shape
    chapters = prompt_ref.shape[0]
    for g in range(members):
        for h in range(heads):
            spot = (g * heads + h) * HEAD_DIM
            for kind in range(4):
                at = (kind % 2) * HEAD_DIM
                parts[kind, :, spot : spot + HEAD_DIM] = token_ref[
                    g, h, kind // 2, :, at : at + HEAD_DIM
                ]
            total = prompt_ref[0, g, h].astype(jnp.float32)
            for c in range(1, chapters):
                total += prompt_ref[c, g, h].astype(jnp.float32)
            total = total.astype(jnp.bfloat16)
            for kind in range(2):
                prompts[kind, :, spot : spot + HEAD_DIM] = total[
                    :, kind * HEAD_DIM : (kind + 1) * HEAD_DIM
                ]
    copy.wait()
    query, key, value = (weight[:, i * D : (i + 1) * D] for i in range(3))
    content = residual_ref[:tokens, :] + mm(parts[0], query, NT)
    content += mm(parts[2], key, NT)
    content += mm(parts[3], value, NT)
    content_ref[...] = content.astype(jnp.bfloat16)
    query_ref[...] = (residual_ref[tokens:, :] + mm(parts[1], query, NT)).astype(jnp.bfloat16)
    out_prompt_ref[...] = (mm(prompts[0], key, NT) + mm(prompts[1], value, NT)).astype(
        jnp.bfloat16
    )


def finish(token_back, prompt_back, residual, weights):
    tokens = token_back.shape[3]
    prompt = prompt_back.shape[3]
    vmem = pl.BlockSpec(memory_space=pltpu.VMEM)
    return pl.pallas_call(
        finish_kernel,
        in_specs=[vmem] * 3 + [pl.BlockSpec(memory_space=pl.ANY)],
        out_specs=[vmem] * 3,
        out_shape=[
            jax.ShapeDtypeStruct((tokens, D), jnp.bfloat16),
            jax.ShapeDtypeStruct((tokens, D), jnp.bfloat16),
            jax.ShapeDtypeStruct((prompt, D), jnp.bfloat16),
        ],
        scratch_shapes=[
            pltpu.VMEM(weights.shape, jnp.bfloat16),
            pltpu.VMEM((4, tokens, D), jnp.bfloat16),
            pltpu.VMEM((2, prompt, D), jnp.bfloat16),
            pltpu.SemaphoreType.DMA,
        ],
        compiler_params=pltpu.CompilerParams(vmem_limit_bytes=48 * 2**20),
        cost_estimate=pl.CostEstimate(
            flops=8 * tokens * D * D, bytes_accessed=8 * 2**20, transcendentals=0
        ),
        name="finish",
    )(token_back, prompt_back, residual, weights)


def axes_size(axes):
    size = 1
    for name in axes:
        size *= lax.axis_size(name)
    return size


def flat_index(axes):
    index = 0
    for name in axes:
        index = index * lax.axis_size(name) + lax.axis_index(name)
    return index


def swap(x, axes, mask):
    return lax.ppermute(x, axes, [(i, i ^ mask) for i in range(axes_size(axes))])


def bits_of(axes):
    return range(axes_size(axes).bit_length() - 1)


def pieces_of(x, axes):
    pieces = {0: x}
    for bit in reversed(bits_of(axes)):
        for mask in list(pieces):
            pieces[mask | 1 << bit] = swap(pieces[mask], axes, 1 << bit)
    return [pieces[m] for m in range(axes_size(axes))]


def in_order(pieces, index):
    count = len(pieces)
    result = jnp.zeros((count,) + pieces[0].shape, pieces[0].dtype)
    for m, piece in enumerate(pieces):
        result = lax.dynamic_update_slice(result, piece[None], (index ^ m,) + (0,) * piece.ndim)
    return result


def pick(x, index, axis=0):
    return lax.dynamic_index_in_dim(x, index, axis, keepdims=False)


def add_low(x, y):
    return (x.astype(jnp.float32) + y.astype(jnp.float32)).astype(jnp.bfloat16)


def half_sum(x, axes, bit, axis):
    own = flat_index(axes) >> bit & 1
    return add_low(pick(x, own, axis), swap(pick(x, 1 - own, axis), axes, 1 << bit))


def split_axis(x, axis):
    return x.reshape(x.shape[:axis] + (2, x.shape[axis] // 2) + x.shape[axis + 1 :])


def stages_of(names):
    return [((name,), bit) for name in names for bit in bits_of((name,))]


def full_sum(x, stages):
    for axes, bit in stages:
        x = add_low(x, swap(x, axes, 1 << bit))
    return x


def group_pieces(x, axes):
    return [x] + [swap(x, axes, m) for m in range(1, axes_size(axes))]


def back_through(grad_rows, weight):
    return jnp.einsum("rc,dc->rd", grad_rows, weight, preferred_element_type=jnp.float32)


def outer_sum(rows_in, grad_rows):
    return jnp.einsum("rd,rc->dc", rows_in, grad_rows, preferred_element_type=jnp.float32)


def sinusoid_rows(first, rows):
    frequency = jnp.asarray(
        np.power(10000.0, -2.0 * np.arange(D // 2) / D).astype(np.float32)
    )
    fine = jnp.arange(64, dtype=jnp.float32)[:, None] * frequency
    coarse = (first - 64 * jnp.arange(rows // 64, dtype=jnp.int32)).astype(jnp.float32)
    coarse = coarse[:, None] * frequency
    fs, fc = jnp.sin(fine)[None], jnp.cos(fine)[None]
    cs, cc = jnp.sin(coarse)[:, None], jnp.cos(coarse)[:, None]
    both = jnp.concatenate([cs * fc - cc * fs, cc * fc + cs * fs], axis=-1)
    return both.reshape(rows, D).astype(jnp.bfloat16)


GROUP = ("half", "head")
JOB = ("cont", "half", "head")
SHARD = ("wshard",)


def per_device(
    prompt_states, content_states, query_states, visible_length, start_offsets,
    prompt_segments, token_segments, order_ranks,
    query_weights, key_weights, value_weights, output_weights, relative_weights,
    content_bias, position_bias, segment_bias, segment_vectors,
    attention_gain, attention_shift, hidden_weights, hidden_bias, return_weights, return_bias,
    final_gain, final_shift, content_upstream, query_upstream,
):
    members = axes_size(GROUP)
    member = flat_index(GROUP)
    shards = lax.axis_size("wshard")
    shard = lax.axis_index("wshard")
    chapters = lax.axis_size("cont")
    chapter = lax.axis_index("cont")
    width = D // members
    local_heads = HEADS // members
    content_rows = content_states[0]
    query_rows = query_states[0]
    tokens = content_rows.shape[0]
    prompt_part = prompt_states.shape[1]
    prompt_total = prompt_segments.shape[1]
    keys = prompt_total + LEN
    rows_w = query_weights.shape[0]

    def columns(x):
        return lax.dynamic_slice_in_dim(x, member * width, width, x.ndim - 1)

    content = {0: content_rows}
    query = {0: query_rows}
    content[1], query[2] = swap(content_rows, GROUP, 1), swap(query_rows, GROUP, 2)
    first_weights = jnp.stack(
        [columns(w) for w in (query_weights, key_weights, value_weights, relative_weights)], axis=0
    )
    small = jnp.concatenate(
        [
            jnp.stack([content_bias, position_bias, segment_bias]),
            segment_vectors,
            jnp.stack([attention_gain, attention_shift, return_bias, final_gain, final_shift]),
            hidden_bias.reshape(-1, rows_w),
            jnp.zeros((2, rows_w), jnp.bfloat16),
        ],
        axis=0,
    )
    first_pieces = pieces_of(first_weights, SHARD)
    small_pieces = pieces_of(small, SHARD)
    query[1], content[2] = swap(query_rows, GROUP, 1), swap(content_rows, GROUP, 2)
    content[3], query[3] = swap(content[1], GROUP, 2), swap(query[2], GROUP, 1)
    prompt_all = lax.all_to_all(
        jnp.broadcast_to(prompt_states, (chapters * members,) + prompt_states.shape[1:]),
        JOB,
        0,
        0,
        tiled=True,
    ).reshape(prompt_total, D)
    output_full = lax.all_gather(output_weights, "wshard", axis=0, tiled=True)
    hidden_full = lax.all_gather(hidden_weights, "wshard", axis=0, tiled=True)
    return_full = lax.all_gather(return_weights, "wshard", axis=0, tiled=True)
    attention_weights = jnp.concatenate([query_weights, key_weights, value_weights], axis=1)
    attention_full = lax.all_gather(attention_weights, "wshard", axis=0, tiled=True)

    seen = pick(visible_length[0], chapter)
    base = seen + pick(start_offsets[0], chapter)
    segments = lax.dynamic_slice_in_dim(token_segments[0], chapter * LEN, LEN)
    ranks = lax.dynamic_slice_in_dim(order_ranks[0], chapter * LEN, LEN)
    reversed_segments = jnp.flip(segments.reshape(-1, TQ), 1).reshape(-1)
    qinfo = jnp.stack([segments, ranks, reversed_segments, segments], axis=1)
    key_segments = jnp.concatenate([prompt_segments[0], segments])
    hidden_keys = (jnp.arange(keys, dtype=jnp.int32) < prompt_total) & (
        jnp.arange(keys, dtype=jnp.int32) >= seen
    )
    kinfo = jnp.stack([key_segments, hidden_keys.astype(jnp.int32)], axis=1)
    place = jnp.stack([shard, member])

    frequency = jnp.asarray(np.power(10000.0, -2.0 * np.arange(D // 2) / D).astype(np.float32))
    starts = jnp.concatenate(
        [
            base + LEN - 1 - 64 * jnp.arange((LEN + prompt_total) // 64, dtype=jnp.int32),
            LEN - 1 - 64 * jnp.arange(2 * LEN // 64, dtype=jnp.int32),
        ]
    )
    coarse = starts.astype(jnp.float32)[:, None] * frequency
    coarse = jnp.stack([jnp.sin(coarse), jnp.cos(coarse)])
    fine = jnp.arange(64, dtype=jnp.float32)[:, None] * frequency
    fine = jnp.stack([jnp.sin(fine), jnp.cos(fine)])

    first_full, rt, positions, vectors, inner_full, head_bias = project_table(
        place, first_pieces, small_pieces, coarse, fine
    )
    q, k, v, states = project_states(
        place,
        [content[m] for m in range(members)],
        [query[m] for m in range(members)],
        prompt_all,
        first_full,
    )
    p, a, mixture, kaug, vaug, table_rows = attend_forward(
        q, k, v, rt, head_bias, qinfo, kinfo, ranks[None], tokens
    )
    mixture = lax.all_to_all(mixture, GROUP, 0, 0, tiled=True)

    (
        out_content, out_query, mixed_flat, inner_in, active, returned_grad, inner_grad,
        residual_grad, branch_grad, grad_out, token_sums, inner_bias_grad,
    ) = layer(
        shards, mixture, content_rows, query_rows, content_upstream[0], query_upstream[0],
        vectors, inner_full, output_full, hidden_full, return_full,
    )
    grad_out, attention_full = lax.optimization_barrier((grad_out, attention_full))
    grad_out = lax.all_to_all(grad_out, GROUP, 0, 0, tiled=True)

    core = shard & 1
    grads = (active, inner_in, mixed_flat, returned_grad, inner_grad, branch_grad)
    sent = swap(token_grads(1 - core, *grads), SHARD, 1)
    total = add_low(token_grads(core, *grads), sent)
    third = total.shape[1] // 3
    chains = [total[:, i * third : (i + 1) * third] for i in range(3)]
    rest = [(SHARD, bit) for bit in bits_of(SHARD) if bit > 0]
    head_stage, half_stage, cont_stage = (stages_of((name,)) for name in ("head", "half", "cont"))
    orders = (
        (rest, head_stage, half_stage),
        (head_stage, half_stage, rest),
        (half_stage, rest, head_stage),
    )

    def chain_stage(x, stages):
        for axes, bit in stages:
            if axes == SHARD:
                x = half_sum(x.reshape((-1, 2) + x.shape[1:]), axes, bit, 1)
            else:
                x = half_sum(split_axis(x, 1), axes, bit, 1)
        return x

    small_grads = (token_sums, inner_bias_grad)
    backward, head_parts = [], []
    for h in range(local_heads):
        grad_out, chains = lax.optimization_barrier((grad_out, chains))
        backward.append(
            attend_backward(h, q, head_bias, qinfo, kaug, vaug, table_rows, p, a, grad_out)
        )
        chains = [chain_stage(x, orders[i][h]) for i, x in enumerate(chains)]
        if h == local_heads - 2:
            dq, dkv, dt, _ = zip(*backward)
            x = head_grads(place, shards, states, positions, dq, dkv, dt)
            x = half_sum(x.reshape((-1, 2) + x.shape[1:]), SHARD, 0, 1)
            head_parts.append(x)
            grad_out, head_parts = lax.optimization_barrier((grad_out, head_parts))
    dq, dkv, dt, sums = zip(*backward)
    x = head_grads(
        place, shards, states, positions, dq[-1:], dkv[-1:], dt[-1:], small_grads + sums
    )
    head_parts.append(half_sum(x.reshape((-1, 2) + x.shape[1:]), SHARD, 0, 1))
    token_back = jnp.stack(
        [
            jnp.stack([dq[h], dkv[h][prompt_total:].reshape(dq[h].shape)], axis=1)
            for h in range(local_heads)
        ],
        axis=1,
    )
    token_back = lax.all_to_all(token_back, GROUP, 0, 0, tiled=True)
    prompt_back = jnp.stack(
        [x[:prompt_total].reshape(chapters * members, prompt_part, -1) for x in dkv], axis=1
    )
    prompt_back = lax.all_to_all(prompt_back, JOB, 0, 0, tiled=True)
    prompt_back = prompt_back.reshape((chapters, members) + prompt_back.shape[1:])

    chains = jnp.concatenate(chains)
    chains = full_sum(chains, cont_stage)
    hidden_total, return_total, output_total = unpack_tokens(
        place, rows_w, lax.axis_size("head"), group_pieces(chains, GROUP)
    )
    head_pieces = []
    for x in head_parts:
        for axes, bit in rest:
            x = half_sum(x.reshape((-1, 2) + x.shape[1:]), axes, bit, 1)
        head_pieces.append(group_pieces(full_sum(x[0], cont_stage), GROUP))
    query_grad, key_grad, value_grad, relative_grad, small_total = unpack(
        place, rows_w, *head_pieces
    )
    vector_total = small_total[:10, :rows_w]
    inner_total = small_total[10:14, :rows_w].reshape(-1)
    content_grad, queries_grad, prompt_grad = finish(
        token_back, prompt_back, residual_grad, attention_full
    )
    return (
        out_content[None],
        out_query[None],
        prompt_grad[None],
        content_grad[None],
        queries_grad[None],
        query_grad,
        key_grad,
        value_grad,
        output_total,
        relative_grad,
        vector_total[5],
        vector_total[6],
        vector_total[7],
        vector_total[8:10],
        vector_total[0],
        vector_total[1],
        hidden_total,
        inner_total,
        return_total,
        vector_total[2],
        vector_total[3],
        vector_total[4],
    )


def solution(mesh):
    rows = P("wshard", JOB, None)
    job = P("wshard", None)
    matrix = P("wshard", None)
    vector = P("wshard")
    pair = P(None, "wshard")
    in_specs = (
        (rows,) * 3 + (job,) * 5 + (matrix,) * 5 + (vector,) * 3 + (pair,)
        + (vector, vector, matrix, vector, matrix, vector, vector, vector, rows, rows)
    )
    out_specs = (
        (rows,) * 5 + (matrix,) * 5 + (vector,) * 3 + (pair,)
        + (vector, vector, matrix, vector, matrix, vector, vector, vector)
    )

    def run(*arguments):
        seq_count, head_count, shard_count = mesh.devices.shape
        tokens = arguments[1].shape[1] // (seq_count * head_count)
        halves = LEN // (tokens * head_count)
        split = Mesh(
            mesh.devices.reshape(seq_count // halves, halves, head_count, shard_count),
            ("cont", "half", "head", "wshard"),
        )
        return jax.shard_map(
            per_device, mesh=split, in_specs=in_specs, out_specs=out_specs, check_vma=False
        )(*arguments)

    return run
```

time: 632 us -> 429 us (0.68)
  local copies, waits for them, and re-layouts: 146 us -> 32.9 us
  matrix products: 90.3 us -> 0 us
  Pallas kernels: 112 us -> 194 us
  waiting for transfers between devices: 137 us -> 104 us
  starting transfers between devices: 87.1 us -> 56.8 us
  other arithmetic: 44.2 us -> 19.6 us
  between operations: 4.06 us -> 16.3 us
    dot_general x23 -> x0, matrix products: 90.3 us -> none  [the longest x7 36.8 us: project(): return jnp.dot(rows_in, weight, preferred_element_type=jnp.float32)]
    pallas_call x3 -> x11, Pallas kernels: 60.3 us -> 137 us  [the longest x1 54.8 us: attend_forward(): pl.pallas_call(forward_kernel, grid=(steps,), in_specs=[pl.BlockSpec((2,...]
    ppermute x68 -> x38, waiting for transfers between devices: 136 us -> 87.6 us  [swap(): lax.ppermute(x, axes, [(i, i ^ mask) for i in range(axes_size(axes))])]
    dynamic_update_slice x68 -> x0, local copies, waits for them, and re-layouts: 41.5 us -> none  [the longest x51 40.9 us: gather(): lax.dynamic_update_slice(result, piece[None], (index ^ mask,) + (0,) * x....]
    ppermute x68 -> x38, starting transfers between devices: 70.1 us -> 37.1 us  [swap(): lax.ppermute(x, axes, [(i, i ^ mask) for i in range(axes_size(axes))])]
    add x14 -> x0, other arithmetic: 17.6 us -> none  [the longest x8 16.3 us: scatter_sum(): kept.astype(jnp.float32)]
    convert_element_type x20 -> x0, local copies, waits for them, and re-layouts: 17.5 us -> none  [the longest x7 13.6 us: scatter_sum(): sent.astype(jnp.bfloat16)]
    concatenate x13 -> x0, local copies, waits for them, and re-layouts: 11.1 us -> none  [the longest x1 4.06 us: per_device(): jnp.concatenate([dq, dk[prompt_total:].reshape(members, 1, tokens, width)...]
  transfers between devices with their start and end apart: 72 -> 47, of which waited for: 35 -> 15; matrix products, arithmetic and copies ran while one was open for 36% -> 10% of each run, Pallas kernels for 18% -> 38%
where the time goes in v2:
time: 429 us; the launch traced here: 423 us
  Pallas kernels  194 us (45%)
  waiting for transfers between devices  104 us (24%)
  starting transfers between devices  56.8 us (13%)
  local copies, waits for them, and re-layouts  32.9 us (8%)
  other arithmetic  19.6 us (5%)
  between operations  16.3 us (4%)
    ppermute x38, waiting for transfers between devices, swap(): lax.ppermute(x, axes, [(i, i ^ mask) for i in range(axes_size(axes))])  87.6 us
    pallas_call x3, Pallas kernels, attend_backward(): pl.pallas_call(partial(backward_kernel, head), grid=(steps,), in_specs=[p...  56.6 us
    pallas_call x1, Pallas kernels, attend_forward(): pl.pallas_call(forward_kernel, grid=(steps,), in_specs=[pl.BlockSpec((2,...  54.8 us
    ppermute x38, starting transfers between devices, swap(): lax.ppermute(x, axes, [(i, i ^ mask) for i in range(axes_size(axes))])  37.1 us
    pallas_call x1, Pallas kernels, layer(): pl.pallas_call(layer_kernel, in_specs=[vmem] * 7 + [pl.BlockSpec(memory_s...  27.5 us
    pallas_call x2, Pallas kernels, token_grads(): pl.pallas_call(token_grads_kernel, grid_spec=pltpu.PrefetchScalarGridSpec...  15.1 us
    pallas_call x2, Pallas kernels, head_grads(): pl.pallas_call(partial(head_grads_kernel, shards, heads), in_specs=[pl.Bl...  14 us
    convert_element_type x15, other arithmetic, add_low(): return (x.astype(jnp.float32) + y.astype(jnp.float32)).astype(jnp.bfloat16)  11.9 us
  transfers between devices with their start and end apart: 47, of which 15 were waited for; matrix products, arithmetic and copies ran while one was open for 10% of the time, Pallas kernels for 38%

profile of v2, /device:TPU:0, one launch (start us, length us, event | category | flops | bytes accessed | tf_op | source)
XLA Modules:
  0.0 423.1 jit_solution(3334757426243758667)
XLA Ops:
  19.7 3.9 all-to-all-start
  38.7 8.3 %project_table.1 = (bf16[4,768,192]{2,1,0:T(8,128)(2,1)S(1)}, bf16[3328,192]{1,0:T(8,128)(2,1)S(1)}, bf16[3328,768]{1,0:T(8,128)(2,1)}, f32[8,768]{1,0:T(8,128)S...) custom-call(s32[2]{0:T(128)S(1)} %pad_add_fusion.3.place_ref, bf16[4,192,192]{2,1,0:T(8,128)(2,1)S(1)} %pad_maximum_fusion.3.refs_0_, ...), custom_call_target="tpu_custom_call" | custom-call | tf_op jit(solution)/shard_map/project_table/pallas_call | solution.py:388
  52.2 5.5 %project_states.1 = (bf16[2,1024,192]{2,1,0:T(8,128)(2,1)S(1)}, bf16[1280,192]{1,0:T(8,128)(2,1)S(1)}, bf16[1280,192]{1,0:T(8,128)(2,1)S(1)}, bf16[2304,768]{1,0:T(8,128)(2,1)}) custom-call(s32[2]{0:T(128)S(1)} %pad_add_fusion.3.place_ref, bf16[256,768]{1,0:T(8,128)(2,1)S(1)} %bitcast.130, bf16[256,768]{1,0:T(8,128)(2,1)S(1)} %collective-permute-done.refs_1_, ...), custom_call_target="tpu_custom_call" | custom-call | tf_op jit(solution)/shard_map/project_states/pallas_call | solution.py:447
  60.4 54.8 %attend_forward.1 = (bf16[3,8,256,1280]{3,2,1,0:T(8,128)(2,1)}, f32[3,2,1024,128]{3,2,1,0:T(8,128)}, bf16[4,3,256,128]{3,2,1,0:T(8,128)(2,1)}, bf16[3,1280,128]{...) custom-call(bf16[2,1024,192]{2,1,0:T(8,128)(2,1)} %copy-done.9, ...), custom_call_target="tpu_custom_call" | custom-call | flops 12079595520 | bytes 15728640 | tf_op jit(solution)/shard_map/attend_forward/pallas_call | solution.py:231
  120.0 9.3 %all-to-all-done.1.a_ref = bf16[4,3,256,128]{3,2,1,0:T(8,128)(2,1)S(1)} async-done(((bf16[4,3,256,128]{3,2,1,0:T(8,128)(2,1)}), bf16[4,3,256,128]{3,2,1,0:T(8,128)(2,1)S(1)}, u32[]{:S(2)}, u32[]{:S(2)}) %all-to-all-start.1) | async-done | bytes 786464 | tf_op jit(solution)/shard_map/all_to_all | solution.py:1107
  130.2 27.5 %layer.1 = (bf16[256,768]{1,0:T(8,128)(2,1)}, bf16[256,768]{1,0:T(8,128)(2,1)}, bf16[4,512,192]{2,1,0:T(8,128)(2,1)}, bf16[4,512,192]{2,1,0:T(8,128)(2,1)}, bf16...) custom-call(bf16[4,3,256,128]{3,2,1,0:T(8,128)(2,1)} %copy-done.26, ...), custom_call_target="tpu_custom_call" | custom-call | flops 9663676416 | bytes 25165824 | tf_op jit(solution)/shard_map/layer/pallas_call | solution.py:610
  157.7 7.6 %token_grads.3 = bf16[2,1728,768]{2,1,0:T(8,128)(2,1)} custom-call(s32[1]{0:T(128)} %bitcast.23.core_ref, bf16[512,3072]{1,0:T(8,128)(2,1)} %get-tuple-element.107.active_ref, bf16[4,512,192]{2,1,0:T(8,128)(2,1)} %get-tuple-element.108.inner_ref, bf16[4,512,192]{2,1,0:T(8,128)(2,1)} %get-tuple-element.109.mixed_ref, ...), custom_call_target="tpu_custom_call" | custom-call | flops 2415919104 | bytes 16777216 | tf_op jit(solution)/shard_map/token_grads/pallas_call | solution.py:671
  165.4 4.5 %all-to-all-start.2 = ((bf16[4,3,256,128]{3,2,1,0:T(8,128)(2,1)}), bf16[4,3,256,128]{3,2,1,0:T(8,128)(2,1)}, u32[]{:S(2)}, u32[]{:S(2)}) async-start(bf16[4,3,256,128]{3,2,1,0:T(8,128)(2,1)} %get-tuple-element.106), calls=%async_computation.2 | async-start | bytes 1572864 | tf_op jit(solution)/shard_map/all_to_all | solution.py:1117
  169.8 7.5 %token_grads.2 = bf16[2,1728,768]{2,1,0:T(8,128)(2,1)} custom-call(s32[1]{0:T(128)} %bitcast.22.core_ref, bf16[512,3072]{1,0:T(8,128)(2,1)} %get-tuple-element.107.active_ref, bf16[4,512,192]{2,1,0:T(8,128)(2,1)} %get-tuple-element.108.inner_ref, bf16[4,512,192]{2,1,0:T(8,128)(2,1)} %get-tuple-element.109.mixed_ref, ...), custom_call_target="tpu_custom_call" | custom-call | flops 2415919104 | bytes 16777216 | tf_op jit(solution)/shard_map/token_grads/pallas_call | solution.py:671
  177.4 5.3 %add_convert_fusion = bf16[2,1728,768]{2,1,0:T(8,128)(2,1)S(1)} fusion(bf16[2,1728,768]{2,1,0:T(8,128)(2,1)} %collective-permute-done.12, bf16[2,1728,768]{2,1,0:T(8,128)(2,1)} %token_grads.2), kind=kLoop, calls=%fused_computation | loop fusion | flops 10616832 | bytes 15925248 | tf_op jit(solution)/shard_map/convert_element_type | solution.py:957
  195.0 18.5 %attend_backward.3 = (bf16[4,256,128]{2,1,0:T(8,128)(2,1)}, bf16[1280,128]{1,0:T(8,128)(2,1)}, bf16[3328,64]{1,0:T(8,128)(2,1)}, f32[8,64]{1,0:T(8,128)}) custom-call(bf16[2,1024,192]{2,1,0:T(8,128)(2,1)} %copy-done.9, f32[8,192]{1,0:T(8,128)} %copy-done.14, s32[1024,4]{1,0:T(8,128)} %copy.67.qinfo_ref, bf16[3,1280,128]{2,1,0:T(8,128)(2,1)} %get-tuple-element.100.kaug_ref, ...), custom_call_target="tpu_custom_call" | custom-call | flops 8053063680 | bytes 5242880 | tf_op jit(solution)/shard_map/attend_backward/pallas_call | solution.py:283
  219.5 19.6 %attend_backward.4 = (bf16[4,256,128]{2,1,0:T(8,128)(2,1)}, bf16[1280,128]{1,0:T(8,128)(2,1)}, bf16[3328,64]{1,0:T(8,128)(2,1)}, f32[8,64]{1,0:T(8,128)}) custom-call(bf16[2,1024,192]{2,1,0:T(8,128)(2,1)} %copy-done.9, f32[8,192]{1,0:T(8,128)} %copy-done.14, s32[1024,4]{1,0:T(8,128)} %copy.67.qinfo_ref, bf16[3,1280,128]{2,1,0:T(8,128)(2,1)} %get-tuple-element.100.kaug_ref, ...), custom_call_target="tpu_custom_call" | custom-call | flops 8053063680 | bytes 5242880 | tf_op jit(solution)/shard_map/attend_backward/pallas_call | solution.py:283
  239.1 7.5 %head_grads.2 = bf16[4,192,512]{2,1,0:T(8,128)(2,1)} custom-call(s32[2]{0:T(128)} %copy-done.6, bf16[2304,768]{1,0:T(8,128)(2,1)} %get-tuple-element.122.states_ref, bf16[3328,768]{1,0:T(8,128)(2,1)} %get-tuple-element.123.position_ref, bf16[4,256,128]{2,1,0:T(8,128)(2,1)} %get-tuple-element.114.rest_0_, bf16[4,256,128]{2,1,0:T(8,128)(2,1)} %get-tuple-element.120.rest_1_, ...), custom_call_target="tpu_custom_call" | custom-call | flops 2617245696 | bytes 12582912 | tf_op jit(solution)/shard_map/head_grads/pallas_call | solution.py:791
  251.7 9.2 %collective-permute-done.19 = bf16[1,288,768]{2,1,0:T(8,128)(2,1)S(1)} collective-permute-done((bf16[1,288,768]{2,1,0:T(8,128)(2,1)S(1)}, bf16[1,288,768]{2,1,0:T(8,128)(2,1)S(1)}, u32[]{:S(2)}, u32[]{:S(2)}) %collective-permute-start.19) | collective-permute-done | bytes 442400 | tf_op jit(solution)/shard_map/ppermute | solution.py:929
  261.3 18.5 %attend_backward.5 = (bf16[4,256,128]{2,1,0:T(8,128)(2,1)}, bf16[1280,128]{1,0:T(8,128)(2,1)}, bf16[3328,64]{1,0:T(8,128)(2,1)}, f32[8,64]{1,0:T(8,128)}) custom-call(bf16[2,1024,192]{2,1,0:T(8,128)(2,1)} %copy-done.9, f32[8,192]{1,0:T(8,128)} %copy-done.14, s32[1024,4]{1,0:T(8,128)} %copy.67.qinfo_ref, bf16[3,1280,128]{2,1,0:T(8,128)(2,1)} %get-tuple-element.100.kaug_ref, ...), custom_call_target="tpu_custom_call" | custom-call | flops 8053063680 | bytes 5242880 | tf_op jit(solution)/shard_map/attend_backward/pallas_call | solution.py:283
  287.3 6.5 %head_grads.3 = bf16[4,208,256]{2,1,0:T(8,128)(2,1)} custom-call(s32[2]{0:T(128)} %copy-done.6, bf16[2304,768]{1,0:T(8,128)(2,1)} %get-tuple-element.122.states_ref, bf16[3328,768]{1,0:T(8,128)(2,1)} %get-tuple-element.123.position_ref, bf16[4,256,128]{2,1,0:T(8,128)(2,1)} %get-tuple-element.131.rest_0_, bf16[1280,128]{1,0:T(8,128)(2,1)} %get-tuple-element.132.rest_1_, ...), custom_call_target="tpu_custom_call" | custom-call | flops 2617245696 | bytes 12582912 | tf_op jit(solution)/shard_map/head_grads/pallas_call | solution.py:791
  296.2 3.8 all-to-all-start.4
  304.1 4.7 %all-to-all-done.4 = bf16[8,3,32,128]{3,2,1,0:T(8,128)(2,1)S(1)} async-done(((bf16[8,3,32,128]{3,2,1,0:T(8,128)(2,1)}), bf16[8,3,32,128]{3,2,1,0:T(8,128)(2,1)S(1)}, u32[]{:S(2)}, u32[]{:S(2)}) %all-to-all-start.4) | async-done | bytes 196640 | tf_op jit(solution)/shard_map/all_to_all | solution.py:1171
  308.7 3.7 all-to-all-start.3
  319.4 37.1 %collective-permute-done.27 = bf16[208,256]{1,0:T(8,128)(2,1)S(1)} collective-permute-done((bf16[208,256]{1,0:T(8,128)(2,1)S(1)}, bf16[208,256]{1,0:T(8,128)(2,1)S(1)}, u32[]{:S(2)}, u32[]{:S(2)}) %collective-permute-start.27) | collective-permute-done | bytes 106528 | tf_op jit(solution)/shard_map/ppermute | solution.py:929
  365.7 27.8 %collective-permute-done.30.refs_7_ = bf16[208,256]{1,0:T(8,128)(2,1)S(1)} collective-permute-done((bf16[208,256]{1,0:T(8,128)(2,1)S(1)}, bf16[208,256]{1,0:T(8,128)(2,1)S(1)}, u32[]{:S(2)}, u32[]{:S(2)}) %collective-permute-start.30) | collective-permute-done | bytes 106528 | tf_op jit(solution)/shard_map/ppermute | solution.py:929
  394.5 5.2 %collective-permute-done.23.refs_2_ = bf16[192,512]{1,0:T(8,128)(2,1)S(1)} collective-permute-done((bf16[192,512]{1,0:T(8,128)(2,1)S(1)}, bf16[192,512]{1,0:T(8,128)(2,1)S(1)}, u32[]{:S(2)}, u32[]{:S(2)}) %collective-permute-start.23) | collective-permute-done | bytes 196640 | tf_op jit(solution)/shard_map/ppermute | solution.py:929
  405.4 4.0 unpack_tokens.1
  410.8 5.5 %finish.1 = (bf16[256,768]{1,0:T(8,128)(2,1)}, bf16[256,768]{1,0:T(8,128)(2,1)}, bf16[32,768]{1,0:T(8,128)(2,1)}) custom-call(bf16[4,3,2,256,128]{4,3,2,1,0:T(8,128)(2,1)S(1)} %all-to-all-done.3.token_ref, bf16[2,4,3,32,128]{4,3,2,1,0:T(8,128)(2,1)S(1)} %bitcast.126, f32[512,768]{1,0:T(8,128)S(1)} %copy-done.2, ...), custom_call_target="tpu_custom_call" | custom-call | flops 1207959552 | bytes 8388608 | tf_op jit(solution)/shard_map/finish/pallas_call | solution.py:891
  (269 shorter events, 100.9 us)
Async XLA Ops:
  7.2 112.7 %all-gather.5.cloned.1.call-start = ((), (), s32[]{:S(2)}) async-start(), calls=%async_computation.5 | async-start | bytes 1474560 | tf_op jit(solution)/shard_map/all_gather | solution.py:1063
  8.1 121.2 %all-gather.7.cloned.1.call-start = ((), (), s32[]{:S(2)}) async-start(), calls=%async_computation.6 | async-start | bytes 5898240 | tf_op jit(solution)/shard_map/all_gather | solution.py:1064
  8.9 120.4 %all-gather.9.cloned.1.call-start = ((), (), s32[]{:S(2)}) async-start(), calls=%async_computation.7 | async-start | bytes 5898240 | tf_op jit(solution)/shard_map/all_gather | solution.py:1065
  12.0 20.1 %collective-permute-start.7 = (bf16[4,192,192]{2,1,0:T(8,128)(2,1)S(1)}, bf16[4,192,192]{2,1,0:T(8,128)(2,1)S(1)}, u32[]{:S(2)}, u32[]{:S(2)}) collective-permute-start(bf16[4,192,192]{2,1,0:T(8,128)(2,1)S(1)} %pad_maximum_fusion.3.refs_0_), channel_id=1, source_target_pairs={{0,2},{1,3},{2,0},{3,1},{4,6},{5,7},{6,4},{7,5},{8,10},{9,11},{10,... | collective-permute-start | bytes 884744 | tf_op jit(solution)/shard_map/ppermute | solution.py:929
  15.0 22.0 %collective-permute-start.6 = (bf16[4,192,192]{2,1,0:T(8,128)(2,1)S(1)}, bf16[4,192,192]{2,1,0:T(8,128)(2,1)S(1)}, u32[]{:S(2)}, u32[]{:S(2)}) collective-permute-start(bf16[4,192,192]{2,1,0:T(8,128)(2,1)S(1)} %pad_maximum_fusion.3.refs_0_), channel_id=1, source_target_pairs={{0,1},{1,0},{2,3},{3,2},{4,5},{5,4},{6,7},{7,6},{8,9},{9,8},{10,11... | collective-permute-start | bytes 884744 | tf_op jit(solution)/shard_map/ppermute | solution.py:929
  19.7 30.9 %all-to-all-start = ((bf16[8,32,768]{2,1,0:T(8,128)(2,1)}), bf16[8,32,768]{2,1,0:T(8,128)(2,1)S(1)}, u32[]{:S(2)}, u32[]{:S(2)}) async-start(bf16[8,32,768]{2,1,0:T(8,128)(2,1)} %broadcast_in_dim.31), calls=%async_computation | async-start | bytes 786432 | tf_op jit(solution)/shard_map/all_to_all | solution.py:1056
  30.7 19.9 %collective-permute-start.1 = (bf16[256,768]{1,0:T(8,128)(2,1)S(1)}, bf16[256,768]{1,0:T(8,128)(2,1)}, u32[]{:S(2)}, u32[]{:S(2)}) collective-permute-start(bf16[256,768]{1,0:T(8,128)(2,1)S(1)} %bitcast.129), channel_id=1, source_target_pairs={{0,8},{4,12},{8,0},{12,4},{1,9},{5,13},{9,1},{13,5},{2,10},{6,14},... | collective-permute-start | bytes 1179656 | tf_op jit(solution)/shard_map/ppermute | solution.py:929
  118.9 46.5 %all-gather.11.cloned.1.call-start = ((), (), s32[]{:S(2)}) async-start(), calls=%async_computation.8 | async-start | bytes 4423680 | tf_op jit(solution)/shard_map/all_gather | solution.py:1067
  186.4 31.3 %collective-permute-start.15 = (bf16[2,288,768]{2,1,0:T(8,128)(2,1)}, bf16[2,288,768]{2,1,0:T(8,128)(2,1)}, u32[]{:S(2)}, u32[]{:S(2)}) collective-permute-start(bf16[2,288,768]{2,1,0:T(8,128)(2,1)} %dynamic-slice_bitcast_fusion), channel_id=1, source_target_pairs={{0,8},{8,0},{1,9},{9,1},{2,10},{10,2},{3,11},{11,3},{4,12},{12,4},... | collective-permute-start | bytes 2654216 | tf_op jit(solution)/shard_map/ppermute | solution.py:929
  189.4 29.6 %collective-permute-start.14 = (bf16[2,288,768]{2,1,0:T(8,128)(2,1)}, bf16[2,288,768]{2,1,0:T(8,128)(2,1)S(1)}, u32[]{:S(2)}, u32[]{:S(2)}) collective-permute-start(bf16[2,288,768]{2,1,0:T(8,128)(2,1)} %dynamic-slice_bitcast_fusion.1), channel_id=1, source_target_pairs={{0,4},{4,0},{1,5},{5,1},{2,6},{6,2},{3,7},{7,3},{8,12},{12,8},{9,1... | collective-permute-start | bytes 2654216 | tf_op jit(solution)/shard_map/ppermute | solution.py:929
  191.9 27.4 %collective-permute-start.13 = (bf16[1,576,768]{2,1,0:T(8,128)(2,1)}, bf16[1,576,768]{2,1,0:T(8,128)(2,1)S(1)}, u32[]{:S(2)}, u32[]{:S(2)}) collective-permute-start(bf16[1,576,768]{2,1,0:T(8,128)(2,1)} %constant_dynamic-slice_fusion.4), channel_id=1, source_target_pairs={{0,2},{1,3},{2,0},{3,1},{4,6},{5,7},{6,4},{7,5},{8,10},{9,11},{10,... | collective-permute-start | bytes 2654216 | tf_op jit(solution)/shard_map/ppermute | solution.py:929
  250.3 67.4 %collective-permute-start.20 = (bf16[1,192,512]{2,1,0:T(8,128)(2,1)}, bf16[1,192,512]{2,1,0:T(8,128)(2,1)}, u32[]{:S(2)}, u32[]{:S(2)}) collective-permute-start(bf16[1,192,512]{2,1,0:T(8,128)(2,1)} %constant_dynamic-slice_fusion.2), channel_id=1, source_target_pairs={{0,2},{1,3},{2,0},{3,1},{4,6},{5,7},{6,4},{7,5},{8,10},{9,11},{10,... | collective-permute-start | bytes 589832 | tf_op jit(solution)/shard_map/ppermute | solution.py:929
  282.4 20.7 %collective-permute-start.31 = (bf16[1,144,768]{2,1,0:T(8,128)(2,1)}, bf16[1,144,768]{2,1,0:T(8,128)(2,1)}, u32[]{:S(2)}, u32[]{:S(2)}) collective-permute-start(bf16[1,144,768]{2,1,0:T(8,128)(2,1)} %dynamic-slice_bitcast_fusion.6), channel_id=1, source_target_pairs={{0,8},{8,0},{1,9},{9,1},{2,10},{10,2},{3,11},{11,3},{4,12},{12,4},... | collective-permute-start | bytes 663560 | tf_op jit(solution)/shard_map/ppermute | solution.py:929
  284.4 28.1 %collective-permute-start.32 = (bf16[1,144,768]{2,1,0:T(8,128)(2,1)}, bf16[1,144,768]{2,1,0:T(8,128)(2,1)}, u32[]{:S(2)}, u32[]{:S(2)}) collective-permute-start(bf16[1,144,768]{2,1,0:T(8,128)(2,1)} %constant_dynamic-slice_fusion), channel_id=1, source_target_pairs={{0,2},{1,3},{2,0},{3,1},{4,6},{5,7},{6,4},{7,5},{8,10},{9,11},{10,... | collective-permute-start | bytes 663560 | tf_op jit(solution)/shard_map/ppermute | solution.py:929
  286.8 26.7 %collective-permute-start.33 = (bf16[1,144,768]{2,1,0:T(8,128)(2,1)}, bf16[1,144,768]{2,1,0:T(8,128)(2,1)}, u32[]{:S(2)}, u32[]{:S(2)}) collective-permute-start(bf16[1,144,768]{2,1,0:T(8,128)(2,1)} %dynamic-slice_bitcast_fusion.5), channel_id=1, source_target_pairs={{0,4},{4,0},{1,5},{5,1},{2,6},{6,2},{3,7},{7,3},{8,12},{12,8},{9,1... | collective-permute-start | bytes 663560 | tf_op jit(solution)/shard_map/ppermute | solution.py:929
  308.7 100.7 %all-to-all-start.3 = ((bf16[4,3,2,256,128]{4,3,2,1,0:T(8,128)(2,1)}), bf16[4,3,2,256,128]{4,3,2,1,0:T(8,128)(2,1)S(1)}, u32[]{:S(2)}, u32[]{:S(2)}) async-start(bf16[4,3,2,256,128]{4,3,2,1,0:T(8,128)(2,1)} %pad_maximum_fusion), calls=%async_computation.3 | async-start | bytes 3145728 | tf_op jit(solution)/shard_map/all_to_all | solution.py:1167
  314.6 43.7 %collective-permute-start.34 = (bf16[3,144,768]{2,1,0:T(8,128)(2,1)S(1)}, bf16[3,144,768]{2,1,0:T(8,128)(2,1)S(1)}, u32[]{:S(2)}, u32[]{:S(2)}) collective-permute-start(bf16[3,144,768]{2,1,0:T(8,128)(2,1)S(1)} %pad_maximum_fusion.2), channel_id=1, source_target_pairs={{0,16},{16,0},{1,17},{17,1},{2,18},{18,2},{3,19},{19,3},{4,20},{20... | collective-permute-start | bytes 1990664 | tf_op jit(solution)/shard_map/ppermute | solution.py:929
  315.4 41.1 %collective-permute-start.27 = (bf16[208,256]{1,0:T(8,128)(2,1)S(1)}, bf16[208,256]{1,0:T(8,128)(2,1)S(1)}, u32[]{:S(2)}, u32[]{:S(2)}) collective-permute-start(bf16[208,256]{1,0:T(8,128)(2,1)S(1)} %fusion.9), channel_id=1, source_target_pairs={{0,16},{16,0},{1,17},{17,1},{2,18},{18,2},{3,19},{19,3},{4,20},{20... | collective-permute-start | bytes 319496 | tf_op jit(solution)/shard_map/ppermute | solution.py:929
  318.7 42.2 %collective-permute-start.21 = (bf16[192,512]{1,0:T(8,128)(2,1)S(1)}, bf16[192,512]{1,0:T(8,128)(2,1)S(1)}, u32[]{:S(2)}, u32[]{:S(2)}) collective-permute-start(bf16[192,512]{1,0:T(8,128)(2,1)S(1)} %fusion.8), channel_id=1, source_target_pairs={{0,16},{16,0},{1,17},{17,1},{2,18},{18,2},{3,19},{19,3},{4,20},{20... | collective-permute-start | bytes 589832 | tf_op jit(solution)/shard_map/ppermute | solution.py:929
  358.5 46.9 %collective-permute-start.35 = (bf16[3,144,768]{2,1,0:T(8,128)(2,1)S(1)}, bf16[3,144,768]{2,1,0:T(8,128)(2,1)S(1)}, u32[]{:S(2)}, u32[]{:S(2)}) collective-permute-start(bf16[3,144,768]{2,1,0:T(8,128)(2,1)S(1)} %add_convert_fusion.2.refs_0_), channel_id=1, source_target_pairs={{0,4},{4,0},{8,12},{12,8},{1,5},{5,1},{9,13},{13,9},{2,6},{6,2},{1... | collective-permute-start | bytes 1990664 | tf_op jit(solution)/shard_map/ppermute | solution.py:929
  358.9 46.5 %collective-permute-start.36 = (bf16[3,144,768]{2,1,0:T(8,128)(2,1)S(1)}, bf16[3,144,768]{2,1,0:T(8,128)(2,1)}, u32[]{:S(2)}, u32[]{:S(2)}) collective-permute-start(bf16[3,144,768]{2,1,0:T(8,128)(2,1)S(1)} %add_convert_fusion.2.refs_0_), channel_id=1, source_target_pairs={{0,8},{4,12},{8,0},{12,4},{1,9},{5,13},{9,1},{13,5},{2,10},{6,14},... | collective-permute-start | bytes 1990664 | tf_op jit(solution)/shard_map/ppermute | solution.py:929
  360.9 44.5 %collective-permute-start.37 = (bf16[3,144,768]{2,1,0:T(8,128)(2,1)S(1)}, bf16[3,144,768]{2,1,0:T(8,128)(2,1)}, u32[]{:S(2)}, u32[]{:S(2)}) collective-permute-start(bf16[3,144,768]{2,1,0:T(8,128)(2,1)S(1)} %add_convert_fusion.2.refs_0_), channel_id=1, source_target_pairs={{0,12},{4,8},{8,4},{12,0},{1,13},{5,9},{9,5},{13,1},{2,14},{6,10},... | collective-permute-start | bytes 1990664 | tf_op jit(solution)/shard_map/ppermute | solution.py:929
  362.5 30.9 %collective-permute-start.22 = (bf16[192,512]{1,0:T(8,128)(2,1)S(1)}, bf16[192,512]{1,0:T(8,128)(2,1)S(1)}, u32[]{:S(2)}, u32[]{:S(2)}) collective-permute-start(bf16[192,512]{1,0:T(8,128)(2,1)S(1)} %add_convert_fusion.5.refs_0_), channel_id=1, source_target_pairs={{0,4},{4,0},{8,12},{12,8},{1,5},{5,1},{9,13},{13,9},{2,6},{6,2},{1... | collective-permute-start | bytes 589832 | tf_op jit(solution)/shard_map/ppermute | solution.py:929
  364.2 29.2 %collective-permute-start.30 = (bf16[208,256]{1,0:T(8,128)(2,1)S(1)}, bf16[208,256]{1,0:T(8,128)(2,1)S(1)}, u32[]{:S(2)}, u32[]{:S(2)}) collective-permute-start(bf16[208,256]{1,0:T(8,128)(2,1)S(1)} %add_convert_fusion.7.refs_4_), channel_id=1, source_target_pairs={{0,12},{4,8},{8,4},{12,0},{1,13},{5,9},{9,5},{13,1},{2,14},{6,10},... | collective-permute-start | bytes 319496 | tf_op jit(solution)/shard_map/ppermute | solution.py:929
  (71 other events, 684.4 us)
Sparse Core Ops, SparseCore 0:
  9.6 22.4 all-gather.4
  33.7 38.8 all-gather.6
  74.2 37.4 all-gather.8
  120.9 32.9 all-gather.10

commit v3 on v2

--- a/solution.py
+++ b/solution.py
@@ -517,7 +517,7 @@
         acc[at, :] = middle + outer
     copies[1].wait()
     copies[2].wait()
-    step = 512
+    step = 1024
     chunks = hidden_w.shape[1] // step
     root = 0.7978845608028654
 
@@ -537,7 +537,7 @@
             acc[part, :] += mm(active, return_w[at, :])
         return carry
 
-    lax.fori_loop(0, chunks, forward, 0)
+    lax.fori_loop(0, chunks, forward, 0, unroll=True)
     sums = []
     for s, (upstream, result) in enumerate(
         ((up_content_ref, out_content_ref), (up_query_ref, out_query_ref))
@@ -573,7 +573,7 @@
         inner_sum_ref[:, at] = total
         return carry
 
-    lax.fori_loop(0, chunks, backward, 0)
+    lax.fori_loop(0, chunks, backward, 0, unroll=True)
     sums = []
     for s in range(2):
         at = slice(s * tokens, (s + 1) * tokens)
@@ -644,62 +644,109 @@
     )(a, content, query, up_content, up_query, vectors, inner, output_w, hidden_w, return_w)
 
 
-def token_grads_kernel(
-    core_ref, active_ref, inner_ref, mixed_ref, returned_ref, zgrad_ref, branch_ref, out_ref
+def shard_grads(inner_ref, active_ref, mixed_ref, returned_ref, zgrad_ref, branch_ref):
+    rows_w = inner_ref.shape[2]
+    count = zgrad_ref.shape[1] // D
+    hidden = mm(inner_ref[0], zgrad_ref[...], TN)
+    back = mm(active_ref[...], returned_ref[...], TN)
+    hidden = [hidden[:, j * D : (j + 1) * D] for j in range(count)]
+    back = [back[j * rows_w : (j + 1) * rows_w] for j in range(count)]
+    mixed = mm(mixed_ref[0], branch_ref[...], TN)
+    return hidden[:3] + back[:3] + [hidden[3], back[3], mixed]
+
+
+def send_grads_kernel(
+    place_ref, active_ref, inner_ref, mixed_ref, returned_ref, zgrad_ref, branch_ref, out_ref
 ):
     rows_w = inner_ref.shape[2]
-    low = partial(jnp.asarray, dtype=jnp.bfloat16)
-    count = zgrad_ref.shape[1] // D
-    block = mm(inner_ref[0], zgrad_ref[...], TN)
-    spots = [0, 1, 2, 6]
-    for j in range(count):
-        at = spots[j] * rows_w
-        out_ref[0, at : at + rows_w, :] = low(block[:, j * D : (j + 1) * D])
-    block = mm(active_ref[...], returned_ref[...], TN)
-    spots = [3, 4, 5, 7]
-    for j in range(count):
-        at = spots[j] * rows_w
-        out_ref[0, at : at + rows_w, :] = low(block[j * rows_w : (j + 1) * rows_w])
-    out_ref[0, 8 * rows_w :, :] = low(mm(mixed_ref[0], branch_ref[...], TN))
-
-
-def token_grads(core, active, inner, mixed, returned, zgrad, branch):
+    blocks = shard_grads(
+        inner_ref, active_ref, mixed_ref, returned_ref, zgrad_ref, branch_ref
+    )
+    for i, block in enumerate(blocks):
+        out_ref[0, i * rows_w : (i + 1) * rows_w, :] = block.astype(jnp.bfloat16)
+
+
+def keep_grads_kernel(
+    place_ref, active_ref, inner_ref, mixed_ref, returned_ref, zgrad_ref, branch_ref, other_ref,
+    keep_y, send_y, keep_x, send_x, keep_z, send_z,
+):
+    rows_w = inner_ref.shape[2]
+    step = pl.program_id(0)
+    blocks = shard_grads(
+        inner_ref, active_ref, mixed_ref, returned_ref, zgrad_ref, branch_ref
+    )
+    sums = []
+    for i, block in enumerate(blocks):
+        other = other_ref[0, i * rows_w : (i + 1) * rows_w, :].astype(jnp.float32)
+        sums.append((block + other).astype(jnp.bfloat16))
+    chains = [jnp.concatenate(sums[i : i + 3], axis=0) for i in (0, 3, 6)]
+    half = chains[0].shape[0] // 2
+    own_y, own_x, own_z = place_ref[1], place_ref[2], place_ref[3]
+
+    @pl.when(step == own_y)
+    def _():
+        keep_y[0] = chains[0]
+
+    @pl.when(step != own_y)
+    def _():
+        send_y[0] = chains[0]
+
+    for chain, own, keep, send in (
+        (chains[1], own_x, keep_x, send_x),
+        (chains[2], own_z, keep_z, send_z),
+    ):
+        keep[0] = jnp.where(own == 0, chain[:half], chain[half:])
+        send[0] = jnp.where(own == 0, chain[half:], chain[:half])
+
+
+def token_grads(place, grads, other=None):
+    active, inner = grads[:2]
     shards, rows, rows_w = inner.shape
     hidden = active.shape[1]
     per = hidden // shards
-    block = (1, 9 * rows_w, D)
+    pairs = shards // 2
+    low = partial(jax.ShapeDtypeStruct, dtype=jnp.bfloat16)
+    whole_block = pl.BlockSpec((1, 9 * rows_w, D), lambda i, c: (i, 0, 0))
+    in_specs = [
+        pl.BlockSpec((rows, per), lambda i, c: (0, 2 * i + c[0])),
+        pl.BlockSpec((1, rows, rows_w), lambda i, c: (2 * i + c[0], 0, 0)),
+        pl.BlockSpec((1, rows, rows_w), lambda i, c: (2 * i + c[0], 0, 0)),
+        pl.BlockSpec((rows, D), lambda i, c: (0, 0)),
+        pl.BlockSpec((rows, hidden), lambda i, c: (0, 0)),
+        pl.BlockSpec((rows, D), lambda i, c: (0, 0)),
+    ]
+    if other is None:
+        kernel, operands = send_grads_kernel, tuple(grads)
+        out_specs, out_shape = whole_block, low((pairs, 9 * rows_w, D))
+    else:
+        kernel, operands = keep_grads_kernel, tuple(grads) + (other,)
+        in_specs.append(whole_block)
+        half = 3 * rows_w // 2
+        out_specs = [pl.BlockSpec((1, 3 * rows_w, D), lambda i, c: (0, 0, 0))] * 2
+        out_specs += [pl.BlockSpec((1, half, D), lambda i, c: (i, 0, 0))] * 4
+        out_shape = [low((1, 3 * rows_w, D))] * 2 + [low((pairs, half, D))] * 4
     return pl.pallas_call(
-        token_grads_kernel,
+        kernel,
         grid_spec=pltpu.PrefetchScalarGridSpec(
-            num_scalar_prefetch=1,
-            grid=(shards // 2,),
-            in_specs=[
-                pl.BlockSpec((rows, per), lambda i, c: (0, 2 * i + c[0])),
-                pl.BlockSpec((1, rows, rows_w), lambda i, c: (2 * i + c[0], 0, 0)),
-                pl.BlockSpec((1, rows, rows_w), lambda i, c: (2 * i + c[0], 0, 0)),
-                pl.BlockSpec((rows, D), lambda i, c: (0, 0)),
-                pl.BlockSpec((rows, hidden), lambda i, c: (0, 0)),
-                pl.BlockSpec((rows, D), lambda i, c: (0, 0)),
-            ],
-            out_specs=pl.BlockSpec(block, lambda i, c: (i, 0, 0)),
+            num_scalar_prefetch=1, grid=(pairs,), in_specs=in_specs, out_specs=out_specs
         ),
-        out_shape=jax.ShapeDtypeStruct((shards // 2,) + block[1:], jnp.bfloat16),
+        out_shape=out_shape,
         compiler_params=pltpu.CompilerParams(vmem_limit_bytes=56 * 2**20),
         cost_estimate=pl.CostEstimate(
             flops=2 * rows * D * hidden, bytes_accessed=16 * 2**20, transcendentals=0
         ),
         name="token_grads",
-    )(core.reshape(1), active, inner, mixed, returned, zgrad, branch)
+    )(place, *operands)
 
 
 def unpack_tokens_kernel(members, head_count, place_ref, *refs):
-    pieces, (hidden_ref, return_ref, output_ref, held) = refs[:members], refs[members:]
+    pieces, (hidden_ref, return_ref, output_ref, held) = refs[: 2 * members], refs[2 * members :]
     rows_w = hidden_ref.shape[0]
     chains, per, _ = held.shape[1:]
     for m in range(members):
-        held[m] = pieces[m][...]
+        held[m, : chains - 1] = pieces[m][...]
+        held[m, chains - 1 :] = pieces[members + m][...]
     member = place_ref[1]
-    targets = {0: 0, 1: 1, 2: 2, 6: 3}
     for g in range(members):
         head, half = g % head_count, g // head_count
         for c in range(chains):
@@ -715,31 +762,32 @@
                 value = held[member ^ g, c, done : done + count, :].astype(jnp.float32)
                 if block == 8:
                     output_ref[at : at + count, :] = value
-                elif block in targets:
-                    j = targets[block]
+                elif block in (0, 1, 2, 6):
+                    j = min(block, 3)
                     hidden_ref[at : at + count, j * D : (j + 1) * D] = value
                 else:
-                    j = {3: 0, 4: 1, 5: 2, 7: 3}[block]
+                    j = min(block - 3, 3)
                     return_ref[j * rows_w + at : j * rows_w + at + count, :] = value
                 done += count
 
 
-def unpack_tokens(place, rows_w, head_count, pieces):
-    members = len(pieces)
+def unpack_tokens(place, rows_w, head_count, early, late):
+    members = len(early)
     vmem = pl.BlockSpec(memory_space=pltpu.VMEM)
+    chains = early[0].shape[0] + late[0].shape[0]
     return pl.pallas_call(
         partial(unpack_tokens_kernel, members, head_count),
-        in_specs=[pl.BlockSpec(memory_space=pltpu.SMEM)] + [vmem] * members,
+        in_specs=[pl.BlockSpec(memory_space=pltpu.SMEM)] + [vmem] * 2 * members,
         out_specs=[vmem] * 3,
         out_shape=[
             jax.ShapeDtypeStruct((rows_w, 4 * D), jnp.float32),
             jax.ShapeDtypeStruct((4 * rows_w, D), jnp.float32),
             jax.ShapeDtypeStruct((rows_w, D), jnp.float32),
         ],
-        scratch_shapes=[pltpu.VMEM((members,) + pieces[0].shape, jnp.bfloat16)],
+        scratch_shapes=[pltpu.VMEM((members, chains) + early[0].shape[1:], jnp.bfloat16)],
         compiler_params=pltpu.CompilerParams(vmem_limit_bytes=48 * 2**20),
         name="unpack_tokens",
-    )(place, *pieces)
+    )(place, *early, *late)
 
 
 def head_grads_kernel(shards, heads, place_ref, states_ref, position_ref, *rest):
@@ -849,28 +897,27 @@
 
 
 def finish_kernel(
-    token_ref, prompt_ref, residual_ref, weight_hbm, content_ref, query_ref, out_prompt_ref,
-    weight, parts, prompts, sem,
+    early_ref, late_ref, prompt_ref, residual_ref, weight_hbm,
+    content_ref, query_ref, out_prompt_ref, weight, parts, prompts, sem,
 ):
     copy = pltpu.make_async_copy(weight_hbm, weight, sem)
     copy.start()
-    members, heads, _, tokens, wide = token_ref.shape
-    chapters = prompt_ref.shape[0]
+    members, before, _, _ = early_ref.shape
+    tokens = content_ref.shape[0]
+    heads = before + late_ref.shape[1]
     for g in range(members):
         for h in range(heads):
             spot = (g * heads + h) * HEAD_DIM
+            source, i = (early_ref, h) if h < before else (late_ref, h - before)
             for kind in range(4):
                 at = (kind % 2) * HEAD_DIM
-                parts[kind, :, spot : spot + HEAD_DIM] = token_ref[
-                    g, h, kind // 2, :, at : at + HEAD_DIM
+                start = (kind // 2) * tokens
+                parts[kind, :, spot : spot + HEAD_DIM] = source[
+                    g, i, start : start + tokens, at : at + HEAD_DIM
                 ]
-            total = prompt_ref[0, g, h].astype(jnp.float32)
-            for c in range(1, chapters):
-                total += prompt_ref[c, g, h].astype(jnp.float32)
-            total = total.astype(jnp.bfloat16)
             for kind in range(2):
-                prompts[kind, :, spot : spot + HEAD_DIM] = total[
-                    :, kind * HEAD_DIM : (kind + 1) * HEAD_DIM
+                prompts[kind, :, spot : spot + HEAD_DIM] = prompt_ref[
+                    g, h, :, kind * HEAD_DIM : (kind + 1) * HEAD_DIM
                 ]
     copy.wait()
     query, key, value = (weight[:, i * D : (i + 1) * D] for i in range(3))
@@ -884,13 +931,13 @@
     )
 
 
-def finish(token_back, prompt_back, residual, weights):
-    tokens = token_back.shape[3]
-    prompt = prompt_back.shape[3]
+def finish(rows_early, rows_late, prompt_back, residual, weights):
+    tokens = residual.shape[0] // 2
+    prompt = prompt_back.shape[2]
     vmem = pl.BlockSpec(memory_space=pltpu.VMEM)
     return pl.pallas_call(
         finish_kernel,
-        in_specs=[vmem] * 3 + [pl.BlockSpec(memory_space=pl.ANY)],
+        in_specs=[vmem] * 4 + [pl.BlockSpec(memory_space=pl.ANY)],
         out_specs=[vmem] * 3,
         out_shape=[
             jax.ShapeDtypeStruct((tokens, D), jnp.bfloat16),
@@ -908,7 +955,7 @@
             flops=8 * tokens * D * D, bytes_accessed=8 * 2**20, transcendentals=0
         ),
         name="finish",
-    )(token_back, prompt_back, residual, weights)
+    )(rows_early, rows_late, prompt_back, residual, weights)
 
 
 def axes_size(axes):
@@ -1033,6 +1080,8 @@
     def columns(x):
         return lax.dynamic_slice_in_dim(x, member * width, width, x.ndim - 1)
 
+    tie = lax.optimization_barrier
+
     content = {0: content_rows}
     query = {0: query_rows}
     content[1], query[2] = swap(content_rows, GROUP, 1), swap(query_rows, GROUP, 2)
@@ -1117,77 +1166,109 @@
     grad_out = lax.all_to_all(grad_out, GROUP, 0, 0, tiled=True)
 
     core = shard & 1
+    bits = [shard >> 1, lax.axis_index("head"), lax.axis_index("half")]
     grads = (active, inner_in, mixed_flat, returned_grad, inner_grad, branch_grad)
-    sent = swap(token_grads(1 - core, *grads), SHARD, 1)
-    total = add_low(token_grads(core, *grads), sent)
-    third = total.shape[1] // 3
-    chains = [total[:, i * third : (i + 1) * third] for i in range(3)]
-    rest = [(SHARD, bit) for bit in bits_of(SHARD) if bit > 0]
-    head_stage, half_stage, cont_stage = (stages_of((name,)) for name in ("head", "half", "cont"))
+    sent = swap(token_grads(jnp.stack([1 - core] + bits), grads), SHARD, 1)
+    parts = token_grads(jnp.stack([core] + bits), grads, sent)
+    stage_y, stage_x, stage_z = (SHARD, 1), (("head",), 0), (("half",), 0)
+    cont_stage = stages_of(("cont",))
     orders = (
-        (rest, head_stage, half_stage),
-        (head_stage, half_stage, rest),
-        (half_stage, rest, head_stage),
-    )
-
-    def chain_stage(x, stages):
-        for axes, bit in stages:
-            if axes == SHARD:
-                x = half_sum(x.reshape((-1, 2) + x.shape[1:]), axes, bit, 1)
-            else:
-                x = half_sum(split_axis(x, 1), axes, bit, 1)
-        return x
+        (stage_y, stage_x, stage_z),
+        (stage_x, stage_z, stage_y),
+        (stage_z, stage_y, stage_x),
+    )
+    chains = [
+        (kept, swap(out, order[0][0], 1 << order[0][1]))
+        for kept, out, order in zip(parts[::2], parts[1::2], orders)
+    ]
+
+    def next_stage(chain, stage):
+        axes, bit = stage
+        x = add_low(*chain)
+        axis = 0 if axes == SHARD else 1
+        x = split_axis(x, axis)
+        own = flat_index(axes) >> bit & 1
+        return pick(x, own, axis), swap(pick(x, 1 - own, axis), axes, 1 << bit)
 
     small_grads = (token_sums, inner_bias_grad)
-    backward, head_parts = [], []
-    for h in range(local_heads):
-        grad_out, chains = lax.optimization_barrier((grad_out, chains))
-        backward.append(
-            attend_backward(h, q, head_bias, qinfo, kaug, vaug, table_rows, p, a, grad_out)
-        )
-        chains = [chain_stage(x, orders[i][h]) for i, x in enumerate(chains)]
-        if h == local_heads - 2:
-            dq, dkv, dt, _ = zip(*backward)
-            x = head_grads(place, shards, states, positions, dq, dkv, dt)
-            x = half_sum(x.reshape((-1, 2) + x.shape[1:]), SHARD, 0, 1)
-            head_parts.append(x)
-            grad_out, head_parts = lax.optimization_barrier((grad_out, head_parts))
+
+    def attend_back(h, grad_out):
+        return attend_backward(h, q, head_bias, qinfo, kaug, vaug, table_rows, p, a, grad_out)
+
+    last = local_heads - 1
+    grad_out, parts = tie((grad_out, parts))
+    backward = [attend_back(0, grad_out)]
+    grad_out, chains = tie((grad_out, chains))
+    chains = [next_stage(x, order[1]) for x, order in zip(chains, orders)]
+    backward += [attend_back(h, grad_out) for h in range(1, last)]
+    backward, chains = tie((backward, chains))
+    chains = [next_stage(x, order[2]) for x, order in zip(chains, orders)]
+    dq, dkv, dt, _ = zip(*backward)
+    x = head_grads(place, shards, states, positions, dq, dkv, dt)
+    x, chains, dq, dkv = tie((x, chains, dq, dkv))
+    chains = [add_low(*x) for x in chains]
+
+    def shard_stage(x, bit):
+        return half_sum(x.reshape((-1, 2) + x.shape[1:]), SHARD, bit, 1)
+
+    def row_parts(heads):
+        parts = []
+        for h in heads:
+            prompts = dkv[h][:prompt_total].reshape(chapters, members, prompt_part, -1)
+            prompts = jnp.transpose(prompts, (1, 0, 2, 3)).reshape(members, -1, dq[h].shape[2])
+            own = dkv[h][prompt_total:].reshape(dq[h].shape)
+            parts.append(jnp.concatenate([dq[h], own, prompts], axis=1))
+        return lax.all_to_all(jnp.stack(parts, axis=1), GROUP, 0, 0, tiled=True)
+
+    first = shard_stage(x, 0)
+    grad_out, chains, first = tie((grad_out, chains, first))
+    early = full_sum(jnp.concatenate(chains[:2]), cont_stage)
+    first = shard_stage(first, 1)
+    rows_early = row_parts(range(last))
+    backward.append(attend_back(last, grad_out))
+    backward[last], late, first, early, rows_early = tie(
+        (backward[last], chains[2], first, early, rows_early)
+    )
+    late = full_sum(late, cont_stage)
+    first = full_sum(first[0], cont_stage)
+    early_near = [early] + [swap(early, GROUP, 1 << bit) for bit in bits_of(GROUP)]
+    early_dq, early_dkv = dq, dkv
     dq, dkv, dt, sums = zip(*backward)
+    dq, dkv = early_dq + dq[last:], early_dkv + dkv[last:]
+    rows_late = row_parts([last])
     x = head_grads(
         place, shards, states, positions, dq[-1:], dkv[-1:], dt[-1:], small_grads + sums
     )
-    head_parts.append(half_sum(x.reshape((-1, 2) + x.shape[1:]), SHARD, 0, 1))
-    token_back = jnp.stack(
-        [
-            jnp.stack([dq[h], dkv[h][prompt_total:].reshape(dq[h].shape)], axis=1)
-            for h in range(local_heads)
-        ],
-        axis=1,
-    )
-    token_back = lax.all_to_all(token_back, GROUP, 0, 0, tiled=True)
-    prompt_back = jnp.stack(
-        [x[:prompt_total].reshape(chapters * members, prompt_part, -1) for x in dkv], axis=1
-    )
-    prompt_back = lax.all_to_all(prompt_back, JOB, 0, 0, tiled=True)
-    prompt_back = prompt_back.reshape((chapters, members) + prompt_back.shape[1:])
-
-    chains = jnp.concatenate(chains)
-    chains = full_sum(chains, cont_stage)
+    x, late, rows_late, first, early_near = tie((x, late, rows_late, first, early_near))
+    early_pieces = dict(zip([0] + [1 << bit for bit in bits_of(GROUP)], early_near))
+    for m in range(members):
+        if m not in early_pieces:
+            early_pieces[m] = swap(early_near[0], GROUP, m)
+    early_pieces = [early_pieces[m] for m in range(members)]
+    late_pieces = group_pieces(late, GROUP)
+    prompt_back = jnp.concatenate([rows_early[:, :, 2 * tokens :], rows_late[:, :, 2 * tokens :]], 1)
+    prompt_back = prompt_back.reshape(prompt_back.shape[:2] + (chapters, prompt_part, -1))
+    prompt_back = jnp.transpose(prompt_back, (2, 0, 1, 3, 4))
+    for axes, bit in reversed(cont_stage):
+        prompt_back = half_sum(split_axis(prompt_back, 0), axes, bit, 0)
+    second = shard_stage(shard_stage(x, 0), 1)
+    first = group_pieces(first, GROUP)
+    second = full_sum(second[0], cont_stage)
+    second, early_pieces, late_pieces, prompt_back = tie(
+        (second, early_pieces, late_pieces, prompt_back)
+    )
+    head_pieces = [first, group_pieces(second, GROUP)]
+
     hidden_total, return_total, output_total = unpack_tokens(
-        place, rows_w, lax.axis_size("head"), group_pieces(chains, GROUP)
-    )
-    head_pieces = []
-    for x in head_parts:
-        for axes, bit in rest:
-            x = half_sum(x.reshape((-1, 2) + x.shape[1:]), axes, bit, 1)
-        head_pieces.append(group_pieces(full_sum(x[0], cont_stage), GROUP))
+        place, rows_w, lax.axis_size("head"), early_pieces, late_pieces
+    )
     query_grad, key_grad, value_grad, relative_grad, small_total = unpack(
         place, rows_w, *head_pieces
     )
     vector_total = small_total[:10, :rows_w]
     inner_total = small_total[10:14, :rows_w].reshape(-1)
     content_grad, queries_grad, prompt_grad = finish(
-        token_back, prompt_back, residual_grad, attention_full
+        rows_early, rows_late, prompt_back[0], residual_grad, attention_full
     )
     return (
         out_content[None],

time: 429 us -> 362 us (0.84)
  waiting for transfers between devices: 104 us -> 53.5 us
  local copies, waits for them, and re-layouts: 32.9 us -> 20.2 us
  starting transfers between devices: 56.8 us -> 68.8 us
  other arithmetic: 19.6 us -> 10.4 us
  Pallas kernels: 194 us -> 188 us
    ppermute x38 -> x43, waiting for transfers between devices: 87.6 us -> 43 us  [swap(): lax.ppermute(x, axes, [(i, i ^ mask) for i in range(axes_size(axes))])]
    ppermute x38 -> x43, starting transfers between devices: 37.1 us -> 49.1 us  [swap(): lax.ppermute(x, axes, [(i, i ^ mask) for i in range(axes_size(axes))])]
    squeeze x13 -> x11, local copies, waits for them, and re-layouts: 9.83 us -> 2.03 us  [pick(): return lax.dynamic_index_in_dim(x, index, axis, keepdims=False)]
    convert_element_type x15 -> x17, other arithmetic: 11.9 us -> 4.43 us  [add_low(): return (x.astype(jnp.float32) + y.astype(jnp.float32)).astype(jnp.bfloat16)]
    pallas_call x1, Pallas kernels: 27.5 us -> 20.8 us  [layer(): pl.pallas_call(layer_kernel, in_specs=[vmem] * 7 + [pl.BlockSpec(memory_s...]
    slice x7 -> x8, local copies, waits for them, and re-layouts: 5.83 us -> 0.09 us  [the longest x3 0.06 us: row_parts(): own = dkv[h][prompt_total:].reshape(dq[h].shape)]
    all_to_all x2, waiting for transfers between devices: 4.65 us -> 0.01 us  [row_parts(): return lax.all_to_all(jnp.stack(parts, axis=1), GROUP, 0, 0, tiled=True)]
    unnamed x96 -> x109, local copies, waits for them, and re-layouts: 8.73 us -> 9.55 us
  transfers between devices with their start and end apart: 47 -> 52, of which waited for: 15 -> 18; matrix products, arithmetic and copies ran while one was open for 10% -> 4% of each run, Pallas kernels for 38% -> 52%
where the time goes in v3:
time: 362 us; the launch traced here: 357 us
  Pallas kernels  188 us (52%)
  starting transfers between devices  68.8 us (19%)
  waiting for transfers between devices  53.5 us (15%)
  local copies, waits for them, and re-layouts  20.2 us (6%)
  between operations  16.5 us (5%)
  other arithmetic  10.4 us (3%)
    pallas_call x3, Pallas kernels, attend_backward(): pl.pallas_call(partial(backward_kernel, head), grid=(steps,), in_specs=[p...  55.9 us
    pallas_call x1, Pallas kernels, attend_forward(): pl.pallas_call(forward_kernel, grid=(steps,), in_specs=[pl.BlockSpec((2,...  54.8 us
    ppermute x43, starting transfers between devices, swap(): lax.ppermute(x, axes, [(i, i ^ mask) for i in range(axes_size(axes))])  49.1 us
    ppermute x43, waiting for transfers between devices, swap(): lax.ppermute(x, axes, [(i, i ^ mask) for i in range(axes_size(axes))])  43 us
    pallas_call x1, Pallas kernels, layer(): pl.pallas_call(layer_kernel, in_specs=[vmem] * 7 + [pl.BlockSpec(memory_s...  20.8 us
    pallas_call x2, Pallas kernels, token_grads(): pl.pallas_call(kernel, grid_spec=pltpu.PrefetchScalarGridSpec(num_scalar_...  17.9 us
    pallas_call x2, Pallas kernels, head_grads(): pl.pallas_call(partial(head_grads_kernel, shards, heads), in_specs=[pl.Bl...  14 us
    unnamed x109, local copies, waits for them, and re-layouts  9.55 us
  transfers between devices with their start and end apart: 52, of which 18 were waited for; matrix products, arithmetic and copies ran while one was open for 4% of the time, Pallas kernels for 52%

profile of v3, /device:TPU:0, one launch (start us, length us, event | category | flops | bytes accessed | tf_op | source)
XLA Modules:
  0.0 357.1 jit_solution(14296911687559404041)
XLA Ops:
  19.7 3.9 %all-to-all-start = ((bf16[8,32,768]{2,1,0:T(8,128)(2,1)}), bf16[8,32,768]{2,1,0:T(8,128)(2,1)S(1)}, u32[]{:S(2)}, u32[]{:S(2)}) async-start(bf16[8,32,768]{2,1,0:T(8,128)(2,1)} %broadcast_in_dim.31), calls=%async_computation | async-start | bytes 786432 | tf_op jit(solution)/shard_map/all_to_all | solution.py:1105
  38.7 8.2 %project_table.1 = (bf16[4,768,192]{2,1,0:T(8,128)(2,1)S(1)}, bf16[3328,192]{1,0:T(8,128)(2,1)S(1)}, bf16[3328,768]{1,0:T(8,128)(2,1)}, f32[8,768]{1,0:T(8,128)S...) custom-call(s32[2]{0:T(128)S(1)} %pad_add_fusion.3.place_ref, bf16[4,192,192]{2,1,0:T(8,128)(2,1)S(1)} %pad_maximum_fusion.2.refs_0_, ...), custom_call_target="tpu_custom_call" | custom-call | tf_op jit(solution)/shard_map/project_table/pallas_call | solution.py:388
  52.2 5.5 %project_states.1 = (bf16[2,1024,192]{2,1,0:T(8,128)(2,1)S(1)}, bf16[1280,192]{1,0:T(8,128)(2,1)S(1)}, bf16[1280,192]{1,0:T(8,128)(2,1)S(1)}, bf16[2304,768]{1,0:T(8,128)(2,1)}) custom-call(s32[2]{0:T(128)S(1)} %pad_add_fusion.3.place_ref, bf16[256,768]{1,0:T(8,128)(2,1)S(1)} %bitcast.123, bf16[256,768]{1,0:T(8,128)(2,1)S(1)} %collective-permute-done.refs_1_, ...), custom_call_target="tpu_custom_call" | custom-call | tf_op jit(solution)/shard_map/project_states/pallas_call | solution.py:447
  60.4 54.8 %attend_forward.1 = (bf16[3,8,256,1280]{3,2,1,0:T(8,128)(2,1)}, f32[3,2,1024,128]{3,2,1,0:T(8,128)}, bf16[4,3,256,128]{3,2,1,0:T(8,128)(2,1)}, bf16[3,1280,128]{...) custom-call(bf16[2,1024,192]{2,1,0:T(8,128)(2,1)} %copy-done.11, ...), custom_call_target="tpu_custom_call" | custom-call | flops 12079595520 | bytes 15728640 | tf_op jit(solution)/shard_map/attend_forward/pallas_call | solution.py:231
  115.3 3.6 %all-to-all-start.1 = ((bf16[4,3,256,128]{3,2,1,0:T(8,128)(2,1)}), bf16[4,3,256,128]{3,2,1,0:T(8,128)(2,1)S(1)}, u32[]{:S(2)}, u32[]{:S(2)}) async-start(bf16[4,3,256,128]{3,2,1,0:T(8,128)(2,1)} %get-tuple-element.150), calls=%async_computation.1 | async-start | bytes 1572864 | tf_op jit(solution)/shard_map/all_to_all | solution.py:1156
  121.0 8.4 %all-to-all-done.1.a_ref = bf16[4,3,256,128]{3,2,1,0:T(8,128)(2,1)S(1)} async-done(((bf16[4,3,256,128]{3,2,1,0:T(8,128)(2,1)}), bf16[4,3,256,128]{3,2,1,0:T(8,128)(2,1)S(1)}, u32[]{:S(2)}, u32[]{:S(2)}) %all-to-all-start.1) | async-done | bytes 786464 | tf_op jit(solution)/shard_map/all_to_all | solution.py:1156
  130.2 20.8 %layer.1 = (bf16[256,768]{1,0:T(8,128)(2,1)}, bf16[256,768]{1,0:T(8,128)(2,1)}, bf16[4,512,192]{2,1,0:T(8,128)(2,1)}, bf16[4,512,192]{2,1,0:T(8,128)(2,1)}, bf16...) custom-call(bf16[4,3,256,128]{3,2,1,0:T(8,128)(2,1)} %copy-done.27, ...), custom_call_target="tpu_custom_call" | custom-call | flops 9663676416 | bytes 25165824 | tf_op jit(solution)/shard_map/layer/pallas_call | solution.py:610
  151.1 8.3 %token_grads.2 = bf16[2,1728,768]{2,1,0:T(8,128)(2,1)} custom-call(s32[4]{0:T(128)} %add_add_fusion.1.place_ref, bf16[512,3072]{1,0:T(8,128)(2,1)} %get-tuple-element.162.active_ref, bf16[4,512,192]{2,1,0:T(8,128)(2,1)} %get-tuple-element.163.inner_ref, bf16[4,512,192]{2,1,0:T(8,128)(2,1)} %get-tuple-element.164.mixed_ref, ...), custom_call_target="tpu_custom_call" | custom-call | flops 2415919104 | bytes 16777216 | tf_op jit(solution)/shard_map/token_grads/pallas_call | solution.py:728
  159.4 4.2 %all-to-all-start.2 = ((bf16[4,3,256,128]{3,2,1,0:T(8,128)(2,1)}), bf16[4,3,256,128]{3,2,1,0:T(8,128)(2,1)}, u32[]{:S(2)}, u32[]{:S(2)}) async-start(bf16[4,3,256,128]{3,2,1,0:T(8,128)(2,1)} %get-tuple-element.161), calls=%async_computation.2 | async-start | bytes 1572864 | tf_op jit(solution)/shard_map/all_to_all | solution.py:1166
  164.2 4.3 %collective-permute-done.12.other_ref = bf16[2,1728,768]{2,1,0:T(8,128)(2,1)} collective-permute-done((bf16[2,1728,768]{2,1,0:T(8,128)(2,1)}, bf16[2,1728,768]{2,1,0:T(8,128)(2,1)}, u32[]{:S(2)}, u32[]{:S(2)}) %collective-permute-start.12) | collective-permute-done | bytes 5308448 | tf_op jit(solution)/shard_map/ppermute | solution.py:976
  168.5 9.7 %token_grads.3 = (bf16[1,576,768]{2,1,0:T(8,128)(2,1)}, bf16[1,576,768]{2,1,0:T(8,128)(2,1)}, bf16[2,288,768]{2,1,0:T(8,128)(2,1)}, bf16[2,288,768]{2,1,0:T(8,12...) custom-call(s32[4]{0:T(128)} %add_add_fusion.place_ref, ...), custom_call_target="tpu_custom_call" | custom-call | flops 2415919104 | bytes 16777216 | tf_op jit(solution)/shard_map/token_grads/pallas_call | solution.py:728
  183.0 18.4 %attend_backward.3 = (bf16[4,256,128]{2,1,0:T(8,128)(2,1)}, bf16[1280,128]{1,0:T(8,128)(2,1)}, bf16[3328,64]{1,0:T(8,128)(2,1)}, f32[8,64]{1,0:T(8,128)}) custom-call(bf16[2,1024,192]{2,1,0:T(8,128)(2,1)} %copy-done.11, f32[8,192]{1,0:T(8,128)} %copy-done.16, s32[1024,4]{1,0:T(8,128)} %copy.68.qinfo_ref, bf16[3,1280,128]{2,1,0:T(8,128)(2,1)} %get-tuple-element.155.kaug_ref, ...), custom_call_target="tpu_custom_call" | custom-call | flops 8053063680 | bytes 5242880 | tf_op jit(solution)/shard_map/attend_backward/pallas_call | solution.py:283
  207.4 19.1 %attend_backward.4 = (bf16[4,256,128]{2,1,0:T(8,128)(2,1)}, bf16[1280,128]{1,0:T(8,128)(2,1)}, bf16[3328,64]{1,0:T(8,128)(2,1)}, f32[8,64]{1,0:T(8,128)}) custom-call(bf16[2,1024,192]{2,1,0:T(8,128)(2,1)} %copy-done.11, f32[8,192]{1,0:T(8,128)} %copy-done.16, s32[1024,4]{1,0:T(8,128)} %copy.68.qinfo_ref, bf16[3,1280,128]{2,1,0:T(8,128)(2,1)} %get-tuple-element.155.kaug_ref, ...), custom_call_target="tpu_custom_call" | custom-call | flops 8053063680 | bytes 5242880 | tf_op jit(solution)/shard_map/attend_backward/pallas_call | solution.py:283
  230.9 7.5 %head_grads.2 = bf16[4,192,512]{2,1,0:T(8,128)(2,1)} custom-call(s32[2]{0:T(128)} %copy-done.8, bf16[2304,768]{1,0:T(8,128)(2,1)} %get-tuple-element.176.states_ref, bf16[3328,768]{1,0:T(8,128)(2,1)} %get-tuple-element.177.position_ref, bf16[4,256,128]{2,1,0:T(8,128)(2,1)} %get-tuple-element.220.rest_0_, bf16[4,256,128]{2,1,0:T(8,128)(2,1)} %get-tuple-element.222.rest_1_, ...), custom_call_target="tpu_custom_call" | custom-call | flops 2617245696 | bytes 12582912 | tf_op jit(solution)/shard_map/head_grads/pallas_call | solution.py:839
  240.7 3.9 %all-to-all-start.3 = ((bf16[4,2,576,128]{3,2,1,0:T(8,128)(2,1)}), bf16[4,2,576,128]{3,2,1,0:T(8,128)(2,1)S(1)}, u32[]{:S(2)}, u32[]{:S(2)}) async-start(bf16[4,2,576,128]{3,2,1,0:T(8,128)(2,1)} %pad_maximum_fusion), calls=%async_computation.3 | async-start | bytes 2359296 | tf_op jit(solution)/shard_map/all_to_all | solution.py:1221
  249.7 18.4 %attend_backward.5 = (bf16[4,256,128]{2,1,0:T(8,128)(2,1)}, bf16[1280,128]{1,0:T(8,128)(2,1)}, bf16[3328,64]{1,0:T(8,128)(2,1)}, f32[8,64]{1,0:T(8,128)}) custom-call(bf16[2,1024,192]{2,1,0:T(8,128)(2,1)} %copy-done.11, f32[8,192]{1,0:T(8,128)} %copy-done.16, s32[1024,4]{1,0:T(8,128)} %copy.68.qinfo_ref, bf16[3,1280,128]{2,1,0:T(8,128)(2,1)} %get-tuple-element.155.kaug_ref, ...), custom_call_target="tpu_custom_call" | custom-call | flops 8053063680 | bytes 5242880 | tf_op jit(solution)/shard_map/attend_backward/pallas_call | solution.py:283
  271.1 3.5 all-to-all-start.4
  281.0 6.5 %head_grads.3 = bf16[4,208,256]{2,1,0:T(8,128)(2,1)} custom-call(s32[2]{0:T(128)} %copy-done.8, bf16[2304,768]{1,0:T(8,128)(2,1)} %get-tuple-element.176.states_ref, bf16[3328,768]{1,0:T(8,128)(2,1)} %get-tuple-element.177.position_ref, bf16[4,256,128]{2,1,0:T(8,128)(2,1)} %get-tuple-element.225.rest_0_, bf16[1280,128]{1,0:T(8,128)(2,1)} %get-tuple-element.226.rest_1_, ...), custom_call_target="tpu_custom_call" | custom-call | flops 2617245696 | bytes 12582912 | tf_op jit(solution)/shard_map/head_grads/pallas_call | solution.py:839
  287.5 8.4 %collective-permute-done.26 = bf16[192,512]{1,0:T(8,128)(2,1)S(1)} collective-permute-done((bf16[192,512]{1,0:T(8,128)(2,1)S(1)}, bf16[192,512]{1,0:T(8,128)(2,1)S(1)}, u32[]{:S(2)}, u32[]{:S(2)}) %collective-permute-start.26) | collective-permute-done | bytes 196640 | tf_op jit(solution)/shard_map/ppermute | solution.py:976
  296.0 3.7 %collective-permute-done.25 = bf16[1,144,768]{2,1,0:T(8,128)(2,1)S(1)} collective-permute-done((bf16[1,144,768]{2,1,0:T(8,128)(2,1)S(1)}, bf16[1,144,768]{2,1,0:T(8,128)(2,1)S(1)}, u32[]{:S(2)}, u32[]{:S(2)}) %collective-permute-start.25) | collective-permute-done | bytes 221216 | tf_op jit(solution)/shard_map/ppermute | solution.py:976
  317.3 3.8 %collective-permute-done.36 = bf16[1,4,3,32,128]{4,3,2,1,0:T(8,128)(2,1)S(1)} collective-permute-done((bf16[1,4,3,32,128]{4,3,2,1,0:T(8,128)(2,1)S(1)}, bf16[1,4,3,32,128]{4,3,2,1,0:T(8,128)(2,1)S(1)}, u32[]{:S(2)}, u32[]{:S(2)}) %collective-permute-start.36) | collective-permute-done | bytes 98336 | tf_op jit(solution)/shard_map/ppermute | solution.py:976
  321.2 3.4 collective-permute-start.31
  325.2 7.7 %collective-permute-done.31 = bf16[208,256]{1,0:T(8,128)(2,1)S(1)} collective-permute-done((bf16[208,256]{1,0:T(8,128)(2,1)S(1)}, bf16[208,256]{1,0:T(8,128)(2,1)S(1)}, u32[]{:S(2)}, u32[]{:S(2)}) %collective-permute-start.31) | collective-permute-done | bytes 106528 | tf_op jit(solution)/shard_map/ppermute | solution.py:976
  340.9 4.8 %finish.1 = (bf16[256,768]{1,0:T(8,128)(2,1)}, bf16[256,768]{1,0:T(8,128)(2,1)}, bf16[32,768]{1,0:T(8,128)(2,1)}) custom-call(bf16[4,2,576,128]{3,2,1,0:T(8,128)(2,1)S(1)} %all-to-all-done.3.early_ref, bf16[4,1,576,128]{3,2,1,0:T(8,128)(2,1)S(1)} %all-to-all-done.4.late_ref, bf16[4,3,32,128]{3,2,1,0:T(8,128)(2,1)S(1)} %bitcast.119, ...), custom_call_target="tpu_custom_call" | custom-call | flops 1207959552 | bytes 8388608 | tf_op jit(solution)/shard_map/finish/pallas_call | solution.py:938
  (297 shorter events, 99.7 us)
Async XLA Ops:
  7.2 113.8 %all-gather.5.cloned.1.call-start = ((), (), s32[]{:S(2)}) async-start(), calls=%async_computation.5 | async-start | bytes 1474560 | tf_op jit(solution)/shard_map/all_gather | solution.py:1112
  8.1 121.3 %all-gather.7.cloned.1.call-start = ((), (), s32[]{:S(2)}) async-start(), calls=%async_computation.6 | async-start | bytes 5898240 | tf_op jit(solution)/shard_map/all_gather | solution.py:1113
  8.9 120.5 %all-gather.9.cloned.1.call-start = ((), (), s32[]{:S(2)}) async-start(), calls=%async_computation.7 | async-start | bytes 5898240 | tf_op jit(solution)/shard_map/all_gather | solution.py:1114
  12.0 20.1 %collective-permute-start.7 = (bf16[4,192,192]{2,1,0:T(8,128)(2,1)S(1)}, bf16[4,192,192]{2,1,0:T(8,128)(2,1)S(1)}, u32[]{:S(2)}, u32[]{:S(2)}) collective-permute-start(bf16[4,192,192]{2,1,0:T(8,128)(2,1)S(1)} %pad_maximum_fusion.2.refs_0_), channel_id=1, source_target_pairs={{0,2},{1,3},{2,0},{3,1},{4,6},{5,7},{6,4},{7,5},{8,10},{9,11},{10,... | collective-permute-start | bytes 884744 | tf_op jit(solution)/shard_map/ppermute | solution.py:976
  15.0 22.0 %collective-permute-start.6 = (bf16[4,192,192]{2,1,0:T(8,128)(2,1)S(1)}, bf16[4,192,192]{2,1,0:T(8,128)(2,1)S(1)}, u32[]{:S(2)}, u32[]{:S(2)}) collective-permute-start(bf16[4,192,192]{2,1,0:T(8,128)(2,1)S(1)} %pad_maximum_fusion.2.refs_0_), channel_id=1, source_target_pairs={{0,1},{1,0},{2,3},{3,2},{4,5},{5,4},{6,7},{7,6},{8,9},{9,8},{10,11... | collective-permute-start | bytes 884744 | tf_op jit(solution)/shard_map/ppermute | solution.py:976
  19.7 31.4 %all-to-all-start = ((bf16[8,32,768]{2,1,0:T(8,128)(2,1)}), bf16[8,32,768]{2,1,0:T(8,128)(2,1)S(1)}, u32[]{:S(2)}, u32[]{:S(2)}) async-start(bf16[8,32,768]{2,1,0:T(8,128)(2,1)} %broadcast_in_dim.31), calls=%async_computation | async-start | bytes 786432 | tf_op jit(solution)/shard_map/all_to_all | solution.py:1105
  30.7 20.4 %collective-permute-start.1 = (bf16[256,768]{1,0:T(8,128)(2,1)S(1)}, bf16[256,768]{1,0:T(8,128)(2,1)}, u32[]{:S(2)}, u32[]{:S(2)}) collective-permute-start(bf16[256,768]{1,0:T(8,128)(2,1)S(1)} %bitcast.122), channel_id=1, source_target_pairs={{0,8},{4,12},{8,0},{12,4},{1,9},{5,13},{9,1},{13,5},{2,10},{6,14},... | collective-permute-start | bytes 1179656 | tf_op jit(solution)/shard_map/ppermute | solution.py:976
  118.9 40.5 %all-gather.11.cloned.1.call-start = ((), (), s32[]{:S(2)}) async-start(), calls=%async_computation.8 | async-start | bytes 4423680 | tf_op jit(solution)/shard_map/all_gather | solution.py:1116
  159.4 23.6 %all-to-all-start.2 = ((bf16[4,3,256,128]{3,2,1,0:T(8,128)(2,1)}), bf16[4,3,256,128]{3,2,1,0:T(8,128)(2,1)}, u32[]{:S(2)}, u32[]{:S(2)}) async-start(bf16[4,3,256,128]{3,2,1,0:T(8,128)(2,1)} %get-tuple-element.161), calls=%async_computation.2 | async-start | bytes 1572864 | tf_op jit(solution)/shard_map/all_to_all | solution.py:1166
  178.1 23.3 %collective-permute-start.13 = (bf16[1,576,768]{2,1,0:T(8,128)(2,1)}, bf16[1,576,768]{2,1,0:T(8,128)(2,1)S(1)}, u32[]{:S(2)}, u32[]{:S(2)}) collective-permute-start(bf16[1,576,768]{2,1,0:T(8,128)(2,1)} %get-tuple-element.169), channel_id=1, source_target_pairs={{0,2},{1,3},{2,0},{3,1},{4,6},{5,7},{6,4},{7,5},{8,10},{9,11},{10,... | collective-permute-start | bytes 2654216 | tf_op jit(solution)/shard_map/ppermute | solution.py:976
  181.2 21.6 %collective-permute-start.14 = (bf16[2,288,768]{2,1,0:T(8,128)(2,1)}, bf16[2,288,768]{2,1,0:T(8,128)(2,1)S(1)}, u32[]{:S(2)}, u32[]{:S(2)}) collective-permute-start(bf16[2,288,768]{2,1,0:T(8,128)(2,1)} %get-tuple-element.171), channel_id=1, source_target_pairs={{0,4},{4,0},{1,5},{5,1},{2,6},{6,2},{3,7},{7,3},{8,12},{12,8},{9,1... | collective-permute-start | bytes 2654216 | tf_op jit(solution)/shard_map/ppermute | solution.py:976
  182.6 21.3 %collective-permute-start.15 = (bf16[2,288,768]{2,1,0:T(8,128)(2,1)}, bf16[2,288,768]{2,1,0:T(8,128)(2,1)S(1)}, u32[]{:S(2)}, u32[]{:S(2)}) collective-permute-start(bf16[2,288,768]{2,1,0:T(8,128)(2,1)} %get-tuple-element.173), channel_id=1, source_target_pairs={{0,8},{8,0},{1,9},{9,1},{2,10},{10,2},{3,11},{11,3},{4,12},{12,4},... | collective-permute-start | bytes 2654216 | tf_op jit(solution)/shard_map/ppermute | solution.py:976
  204.3 22.2 %collective-permute-start.18 = (bf16[1,288,768]{2,1,0:T(8,128)(2,1)S(1)}, bf16[1,288,768]{2,1,0:T(8,128)(2,1)S(1)}, u32[]{:S(2)}, u32[]{:S(2)}) collective-permute-start(bf16[1,288,768]{2,1,0:T(8,128)(2,1)S(1)} %get-tuple-element.266), channel_id=1, source_target_pairs={{0,2},{1,3},{2,0},{3,1},{4,6},{5,7},{6,4},{7,5},{8,10},{9,11},{10,... | collective-permute-start | bytes 1327112 | tf_op jit(solution)/shard_map/ppermute | solution.py:976
  205.0 21.5 %collective-permute-start.17 = (bf16[2,144,768]{2,1,0:T(8,128)(2,1)S(1)}, bf16[2,144,768]{2,1,0:T(8,128)(2,1)S(1)}, u32[]{:S(2)}, u32[]{:S(2)}) collective-permute-start(bf16[2,144,768]{2,1,0:T(8,128)(2,1)S(1)} %get-tuple-element.268), channel_id=1, source_target_pairs={{0,8},{8,0},{1,9},{9,1},{2,10},{10,2},{3,11},{11,3},{4,12},{12,4},... | collective-permute-start | bytes 1327112 | tf_op jit(solution)/shard_map/ppermute | solution.py:976
  205.7 20.8 %collective-permute-start.16 = (bf16[1,288,768]{2,1,0:T(8,128)(2,1)S(1)}, bf16[1,288,768]{2,1,0:T(8,128)(2,1)S(1)}, u32[]{:S(2)}, u32[]{:S(2)}) collective-permute-start(bf16[1,288,768]{2,1,0:T(8,128)(2,1)S(1)} %get-tuple-element.270), channel_id=1, source_target_pairs={{0,4},{4,0},{1,5},{5,1},{2,6},{6,2},{3,7},{7,3},{8,12},{12,8},{9,1... | collective-permute-start | bytes 1327112 | tf_op jit(solution)/shard_map/ppermute | solution.py:976
  240.7 29.4 %all-to-all-start.3 = ((bf16[4,2,576,128]{3,2,1,0:T(8,128)(2,1)}), bf16[4,2,576,128]{3,2,1,0:T(8,128)(2,1)S(1)}, u32[]{:S(2)}, u32[]{:S(2)}) async-start(bf16[4,2,576,128]{3,2,1,0:T(8,128)(2,1)} %pad_maximum_fusion), calls=%async_computation.3 | async-start | bytes 2359296 | tf_op jit(solution)/shard_map/all_to_all | solution.py:1221
  247.0 23.1 %collective-permute-start.24 = (bf16[2,144,768]{2,1,0:T(8,128)(2,1)S(1)}, bf16[2,144,768]{2,1,0:T(8,128)(2,1)S(1)}, u32[]{:S(2)}, u32[]{:S(2)}) collective-permute-start(bf16[2,144,768]{2,1,0:T(8,128)(2,1)S(1)} %constant_dynamic-update-slice_fusion), channel_id=1, source_target_pairs={{0,16},{16,0},{1,17},{17,1},{2,18},{18,2},{3,19},{19,3},{4,20},{20... | collective-permute-start | bytes 1327112 | tf_op jit(solution)/shard_map/ppermute | solution.py:976
  271.1 31.5 %all-to-all-start.4 = ((bf16[4,1,576,128]{3,2,1,0:T(8,128)(2,1)}), bf16[4,1,576,128]{3,2,1,0:T(8,128)(2,1)S(1)}, u32[]{:S(2)}, u32[]{:S(2)}) async-start(bf16[4,1,576,128]{3,2,1,0:T(8,128)(2,1)} %maximum_bitcast_fusion.2), calls=%async_computation.4 | async-start | bytes 1179648 | tf_op jit(solution)/shard_map/all_to_all | solution.py:1221
  274.6 25.2 %collective-permute-start.27 = (bf16[2,144,768]{2,1,0:T(8,128)(2,1)S(1)}, bf16[2,144,768]{2,1,0:T(8,128)(2,1)S(1)}, u32[]{:S(2)}, u32[]{:S(2)}) collective-permute-start(bf16[2,144,768]{2,1,0:T(8,128)(2,1)S(1)} %add_convert_fusion.3.refs_0_), channel_id=1, source_target_pairs={{0,4},{4,0},{8,12},{12,8},{1,5},{5,1},{9,13},{13,9},{2,6},{6,2},{1... | collective-permute-start | bytes 1327112 | tf_op jit(solution)/shard_map/ppermute | solution.py:976
  276.6 25.2 %collective-permute-start.28 = (bf16[2,144,768]{2,1,0:T(8,128)(2,1)S(1)}, bf16[2,144,768]{2,1,0:T(8,128)(2,1)S(1)}, u32[]{:S(2)}, u32[]{:S(2)}) collective-permute-start(bf16[2,144,768]{2,1,0:T(8,128)(2,1)S(1)} %add_convert_fusion.3.refs_0_), channel_id=1, source_target_pairs={{0,8},{4,12},{8,0},{12,4},{1,9},{5,13},{9,1},{13,5},{2,10},{6,14},... | collective-permute-start | bytes 1327112 | tf_op jit(solution)/shard_map/ppermute | solution.py:976
  304.3 20.3 %collective-permute-start.33 = (bf16[1,144,768]{2,1,0:T(8,128)(2,1)S(1)}, bf16[1,144,768]{2,1,0:T(8,128)(2,1)S(1)}, u32[]{:S(2)}, u32[]{:S(2)}) collective-permute-start(bf16[1,144,768]{2,1,0:T(8,128)(2,1)S(1)} %add_convert_fusion.7.refs_4_), channel_id=1, source_target_pairs={{0,4},{4,0},{8,12},{12,8},{1,5},{5,1},{9,13},{13,9},{2,6},{6,2},{1... | collective-permute-start | bytes 663560 | tf_op jit(solution)/shard_map/ppermute | solution.py:976
  308.5 25.5 %collective-permute-start.35 = (bf16[1,144,768]{2,1,0:T(8,128)(2,1)S(1)}, bf16[1,144,768]{2,1,0:T(8,128)(2,1)S(1)}, u32[]{:S(2)}, u32[]{:S(2)}) collective-permute-start(bf16[1,144,768]{2,1,0:T(8,128)(2,1)S(1)} %add_convert_fusion.7.refs_4_), channel_id=1, source_target_pairs={{0,12},{4,8},{8,4},{12,0},{1,13},{5,9},{9,5},{13,1},{2,14},{6,10},... | collective-permute-start | bytes 663560 | tf_op jit(solution)/shard_map/ppermute | solution.py:976
  314.5 19.5 %collective-permute-start.32 = (bf16[2,144,768]{2,1,0:T(8,128)(2,1)S(1)}, bf16[2,144,768]{2,1,0:T(8,128)(2,1)S(1)}, u32[]{:S(2)}, u32[]{:S(2)}) collective-permute-start(bf16[2,144,768]{2,1,0:T(8,128)(2,1)S(1)} %add_convert_fusion.3.refs_0_), channel_id=1, source_target_pairs={{0,12},{4,8},{8,4},{12,0},{1,13},{5,9},{9,5},{13,1},{2,14},{6,10},... | collective-permute-start | bytes 1327112 | tf_op jit(solution)/shard_map/ppermute | solution.py:976
  325.2 20.4 %collective-permute-start.38 = (bf16[192,512]{1,0:T(8,128)(2,1)S(1)}, bf16[192,512]{1,0:T(8,128)(2,1)S(1)}, u32[]{:S(2)}, u32[]{:S(2)}) collective-permute-start(bf16[192,512]{1,0:T(8,128)(2,1)S(1)} %add_convert_fusion.11.refs_0_), channel_id=1, source_target_pairs={{0,8},{4,12},{8,0},{12,4},{1,9},{5,13},{9,1},{13,5},{2,10},{6,14},... | collective-permute-start | bytes 589832 | tf_op jit(solution)/shard_map/ppermute | solution.py:976
  (82 other events, 757.8 us)
Sparse Core Ops, SparseCore 0:
  9.6 22.4 all-gather.4
  33.7 38.8 all-gather.6
  74.2 37.4 all-gather.8
  121.0 32.9 all-gather.10
